TPU v7x, 32 devices: a whole 2x2x4 slice. The times are simulated.
32 devices in a mesh: fsdp: 16 (over z, x, core), tp: 2 (over y).
Axes of the slice: x: 2, y: 2, z: 4, core: 2. Of those that a mesh axis runs over, the one named last changes fastest.
Arguments:
- inputs: bfloat16 [16384, 768], P(('fsdp', 'tp')), may hold values from -12 to 12
- token_ids: int32 [16384], P('fsdp'), may hold values from 0 to 50303, as said below
- hash_table: int32 [50304], replicated, may hold values from 0 to 15, as said below
- segment_lengths: int32 [16, 13], P('fsdp'), may hold values from 1 to 256, 1024 in all within a row
- segment_parents: int32 [16, 13], P('fsdp'), may hold values from 0 to 11, as said below
- first_gain: float32 [768], replicated, may hold values from 0.5 to 1.5
- first_bias: float32 [768], replicated, may hold values from -1.25 to 1.25
- input_weight: bfloat16 [3, 768, 768], P(None, 'fsdp', 'tp'), may hold values from -0.21875 to 0.21875
- output_weight: bfloat16 [768, 768], P('tp', 'fsdp'), may hold values from -0.875 to 0.875
- second_gain: float32 [768], replicated, may hold values from 0.5 to 1.5
- second_bias: float32 [768], replicated, may hold values from -1.25 to 1.25
- expert_in: bfloat16 [16, 768, 3072], P('fsdp', None, 'tp'), may hold values from -0.21875 to 0.21875
- expert_out: bfloat16 [16, 3072, 768], P('fsdp', 'tp'), may hold values from -0.109375 to 0.109375
- cotangent: bfloat16 [16384, 768], P(('fsdp', 'tp')), may hold values from -12 to 12
Outputs:
- out_block: bfloat16 [16384, 768], P(('fsdp', 'tp'))
- input_grad: float32 [16384, 768], P(('fsdp', 'tp'))
- first_gain_grad: float32 [768], replicated
- first_bias_grad: float32 [768], replicated
- input_weight_grad: float32 [3, 768, 768], P(None, 'fsdp', 'tp')
- output_weight_grad: float32 [768, 768], P('tp', 'fsdp')
- second_gain_grad: float32 [768], replicated
- second_bias_grad: float32 [768], replicated
- expert_in_grad: float32 [16, 768, 3072], P('fsdp', None, 'tp')
- expert_out_grad: float32 [16, 3072, 768], P('fsdp', 'tp')
Inputs may be any that keep to these rules, and one draw needn't show every extreme that they name: `token_ids`: in each aligned block of 512 rows at most 64 tokens hash through hash_table to one expert, and in every block 1 expert take exactly 64. `hash_table`: every expert is the value of exactly 3144 entries. `segment_lengths`: the 13 lengths of a tree sum to 1024. `segment_parents`: segment 0 is its own parent; any other segment's parent is a smaller segment number.
All inputs are finite; a program needn't handle non-finite values.
Results may differ from a plain program's by a relative error of at most 0.011.
Values may be sent and summed in bfloat16 or wider, within the bound.
No kernel may reach another device: no remote copies, remote signals or barrier semaphores. Data moves between devices by JAX's collectives and lax.ppermute only.
A program may use at most 192 MiB of HBM per device.

v0:
```python
import functools

import jax
import jax.numpy as jnp
from jax import lax
from jax.experimental import pallas as pl
from jax.experimental.pallas import tpu as pltpu
from jax.sharding import PartitionSpec as P

HD = 64
LANES = 128

norm_eps = 1e-05
masked_score = -1e30
gelu_root = 0.7978845608028654
gelu_cubic = 0.044715
low = jnp.bfloat16
wide = jnp.float32

NN = (((1,), (0,)), ((), ()))
NT = (((1,), (1,)), ((), ()))
TN = (((0,), (0,)), ((), ()))


def dot(left, right, dims=NN):
    return lax.dot_general(left, right, dims, preferred_element_type=wide)


def gelu_both(values):
    squared = values * values
    tangent = jnp.tanh(gelu_root * values * (1.0 + gelu_cubic * squared))
    half_up = 0.5 * (1.0 + tangent)
    slope = half_up + 0.5 * values * (1.0 - tangent * tangent) * gelu_root * (
        1.0 + 3.0 * gelu_cubic * squared
    )
    return values * half_up, slope


def normalize(values):
    average = jnp.mean(values, axis=-1, keepdims=True)
    centred = values - average
    inverse = lax.rsqrt(jnp.mean(centred * centred, axis=-1, keepdims=True) + norm_eps)
    return (centred * inverse, inverse)


def norm_back(upstream, normed, inverse, gain):
    scaled = upstream * gain
    centred_grad = (
        scaled
        - jnp.mean(scaled, axis=-1, keepdims=True)
        - normed * jnp.mean(scaled * normed, axis=-1, keepdims=True)
    )
    return inverse * centred_grad


def array(shape, kind):
    return jax.ShapeDtypeStruct(shape, kind)


def run(kernel, operands, outs, flops=0, limit=32, **more):
    if "in_specs" not in more:
        more["in_specs"] = [spec_of(x) for x in operands]
    moved = sum(x.size * x.dtype.itemsize for x in operands) + sum(
        x.size * x.dtype.itemsize for x in jax.tree.leaves(outs)
    )
    return pl.pallas_call(
        kernel,
        out_shape=outs,
        compiler_params=pltpu.CompilerParams(vmem_limit_bytes=limit << 20),
        cost_estimate=pl.CostEstimate(flops=int(flops), bytes_accessed=int(moved), transcendentals=0),
        **more,
    )(*operands)


def spec_of(x):
    scalar = x.ndim == 1 and x.dtype == jnp.int32
    return pl.BlockSpec(memory_space=pltpu.SMEM if scalar else pltpu.VMEM)


def project_kernel(chips, place_ref, own_ref, other_ref, gain_ref, bias_ref, mine_ref, sibling_ref, full_ref, out_ref):
    place, side = place_ref[0], place_ref[1]
    if chips:
        rows = mine_ref.shape[2]
        for k in range(chips):
            source = place ^ (2 * k)
            full_ref[:, pl.ds(pl.multiple_of(source * rows, rows), rows), :] = mine_ref[k]
            source = source ^ 1
            full_ref[:, pl.ds(pl.multiple_of(source * rows, rows), rows), :] = sibling_ref[k]
    else:
        full_ref[...] = mine_ref[...]
    count, width = own_ref.shape[0], mine_ref.shape[-1]
    for ref, first in ((own_ref, side * count), (other_ref, (1 - side) * count)):
        hat, _ = normalize(ref[...].astype(wide))
        normed = (hat * gain_ref[...] + bias_ref[...]).astype(low)
        for n in range(3):
            out_ref[pl.ds(pl.multiple_of(first, count), count), n * width : (n + 1) * width] = dot(
                normed, full_ref[n]
            ).astype(low)


def attend_kernel(block, place_ref, q_ref, k_ref, v_ref, unreached_ref, member_ref, out_ref, total_ref, keep_ref, give_ref):
    side = place_ref[1]
    rows = q_ref.shape[0]
    lane = lax.broadcasted_iota(jnp.int32, (1, LANES), 1)
    first_head = lane < HD
    ones = jnp.ones((rows, LANES), low)
    keys = jnp.concatenate([k_ref[...], member_ref[...]], axis=1)
    values = jnp.concatenate([v_ref[...], ones], axis=1)
    causal = lax.broadcasted_iota(jnp.int32, (block, block), 1) <= lax.broadcasted_iota(
        jnp.int32, (block, block), 0
    )
    for start in range(0, rows, block):
        stop = start + block
        query = q_ref[start:stop] * HD**-0.5
        unreached = unreached_ref[start:stop]
        halves = []
        for own in (first_head, ~first_head):
            left = jnp.concatenate([jnp.where(own, query, 0).astype(low), unreached], axis=1)
            scores = dot(left, keys[:stop], NT)
            near = jnp.where(causal, scores[:, start:], masked_score)
            top = jnp.max(near, axis=1, keepdims=True)
            if start:
                far = scores[:, :start]
                top = jnp.maximum(top, jnp.max(far, axis=1, keepdims=True))
                weights = jnp.concatenate(
                    [jnp.exp(far - top).astype(low), jnp.exp(near - top).astype(low)], axis=1
                )
            else:
                weights = jnp.exp(near - top).astype(low)
            sums = dot(weights, values[:stop], NN)
            total = sums[:, LANES:]
            halves.append((sums[:, :LANES] / total, top + jnp.log(total)))
        out_ref[start:stop] = jnp.where(first_head, halves[0][0], halves[1][0]).astype(low)
        total_ref[start:stop] = jnp.where(first_head, halves[0][1], halves[1][1])
    half = rows // 2
    keep_ref[...] = out_ref[pl.ds(pl.multiple_of(side * half, half), half)]
    give_ref[...] = out_ref[pl.ds(pl.multiple_of((1 - side) * half, half), half)]


def attend(place, projected, unreached, member, block=256):
    rows, width = projected.shape
    pairs = width // (3 * LANES)

    def part(n, height=rows):
        return pl.BlockSpec((height, LANES), lambda p: (0, n * pairs + p))

    fixed = pl.BlockSpec((rows, LANES), lambda p: (0, 0))
    return run(
        functools.partial(attend_kernel, block),
        (place, projected, projected, projected, unreached, member),
        [
            array((rows, width // 3), low),
            array((rows, width // 3), wide),
            array((rows // 2, width // 3), low),
            array((rows // 2, width // 3), low),
        ],
        flops=12e9,
        grid=(pairs,),
        in_specs=[spec_of(place), part(0), part(1), part(2), fixed, fixed],
        out_specs=[part(0), part(0), part(0, rows // 2), part(0, rows // 2)],
    )


def attend_back_kernel(
    block, place_ref, q_ref, k_ref, v_ref, unreached_ref, member_ref, out_ref, total_ref, mine_ref, more_ref, res_ref, dk, dv, grads
):
    side = place_ref[1]
    rows = q_ref.shape[0]
    half = rows // 2
    grads[pl.ds(pl.multiple_of(side * half, half), half)] = mine_ref[...]
    grads[pl.ds(pl.multiple_of((1 - side) * half, half), half)] = more_ref[...]
    lane = lax.broadcasted_iota(jnp.int32, (1, LANES), 1)
    first_head = lane < HD
    keys = jnp.concatenate([k_ref[...], member_ref[...]], axis=1)
    causal = lax.broadcasted_iota(jnp.int32, (block, block), 1) <= lax.broadcasted_iota(
        jnp.int32, (block, block), 0
    )
    for start in range(rows - block, -1, -block):
        stop = start + block
        query = q_ref[start:stop] * HD**-0.5
        unreached = unreached_ref[start:stop]
        grad = grads[start:stop]
        both = grad.astype(wide) * out_ref[start:stop].astype(wide)
        query_halves = []
        key_terms = []
        value_terms = []
        for head, own in enumerate((first_head, ~first_head)):
            q_own = jnp.where(own, query, 0).astype(low)
            g_own = jnp.where(own, grad, 0).astype(low)
            scores = dot(jnp.concatenate([q_own, unreached], axis=1), keys[:stop], NT)
            total = total_ref[start:stop, HD * head : HD * head + 1]
            centre = jnp.sum(jnp.where(own, both, 0.0), axis=1, keepdims=True)
            near = jnp.exp(jnp.where(causal, scores[:, start:], masked_score) - total)
            if start:
                weights = jnp.concatenate([jnp.exp(scores[:, :start] - total), near], axis=1)
            else:
                weights = near
            gains = dot(g_own, v_ref[:stop], NT)
            slopes = (weights * (gains - centre)).astype(low)
            query_halves.append(dot(slopes, k_ref[:stop], NN))
            key_terms.append(dot(slopes, q_own, TN))
            value_terms.append(dot(weights.astype(low), g_own, TN))
        res_ref[0, start:stop] = (
            jnp.where(first_head, query_halves[0], query_halves[1]) * HD**-0.5
        ).astype(low)
        if stop == rows:
            dk[...] = key_terms[0] + key_terms[1]
            dv[...] = value_terms[0] + value_terms[1]
        else:
            dk[:stop] += key_terms[0] + key_terms[1]
            dv[:stop] += value_terms[0] + value_terms[1]
    res_ref[1] = dk[...].astype(low)
    res_ref[2] = dv[...].astype(low)


def attend_back(place, projected, unreached, member, out, total, mine, more, block=256):
    rows, width = projected.shape
    pairs = width // (3 * LANES)

    def part(n, height=rows):
        return pl.BlockSpec((height, LANES), lambda p: (0, n * pairs + p))

    fixed = pl.BlockSpec((rows, LANES), lambda p: (0, 0))
    return run(
        functools.partial(attend_back_kernel, block),
        (place, projected, projected, projected, unreached, member, out, total, mine, more),
        array((3, rows, width // 3), low),
        flops=24e9,
        grid=(pairs,),
        in_specs=[spec_of(place), part(0), part(1), part(2), fixed, fixed, part(0), part(0)]
        + [part(0, rows // 2)] * 2,
        out_specs=pl.BlockSpec((3, rows, LANES), lambda p: (0, 0, p)),
        scratch_shapes=[pltpu.VMEM((rows, LANES), wide)] * 2 + [pltpu.VMEM((rows, LANES), low)],
    )


def branch_kernel(keep_ref, more_ref, weight_ref, other_ref, residual_ref, gain_ref, bias_ref, middle_ref, normed_ref):
    branch = dot(keep_ref[...], weight_ref[...], NT) + dot(more_ref[...], other_ref[...], NT)
    middle = residual_ref[...].astype(wide) + branch
    middle_ref[...] = middle
    hat, _ = normalize(middle)
    normed_ref[...] = (hat * gain_ref[...] + bias_ref[...]).astype(low)


def pack_kernel(own_ref, sibling_ref, own_slot_ref, sibling_slot_ref, *out_refs):
    capacity = out_refs[0].shape[1]
    slots = len(out_refs) * capacity
    for source, (ref, slot_ref) in enumerate(
        ((own_ref, own_slot_ref), (sibling_ref, sibling_slot_ref))
    ):
        place = lax.broadcasted_iota(jnp.int32, (slots, ref.shape[0]), 0)
        chooser = (place == slot_ref[...]).astype(wide).astype(low)
        packed = dot(chooser, ref[...]).astype(low)
        for k, out_ref in enumerate(out_refs):
            out_ref[source] = packed[k * capacity : (k + 1) * capacity]


def expert_kernel(first, count, chunk, place_ref, in_ref, out_ref, grads_ref, more_grads_ref, *refs):
    pieces, more_pieces = refs[:count], refs[count : 2 * count]
    x_ref, ct_ref, active_ref, slope_ref, keep_ref, give_ref = refs[-6:]
    step = pl.program_id(0)
    place = place_ref[0]
    capacity = pieces[0].shape[1]
    rows = 2 * capacity
    for k in range(count):

        @pl.when(step == k)
        def _(k=k):
            for c in range(2):
                x_ref[0, c * capacity : (c + 1) * capacity] = pieces[k][c]
                x_ref[0, rows + c * capacity : rows + (c + 1) * capacity] = more_pieces[k][c]

    source = place ^ (2 * (first + step))
    for c in range(2):
        ct_ref[0, c * capacity : (c + 1) * capacity] = grads_ref[source ^ c]
        ct_ref[0, rows + c * capacity : rows + (c + 1) * capacity] = more_grads_ref[source ^ c]
    x = x_ref[0]
    ct = ct_ref[0]
    total = None
    for start in range(0, in_ref.shape[1], chunk):
        stop = start + chunk
        pre = dot(x, in_ref[:, start:stop])
        gains = dot(ct, out_ref[start:stop], NT)
        active, slope = gelu_both(pre)
        active_ref[0, :, start:stop] = active.astype(low)
        grad_pre = (gains * slope).astype(low)
        slope_ref[0, :, start:stop] = grad_pre
        term = dot(grad_pre, in_ref[:, start:stop], NT)
        total = term if total is None else total + term
    keep_ref[0] = total[:rows]
    give_ref[0] = total[rows:].astype(low)


def expert_group(place, weight_in, weight_out, grads, more_grads, pieces, more_pieces, buffers, span, chips):
    first, stop = span
    count = stop - first
    capacity, width = pieces[0].shape[1:]
    hidden = weight_in.shape[1]
    rows = 4 * capacity
    operands = [place, weight_in, weight_out, grads, more_grads, *pieces, *more_pieces]
    specs = [spec_of(place)] + [
        pl.BlockSpec(x.shape, lambda i, n=x.ndim: (0,) * n) for x in operands[1:]
    ]
    aliases = {}
    if buffers is not None:
        aliases = {len(operands) + n: n for n in range(4)}
        operands += buffers
        specs += [pl.BlockSpec(memory_space=pl.ANY)] * 4

    def block(height, size, offset):
        return pl.BlockSpec((1, height, size), lambda i: (offset + i, 0, 0))

    res = run(
        functools.partial(expert_kernel, first, count, min(512, hidden)),
        operands,
        [
            array((chips, rows, width), low),
            array((chips, rows, width), low),
            array((chips, rows, hidden), low),
            array((chips, rows, hidden), low),
            array((count, rows // 2, width), wide),
            array((count, rows // 2, width), low),
        ],
        flops=6 * count * rows * width * hidden,
        grid=(count,),
        in_specs=specs,
        out_specs=[
            block(rows, width, first),
            block(rows, width, first),
            block(rows, hidden, first),
            block(rows, hidden, first),
            block(rows // 2, width, 0),
            block(rows // 2, width, 0),
        ],
        input_output_aliases=aliases,
    )
    return res[:4], res[4], res[5]


def pieces_kernel(keep_ref, more_ref, *out_refs):
    capacity = out_refs[0].shape[1]
    for k, out_ref in enumerate(out_refs):
        total = (keep_ref[k] + more_ref[k].astype(wide)).astype(low)
        for c in range(2):
            out_ref[c] = total[c * capacity : (c + 1) * capacity]


def unpack_kernel(own_slot_ref, sibling_slot_ref, *refs):
    pieces, (own_ref, sibling_ref) = refs[:-2], refs[-2:]
    capacity = pieces[0].shape[1]
    slots = len(pieces) * capacity
    for source, (slot_ref, out_ref) in enumerate(
        ((own_slot_ref, own_ref), (sibling_slot_ref, sibling_ref))
    ):
        place = lax.broadcasted_iota(jnp.int32, (slot_ref.shape[0], slots), 1)
        chooser = (place == slot_ref[...]).astype(wide).astype(low)
        values = jnp.concatenate([piece[source] for piece in pieces], axis=0)
        out_ref[...] = dot(chooser, values).astype(low)


def ffn_kernel(active_ref, weight_ref, keep_ref, give_ref):
    values = dot(active_ref[0], weight_ref[...])
    rows = keep_ref.shape[1]
    keep_ref[0] = values[:rows]
    give_ref[0] = values[rows:].astype(low)


def ffn_sum_kernel(place_ref, keep_ref, more_ref, out_ref):
    place = place_ref[0]
    capacity = out_ref.shape[1]
    for k in range(keep_ref.shape[0]):
        total = (keep_ref[k] + more_ref[k].astype(wide)).astype(low)
        for c in range(2):
            out_ref[place ^ (2 * k + c)] = total[c * capacity : (c + 1) * capacity]


def out_kernel(slot_ref, values_ref, middle_ref, out_ref):
    place = lax.broadcasted_iota(jnp.int32, (slot_ref.shape[0], values_ref.shape[0]), 1)
    chooser = (place == slot_ref[...]).astype(wide).astype(low)
    out_ref[...] = (middle_ref[...] + dot(chooser, values_ref[...])).astype(low)


def middle_back_kernel(
    own_ref, more_ref, middle_ref, ct_ref, gain_ref, weight_ref, other_ref,
    grad_ref, branch_ref, mine_ref, give_ref, sums_ref,
):
    grad_second = own_ref[...].astype(wide) + more_ref[...].astype(wide)
    hat, inverse = normalize(middle_ref[...])
    sums_ref[0:1] = jnp.sum(grad_second * hat, axis=0, keepdims=True)
    sums_ref[1:2] = jnp.sum(grad_second, axis=0, keepdims=True)
    grad_middle = ct_ref[...].astype(wide) + norm_back(grad_second, hat, inverse, gain_ref[...])
    grad_ref[...] = grad_middle
    branch = grad_middle.astype(low)
    branch_ref[...] = branch
    give_ref[...] = dot(branch, other_ref[...]).astype(low)
    mine_ref[...] = dot(branch, weight_ref[...]).astype(low)


def output_part_kernel(branch_ref, keep_ref, more_ref, own_ref, give_ref):
    give_ref[...] = dot(branch_ref[...], more_ref[...], TN).astype(low)
    own_ref[...] = dot(branch_ref[...], keep_ref[...], TN)


def first_give_kernel(place_ref, grads_ref, full_ref, give_ref):
    half = give_ref.shape[0]
    first = pl.multiple_of((1 - place_ref[1]) * half, half)
    total = None
    for n in range(3):
        term = dot(grads_ref[n, pl.ds(first, half)], full_ref[n], NT)
        total = term if total is None else total + term
    give_ref[...] = total.astype(low)


def weight_part_kernel(
    chips, place_ref, own_ref, other_ref, gain_ref, bias_ref, grads_ref, part_ref, more_ref, keep_ref, give_ref, normed, parts
):
    place, side = place_ref[0], place_ref[1]
    count = own_ref.shape[0]
    for ref, first in ((own_ref, side * count), (other_ref, (1 - side) * count)):
        hat, _ = normalize(ref[...].astype(wide))
        normed[pl.ds(pl.multiple_of(first, count), count)] = (
            hat * gain_ref[...] + bias_ref[...]
        ).astype(low)
    for n in range(3):
        parts[n] = dot(normed[...], grads_ref[n], TN).astype(low)
    parts[3] = (part_ref[...] + more_ref[...].astype(wide)).astype(low)
    if chips:
        rows = keep_ref.shape[3]
        for k in range(chips):
            target = place ^ (2 * k)
            keep_ref[k % 2, k // 2] = parts[:, pl.ds(pl.multiple_of(target * rows, rows), rows)]
            target = target ^ 1
            give_ref[k % 2, k // 2] = parts[:, pl.ds(pl.multiple_of(target * rows, rows), rows)]
    else:
        keep_ref[...] = parts[...]
        give_ref[...] = jnp.zeros(give_ref.shape, low)


def first_own_kernel(place_ref, grads_ref, full_ref, give_ref, own_in_ref, other_in_ref, own_ref, sums_ref):
    half = own_ref.shape[0]
    first = pl.multiple_of(place_ref[1] * half, half)
    total = None
    for n in range(3):
        term = dot(grads_ref[n, pl.ds(first, half)], full_ref[n], NT)
        total = term if total is None else total + term
    own_ref[...] = total
    hat, _ = normalize(own_in_ref[...].astype(wide))
    more_hat, _ = normalize(other_in_ref[...].astype(wide))
    more = give_ref[...].astype(wide)
    sums_ref[0:1] = jnp.sum(total * hat + more * more_hat, axis=0, keepdims=True)
    sums_ref[1:2] = jnp.sum(total + more, axis=0, keepdims=True)


def halves_kernel(keep_ref, more_ref, near_ref, far_ref):
    near_ref[...] = (keep_ref[0].astype(wide) + more_ref[0].astype(wide)).astype(low)
    far_ref[...] = (keep_ref[1].astype(wide) + more_ref[1].astype(wide)).astype(low)


def quarters_kernel(keep_ref, more_ref, own_ref, *out_refs):
    own_ref[...] = keep_ref[0].astype(wide) + more_ref[0].astype(wide)
    for n, out_ref in enumerate(out_refs):
        out_ref[...] = (keep_ref[n + 1].astype(wide) + more_ref[n + 1].astype(wide)).astype(low)


def total_kernel(own_ref, *refs):
    total = own_ref[...]
    for ref in refs[:-2]:
        total = total + ref[...].astype(wide)
    refs[-2][...] = total[:3]
    refs[-1][...] = total[3]


def input_grad_kernel(grad_ref, own_ref, more_ref, input_ref, gain_ref, out_ref):
    hat, inverse = normalize(input_ref[...].astype(wide))
    upstream = own_ref[...] + more_ref[...].astype(wide)
    out_ref[...] = grad_ref[...] + norm_back(upstream, hat, inverse, gain_ref[...])


def across(values):
    return lax.ppermute(values, "tp", [(0, 1), (1, 0)])


def swapped(values, offset):
    if offset == 0:
        return values
    count = lax.axis_size("fsdp")
    return lax.ppermute(values, "fsdp", [(i, i ^ offset) for i in range(count)])


def after(values, *earlier):
    return lax.optimization_barrier((values, earlier))[0]


def reduce_blocks(blocks, index, count):
    bit = 0
    part = blocks
    while count > 1:
        mine = (index >> bit) & 1
        split = part.reshape(count // 2, 2, *blocks.shape[1:])
        keep = lax.dynamic_index_in_dim(split, mine, 1, keepdims=False)
        give = lax.dynamic_index_in_dim(split, 1 - mine, 1, keepdims=False)
        got = swapped(give.astype(low), 1 << bit)
        part = keep.astype(wide) + got.astype(wide)
        if count > 2:
            part = part.astype(low)
        count //= 2
        bit += 1
    return part[0]


def tree_masks(lengths, parents, tree_size):
    segment_count = lengths.shape[0]
    number = jnp.arange(segment_count, dtype=jnp.int32)
    segment_end = jnp.sum(jnp.where(number[None, :] <= number[:, None], lengths[None, :], 0), axis=1)
    starts = segment_end - lengths
    position = jnp.arange(tree_size, dtype=jnp.int32)
    member = (
        (position[:, None] >= starts[None, :]) & (position[:, None] < segment_end[None, :])
    ).astype(wide)
    closure = jnp.maximum(
        jnp.eye(segment_count, dtype=wide), (parents[:, None] == number[None, :]).astype(wide)
    )
    steps = 1
    while steps < segment_count:
        closure = jnp.minimum(jnp.dot(closure, closure), 1.0)
        steps *= 2
    unreached = (1.0 - jnp.dot(member, closure)) * masked_score
    padding = ((0, 0), (0, LANES - segment_count))
    return jnp.pad(unreached, padding).astype(low), jnp.pad(member, padding).astype(low)


def shards(
    inputs,
    token_ids,
    hash_table,
    segment_lengths,
    segment_parents,
    first_gain,
    first_bias,
    input_weight,
    output_weight,
    second_gain,
    second_bias,
    expert_in,
    expert_out,
    cotangent,
):
    own_count, width = inputs.shape
    experts_in_all = lax.axis_size("fsdp")
    tree_size = token_ids.shape[0]
    capacity = 2 * own_count // experts_in_all
    local_width = input_weight.shape[2]
    chips = experts_in_all // 2
    shard_rows = input_weight.shape[1]
    hidden = expert_in.shape[2]
    index = lax.axis_index("fsdp")
    side = lax.axis_index("tp")
    place = jnp.stack([index, side]).astype(jnp.int32)
    in_kernel = shard_rows % 16 == 0
    first_gain, first_bias = first_gain[None], first_bias[None]
    second_gain, second_bias = second_gain[None], second_bias[None]

    other_inputs = across(inputs)
    shard = jnp.concatenate([input_weight, output_weight.T[None]])
    pieces = {0: shard}
    for k in range(2, chips, 2):
        pieces[k] = swapped(shard, 2 * k)
    for k in range(1, chips, 2):
        pieces[k] = swapped(pieces[k - 1], 2)
    mine = jnp.stack([pieces[k] for k in range(chips)])
    sibling = swapped(mine, 1)

    own_ids = lax.dynamic_slice_in_dim(token_ids, side * own_count, own_count, 0)
    table = hash_table.reshape(-1, LANES).astype(low)
    row_hot = (own_ids[:, None] // LANES == jnp.arange(table.shape[0])[None, :]).astype(low)
    lane_hot = own_ids[:, None] % LANES == jnp.arange(LANES)[None, :]
    experts = jnp.sum(jnp.where(lane_hot, dot(row_hot, table), 0.0), axis=1).astype(jnp.int32)
    hot = (experts[:, None] == jnp.arange(experts_in_all)[None, :]).astype(low)
    earlier = (jnp.arange(own_count)[:, None] > jnp.arange(own_count)[None, :]).astype(low)
    rank = jnp.sum(dot(earlier, hot) * hot.astype(wide), axis=1).astype(jnp.int32)
    own_slot = experts * capacity + rank
    sibling_slot = swapped(own_slot, 1)

    def chip_slot(slot):
        offset = (slot // capacity) ^ index
        return jnp.where(offset & 1 == 0, (offset >> 1) * capacity + slot % capacity, -1)

    own_place, sibling_place = chip_slot(own_slot), chip_slot(sibling_slot)

    slot_count = experts_in_all * capacity
    straight = (own_slot[None, :] == jnp.arange(slot_count)[:, None]).astype(low)
    packed_grads = after(dot(straight, cotangent).astype(low), mine)
    slot_grads = lax.all_to_all(
        packed_grads.reshape(experts_in_all, capacity, width), "fsdp", 0, 0, tiled=True
    )
    more_slot_grads = across(slot_grads)

    if in_kernel:
        weights = (mine, sibling)
    else:
        both = jnp.stack([mine, sibling], 1)
        both = both.reshape(experts_in_all, 4, shard_rows, local_width)
        full = jnp.concatenate(
            [lax.dynamic_index_in_dim(both, index ^ n, 0, False) for n in range(experts_in_all)], axis=1
        )
        weights = (full, full[:1, :16])
    full_weight, projected = run(
        functools.partial(project_kernel, chips if in_kernel else 0),
        (place, inputs, other_inputs, first_gain, first_bias, *weights),
        [array((4, width, local_width), low), array((tree_size, 3 * local_width), low)],
        flops=2 * tree_size * width * 3 * local_width,
    )
    out_weight = full_weight[3]
    other_out_weight = across(out_weight)
    unreached, member = tree_masks(segment_lengths[0], segment_parents[0], tree_size)
    attended, totals, attended_keep, attended_give = attend(place, projected, unreached, member)
    attended_more = across(attended_give)
    middle, second_normed = run(
        branch_kernel,
        (attended_keep, attended_more, out_weight, other_out_weight, inputs, second_gain, second_bias),
        [array((own_count, width), wide), array((own_count, width), low)],
        flops=2 * own_count * width * width,
    )

    sibling_normed = swapped(second_normed, 1)
    piece = array((2, capacity, width), low)
    packed = run(
        pack_kernel,
        (second_normed, sibling_normed, own_place[None], sibling_place[None]),
        [piece] * chips,
        flops=4 * own_count * own_count * width,
    )
    packed = after(packed, slot_grads)
    spans = [(0, chips // 2), (chips // 2, 3 * chips // 4), (3 * chips // 4, chips)]
    arrived = {}
    for k in range(*spans[1]):
        arrived[k] = swapped(packed[k], 2 * k)
    for k in range(*spans[0]):
        arrived[k] = swapped(packed[k], 2 * k)
    for k in range(*spans[2]):
        arrived[k] = swapped(after(packed[k], *[arrived[n] for n in range(*spans[0])]), 2 * k)
    more_arrived = {k: across(arrived[k]) for k in range(chips)}

    weight_in, weight_out = expert_in[0], expert_out[0]
    buffers = None
    returned = []
    for span in spans:
        buffers, keep, give = expert_group(
            place, weight_in, weight_out, slot_grads, more_slot_grads,
            [arrived[k] for k in range(*span)], [more_arrived[k] for k in range(*span)],
            buffers, span, chips,
        )
        sums = run(pieces_kernel, (keep, across(give)), [piece] * (span[1] - span[0]))
        returned += [swapped(sums[k - span[0]], 2 * k) for k in range(*span)]
    own_part, sibling_part = run(
        unpack_kernel,
        (own_place[:, None], sibling_place[:, None], *returned),
        [array((own_count, width), low)] * 2,
        flops=4 * own_count * own_count * width,
    )
    sibling_part = swapped(sibling_part, 1)
    slot_rows, grad_rows, actives, grad_pres = after(buffers, *sums)
    rows = 4 * capacity
    ffn_keep, ffn_give = run(
        ffn_kernel,
        (actives, weight_out),
        [array((chips, rows // 2, width), wide), array((chips, rows // 2, width), low)],
        flops=2 * chips * rows * width * hidden,
        grid=(chips,),
        in_specs=[
            pl.BlockSpec((1, rows, hidden), lambda i: (i, 0, 0)),
            pl.BlockSpec((hidden, width), lambda i: (0, 0)),
        ],
        out_specs=[pl.BlockSpec((1, rows // 2, width), lambda i: (i, 0, 0))] * 2,
    )
    ffn_sums = run(
        ffn_sum_kernel, (place, ffn_keep, across(ffn_give)), array((experts_in_all, capacity, width), low)
    )
    ffn_back = lax.all_to_all(ffn_sums, "fsdp", 0, 0, tiled=True)
    grad_rows, slot_rows = grad_rows.reshape(-1, width), slot_rows.reshape(-1, width)
    expert_out_grad = dot(actives.reshape(-1, hidden), grad_rows, TN)
    expert_in_grad = dot(slot_rows, grad_pres.reshape(-1, hidden), TN)

    grad_middle, grad_branch, grad_mine, grad_give, second_sums = run(
        middle_back_kernel,
        (own_part, sibling_part, middle, cotangent, second_gain, out_weight, other_out_weight),
        [
            array((own_count, width), wide),
            array((own_count, width), low),
            array((own_count, local_width), low),
            array((own_count, local_width), low),
            array((2, width), wide),
        ],
        flops=2 * own_count * width * width,
    )
    grad_more = across(grad_give)
    output_own, output_give = run(
        output_part_kernel,
        (grad_branch, attended_keep, attended_more),
        [array((width, local_width), wide), array((width, local_width), low)],
        flops=2 * own_count * width * width,
    )
    output_more = across(output_give)
    grad_projected = attend_back(
        place, projected, unreached, member, attended, totals, grad_mine, grad_more
    )

    first_give = run(
        first_give_kernel,
        (place, grad_projected, full_weight),
        array((own_count, width), low),
        flops=2 * own_count * width * 3 * local_width,
    )
    first_more = across(first_give)
    if in_kernel:
        block = array((2, chips // 2, 4, shard_rows, local_width), low)
        part_outs = [block, block]
    else:
        part_outs = [array((4, width, local_width), low), array((8, LANES), low)]
    part_keep, part_give = run(
        functools.partial(weight_part_kernel, chips if in_kernel else 0),
        (place, inputs, other_inputs, first_gain, first_bias, grad_projected, output_own, output_more),
        part_outs,
        flops=2 * tree_size * width * 3 * local_width,
        scratch_shapes=[
            pltpu.VMEM((tree_size, width), low),
            pltpu.VMEM((4, width, local_width), low),
        ],
    )
    if in_kernel:
        part_more = swapped(part_give, 1)
        quarter = array((chips // 2, 4, shard_rows, local_width), low)
        near, far = run(halves_kernel, (part_keep, part_more), [quarter, quarter])
        shape = (4, shard_rows, local_width)
        own_sum, *away = run(
            quarters_kernel,
            (near, swapped(far, 2)),
            [array(shape, wide)] + [array(shape, low)] * (chips // 2 - 1),
        )
        away = [swapped(away[k - 1], 4 * k) for k in range(1, chips // 2)]
        input_weight_grad, output_weight_grad = run(
            total_kernel, (own_sum, *away), [array((3, *shape[1:]), wide), array(shape[1:], wide)]
        )
    else:
        blocks = part_keep.reshape(4, experts_in_all, shard_rows, local_width).transpose(1, 0, 2, 3)
        summed = reduce_blocks(blocks, index, experts_in_all)
        input_weight_grad, output_weight_grad = summed[:3], summed[3]
    output_weight_grad = output_weight_grad.T
    first_own, first_sums = run(
        first_own_kernel,
        (place, grad_projected, full_weight, first_give, inputs, other_inputs),
        [array((own_count, width), wide), array((2, width), wide)],
        flops=2 * own_count * width * 3 * local_width,
    )
    norm_sums = jnp.concatenate([first_sums, second_sums])
    bit = 1
    while bit < experts_in_all:
        norm_sums = norm_sums + swapped(norm_sums, bit)
        bit *= 2
    norm_sums = norm_sums + across(norm_sums)
    input_grad = run(
        input_grad_kernel,
        (grad_middle, first_own, first_more, inputs, first_gain),
        array((own_count, width), wide),
    )
    out_block = run(
        out_kernel,
        (own_slot[:, None], ffn_back.reshape(slot_count, width), middle),
        array((own_count, width), low),
        flops=2 * own_count * slot_count * width,
    )
    return (
        out_block,
        input_grad,
        norm_sums[0],
        norm_sums[1],
        input_weight_grad,
        output_weight_grad,
        norm_sums[2],
        norm_sums[3],
        expert_in_grad[None],
        expert_out_grad[None],
    )


def solution(mesh):
    return jax.shard_map(
        shards,
        mesh=mesh,
        in_specs=(
            P(("fsdp", "tp"), None),
            P("fsdp"),
            P(),
            P("fsdp", None),
            P("fsdp", None),
            P(),
            P(),
            P(None, "fsdp", "tp"),
            P("tp", "fsdp"),
            P(),
            P(),
            P("fsdp", None, "tp"),
            P("fsdp", "tp", None),
            P(("fsdp", "tp"), None),
        ),
        out_specs=(
            P(("fsdp", "tp"), None),
            P(("fsdp", "tp"), None),
            P(),
            P(),
            P(None, "fsdp", "tp"),
            P("tp", "fsdp"),
            P(),
            P(),
            P("fsdp", None, "tp"),
            P("fsdp", "tp", None),
        ),
        check_vma=False,
    )
```

profile of v0, /device:TPU:0, one launch (start us, length us, event | category | flops | bytes accessed | tf_op | source)
XLA Modules:
  0.0 364.7 jit_solution(13607953010973893838)
XLA Ops:
  28.5 5.3 %all-to-all-start = ((bf16[16,64,768]{2,1,0:T(8,128)(2,1)}), bf16[16,64,768]{2,1,0:T(8,128)(2,1)S(1)}, u32[]{:S(2)}, u32[]{:S(2)}) async-start(bf16[16,64,768]{2,1,0:T(8,128)(2,1)} %bitcast.73), calls=%async_computation | async-start | bytes 3145728 | tf_op jit(solution)/shard_map/all_to_all | solution.py:593
  35.0 5.2 %shard_map.213 = (bf16[4,768,384]{2,1,0:T(8,128)(2,1)S(1)}, bf16[1024,1152]{1,0:T(8,128)(2,1)S(1)}) custom-call(s32[2]{0:T(128)S(1)} %pad_add_fusion.place_ref, bf16[512,768]{1,0:T(8,128)(2,1)S(1)} %copy-done.14, bf16[512,768]{1,0:T(8,128)(2,1)S(1)} %collective-permute-done.8.other_ref.other_in_ref, f32[1,768]{1,0:T(1,128)S(1)} %broadcast_in_dim.70.gain_ref, ...), custom_call_target="tpu_custom_call" | custom-call | flops 1811939328 | bytes 8656904 | tf_op jit(solution)/shard_map/pallas_call | solution.py:66
  42.2 9.3 %shard_map.214 = (bf16[1024,384]{1,0:T(8,128)(2,1)S(1)}, f32[1024,384]{1,0:T(8,128)S(1)}, bf16[512,384]{1,0:T(8,128)(2,1)S(1)}, bf16[512,384]{1,0:T(8,128)(2,1)}) custom-call(s32[2]{0:T(128)S(1)} %pad_add_fusion.place_ref, bf16[1024,1152]{1,0:T(8,128)(2,1)S(1)} %get-tuple-element.91.q_ref.k_ref.v_ref, ...), custom_call_target="tpu_custom_call" | custom-call | flops 12000000000 | bytes 10747912 | tf_op jit(solution)/shard_map/pallas_call | solution.py:66
  56.6 9.2 %all-to-all-done.grads_ref = bf16[16,64,768]{2,1,0:T(8,128)(2,1)S(1)} async-done(((bf16[16,64,768]{2,1,0:T(8,128)(2,1)}), bf16[16,64,768]{2,1,0:T(8,128)(2,1)S(1)}, u32[]{:S(2)}, u32[]{:S(2)}) %all-to-all-start) | async-done | bytes 1572896 | tf_op jit(solution)/shard_map/all_to_all | solution.py:593
  76.4 4.6 %collective-permute-start.15 = (bf16[2,64,768]{2,1,0:T(8,128)(2,1)S(1)}, bf16[2,64,768]{2,1,0:T(8,128)(2,1)S(1)}, u32[]{:S(2)}, u32[]{:S(2)}) collective-permute-start(bf16[2,64,768]{2,1,0:T(8,128)(2,1)S(1)} %get-tuple-element.107), channel_id=1, source_target_pairs={{0,8},{2,10},{4,12},{6,14},{8,0},{10,2},{12,4},{14,6},{16,24},{18,... | collective-permute-start | bytes 589832 | tf_op jit(solution)/shard_map/ppermute | solution.py:487
  82.6 5.2 %collective-permute-start.21 = (bf16[2,64,768]{2,1,0:T(8,128)(2,1)S(1)}, bf16[2,64,768]{2,1,0:T(8,128)(2,1)S(1)}, u32[]{:S(2)}, u32[]{:S(2)}) collective-permute-start(bf16[2,64,768]{2,1,0:T(8,128)(2,1)S(1)} %get-tuple-element.112), channel_id=1, source_target_pairs={{0,16},{2,18},{4,20},{6,22},{8,24},{10,26},{12,28},{14,30},{16,0},... | collective-permute-start | bytes 589832 | tf_op jit(solution)/shard_map/ppermute | solution.py:487
  90.1 4.6 %collective-permute-done.16.refs_3_ = bf16[2,64,768]{2,1,0:T(8,128)(2,1)S(1)} collective-permute-done((bf16[2,64,768]{2,1,0:T(8,128)(2,1)S(1)}, bf16[2,64,768]{2,1,0:T(8,128)(2,1)S(1)}, u32[]{:S(2)}, u32[]{:S(2)}) %collective-permute-start.16) | collective-permute-done | bytes 196640 | tf_op jit(solution)/shard_map/ppermute | solution.py:487
  96.2 11.0 %collective-permute-done.25.refs_4_ = bf16[2,64,768]{2,1,0:T(8,128)(2,1)S(1)} collective-permute-done((bf16[2,64,768]{2,1,0:T(8,128)(2,1)S(1)}, bf16[2,64,768]{2,1,0:T(8,128)(2,1)S(1)}, u32[]{:S(2)}, u32[]{:S(2)}) %collective-permute-start.25) | collective-permute-done | bytes 196640 | tf_op jit(solution)/shard_map/ppermute | solution.py:480
  109.3 7.7 %collective-permute-start.18 = (bf16[2,64,768]{2,1,0:T(8,128)(2,1)S(1)}, bf16[2,64,768]{2,1,0:T(8,128)(2,1)S(1)}, u32[]{:S(2)}, u32[]{:S(2)}) collective-permute-start(bf16[2,64,768]{2,1,0:T(8,128)(2,1)S(1)} %get-tuple-element.111), channel_id=1, source_target_pairs={{0,28},{2,30},{4,24},{6,26},{8,20},{10,22},{12,16},{14,18},{16,12}... | collective-permute-start | bytes 589832 | tf_op jit(solution)/shard_map/ppermute | solution.py:487
  125.1 11.8 %shard_map.217 = (bf16[8,256,768]{2,1,0:T(8,128)(2,1)S(1)}, bf16[8,256,768]{2,1,0:T(8,128)(2,1)S(1)}, bf16[8,256,1536]{2,1,0:T(8,128)(2,1)}, bf16[8,256,1536]{2,...) custom-call(s32[2]{0:T(128)S(1)} %pad_add_fusion.place_ref, bf16[768,1536]{1,0:T(8,128)(2,1)S(1)} %bitcast.62, ...), custom_call_target="tpu_custom_call" | custom-call | flops 7247757312 | bytes 30670856 | tf_op jit(solution)/shard_map/pallas_call | solution.py:66
  143.8 6.6 %shard_map.218 = (bf16[8,256,768]{2,1,0:T(8,128)(2,1)S(1)}, bf16[8,256,768]{2,1,0:T(8,128)(2,1)S(1)}, bf16[8,256,1536]{2,1,0:T(8,128)(2,1)S(1)}, bf16[8,256,1536...) custom-call(s32[2]{0:T(128)S(1)} %pad_add_fusion.place_ref, ...), custom_call_target="tpu_custom_call", output_to_operand_aliasing={{0}: (9, {}), {1}: (10, {}), {2}: (11, {}), {3}: (12, {})} | custom-call | flops 3623878656 | bytes 47579144 | tf_op jit(solution)/shard_map/pallas_call | solution.py:66
  150.9 6.4 %shard_map.219 = (bf16[8,256,768]{2,1,0:T(8,128)(2,1)S(1)}, bf16[8,256,768]{2,1,0:T(8,128)(2,1)S(1)}, bf16[8,256,1536]{2,1,0:T(8,128)(2,1)S(1)}, bf16[8,256,1536...) custom-call(s32[2]{0:T(128)S(1)} %pad_add_fusion.place_ref, ...), custom_call_target="tpu_custom_call", output_to_operand_aliasing={{0}: (9, {}), {1}: (10, {}), {2}: (11, {}), {3}: (12, {})} | custom-call | flops 3623878656 | bytes 47579144 | tf_op jit(solution)/shard_map/pallas_call | solution.py:66
  165.6 8.9 %collective-permute-start.36 = (bf16[2,64,768]{2,1,0:T(8,128)(2,1)}, bf16[2,64,768]{2,1,0:T(8,128)(2,1)S(1)}, u32[]{:S(2)}, u32[]{:S(2)}) collective-permute-start(bf16[2,64,768]{2,1,0:T(8,128)(2,1)} %get-tuple-element.142), channel_id=1, source_target_pairs={{0,16},{2,18},{4,20},{6,22},{8,24},{10,26},{12,28},{14,30},{16,0},... | collective-permute-start | bytes 589832 | tf_op jit(solution)/shard_map/ppermute | solution.py:487
  189.8 7.4 %collective-permute-done.36.refs_4_ = bf16[2,64,768]{2,1,0:T(8,128)(2,1)S(1)} collective-permute-done((bf16[2,64,768]{2,1,0:T(8,128)(2,1)}, bf16[2,64,768]{2,1,0:T(8,128)(2,1)S(1)}, u32[]{:S(2)}, u32[]{:S(2)}) %collective-permute-start.36) | collective-permute-done | bytes 196640 | tf_op jit(solution)/shard_map/ppermute | solution.py:487
  197.8 5.2 %collective-permute-done.37.refs_5_ = bf16[2,64,768]{2,1,0:T(8,128)(2,1)} collective-permute-done((bf16[2,64,768]{2,1,0:T(8,128)(2,1)}, bf16[2,64,768]{2,1,0:T(8,128)(2,1)}, u32[]{:S(2)}, u32[]{:S(2)}) %collective-permute-start.37) | collective-permute-done | bytes 196640 | tf_op jit(solution)/shard_map/ppermute | solution.py:487
  226.2 6.3 %shard_map.221 = (f32[8,128,768]{2,1,0:T(8,128)S(1)}, bf16[8,128,768]{2,1,0:T(8,128)(2,1)S(1)}) custom-call(bf16[8,256,1536]{2,1,0:T(8,128)(2,1)S(1)} %bitcast.59, bf16[1536,768]{1,0:T(8,128)(2,1)S(1)} %bitcast.68), custom_call_target="tpu_custom_call" | custom-call | flops 4831838208 | bytes 13369344 | tf_op jit(solution)/shard_map/pallas_call | solution.py:66
  236.7 14.9 %shard_map.228.grads_ref = bf16[3,1024,384]{2,1,0:T(8,128)(2,1)S(1)} custom-call(s32[2]{0:T(128)S(1)} %pad_add_fusion.place_ref, bf16[1024,1152]{1,0:T(8,128)(2,1)S(1)} %copy-done.51, bf16[1024,1152]{1,0:T(8,128)(2,1)S(1)} %copy-done.51, bf16[1024,1152]{1,0:T(8,128)(2,1)S(1)} %copy-done.51, bf16[1024,128]{1,0:T(8,128)(2,1)S(1)} %copy-done.40, ...), custom_call_target="tpu_custom_call" | custom-call | flops 24000000000 | bytes 13107208 | tf_op jit(solution)/shard_map/pallas_call | solution.py:66
  251.7 30.4 %collective-permute-done.48.more_ref = bf16[768,384]{1,0:T(8,128)(2,1)S(1)} collective-permute-done((bf16[768,384]{1,0:T(8,128)(2,1)S(1)}, bf16[768,384]{1,0:T(8,128)(2,1)S(1)}, u32[]{:S(2)}, u32[]{:S(2)}) %collective-permute-start.48) | collective-permute-done | bytes 589856 | tf_op jit(solution)/shard_map/ppermute | solution.py:480
  282.1 6.1 %shard_map.233 = (bf16[2,4,4,48,384]{4,3,2,1,0:T(8,128)(2,1)S(1)}, bf16[2,4,4,48,384]{4,3,2,1,0:T(8,128)(2,1)}) custom-call(s32[2]{0:T(128)S(1)} %pad_add_fusion.place_ref, bf16[512,768]{1,0:T(8,128)(2,1)S(1)} %copy-done.14, bf16[512,768]{1,0:T(8,128)(2,1)S(1)} %copy-done.30, f32[1,768]{1,0:T(1,128)S(1)} %broadcast_in_dim.70.gain_ref, ...), custom_call_target="tpu_custom_call" | custom-call | flops 1811939328 | bytes 8067080 | tf_op jit(solution)/shard_map/pallas_call | solution.py:66
  291.4 5.9 %all-to-all-start.1 = ((bf16[16,64,768]{2,1,0:T(8,128)(2,1)}), bf16[16,64,768]{2,1,0:T(8,128)(2,1)}, u32[]{:S(2)}, u32[]{:S(2)}) async-start(bf16[16,64,768]{2,1,0:T(8,128)(2,1)} %copy-done.17), calls=%async_computation.1 | async-start | bytes 3145728 | tf_op jit(solution)/shard_map/all_to_all | solution.py:679
  312.5 11.4 %collective-permute-done.45 = f32[4,768]{1,0:T(4,128)S(1)} collective-permute-done((f32[4,768]{1,0:T(4,128)S(1)}, f32[4,768]{1,0:T(4,128)S(1)}, u32[]{:S(2)}, u32[]{:S(2)}) %collective-permute-start.45) | collective-permute-done | bytes 12320 | tf_op jit(solution)/shard_map/ppermute | solution.py:487
  323.9 4.4 %collective-permute-start.46 = (f32[4,768]{1,0:T(4,128)S(1)}, f32[4,768]{1,0:T(4,128)S(1)}, u32[]{:S(2)}, u32[]{:S(2)}) collective-permute-start(f32[4,768]{1,0:T(4,128)S(1)} %add.136), channel_id=1, source_target_pairs={{0,16},{2,18},{4,20},{6,22},{8,24},{10,26},{12,28},{14,30},{16,0},... | collective-permute-start | bytes 36872 | tf_op jit(solution)/shard_map/ppermute | solution.py:487
  331.6 6.9 %convolution_bitcast_fusion = f32[1,1536,768]{2,1,0:T(8,128)} fusion(bf16[8,256,1536]{2,1,0:T(8,128)(2,1)S(1)} %bitcast.61, bf16[8,256,768]{2,1,0:T(8,128)(2,1)S(1)} %copy-done.5), kind=kOutput, calls=%fused_computation | convolution fusion | flops 4831838208 | bytes 14155776 | tf_op jit(solution)/shard_map/dot_general | solution.py:26
  349.3 6.8 %convolution_bitcast_fusion.1 = f32[1,768,1536]{2,1,0:T(8,128)} fusion(bf16[8,256,768]{2,1,0:T(8,128)(2,1)S(1)} %copy-done.3, bf16[8,256,1536]{2,1,0:T(8,128)(2,1)S(1)} %bitcast.72), kind=kOutput, calls=%fused_computation.1 | convolution fusion | flops 4831838208 | bytes 14155776 | tf_op jit(solution)/shard_map/dot_general | solution.py:26
  (300 shorter events, 161.5 us)
Async XLA Ops:
  1.6 20.5 %collective-permute-start = (bf16[4,48,384]{2,1,0:T(8,128)(2,1)S(1)}, bf16[4,48,384]{2,1,0:T(8,128)(2,1)S(1)}, u32[]{:S(2)}, u32[]{:S(2)}) collective-permute-start(bf16[4,48,384]{2,1,0:T(8,128)(2,1)S(1)} %pad_maximum_fusion), channel_id=1, source_target_pairs={{0,4},{2,6},{4,0},{6,2},{8,12},{10,14},{12,8},{14,10},{16,20},{18,... | collective-permute-start | bytes 442376 | tf_op jit(solution)/shard_map/ppermute | solution.py:487
  9.0 26.0 %collective-permute-start.8 = (bf16[512,768]{1,0:T(8,128)(2,1)}, bf16[512,768]{1,0:T(8,128)(2,1)S(1)}, u32[]{:S(2)}, u32[]{:S(2)}) collective-permute-start(bf16[512,768]{1,0:T(8,128)(2,1)} %own_ref.3), channel_id=1, source_target_pairs={{0,1},{1,0},{2,3},{3,2},{4,5},{5,4},{6,7},{7,6},{8,9},{9,8},{10,11... | collective-permute-start | bytes 2359304 | tf_op jit(solution)/shard_map/ppermute | solution.py:480
  28.5 37.3 %all-to-all-start = ((bf16[16,64,768]{2,1,0:T(8,128)(2,1)}), bf16[16,64,768]{2,1,0:T(8,128)(2,1)S(1)}, u32[]{:S(2)}, u32[]{:S(2)}) async-start(bf16[16,64,768]{2,1,0:T(8,128)(2,1)} %bitcast.73), calls=%async_computation | async-start | bytes 3145728 | tf_op jit(solution)/shard_map/all_to_all | solution.py:593
  41.7 24.9 %collective-permute-start.11 = (bf16[768,384]{1,0:T(8,128)(2,1)S(1)}, bf16[768,384]{1,0:T(8,128)(2,1)}, u32[]{:S(2)}, u32[]{:S(2)}) collective-permute-start(bf16[768,384]{1,0:T(8,128)(2,1)S(1)} %slice_bitcast_fusion.weight_ref), channel_id=1, source_target_pairs={{0,1},{1,0},{2,3},{3,2},{4,5},{5,4},{6,7},{7,6},{8,9},{9,8},{10,11... | collective-permute-start | bytes 1769480 | tf_op jit(solution)/shard_map/ppermute | solution.py:480
  65.8 59.3 %collective-permute-start.7 = (bf16[16,64,768]{2,1,0:T(8,128)(2,1)S(1)}, bf16[16,64,768]{2,1,0:T(8,128)(2,1)S(1)}, u32[]{:S(2)}, u32[]{:S(2)}) collective-permute-start(bf16[16,64,768]{2,1,0:T(8,128)(2,1)S(1)} %all-to-all-done.grads_ref), channel_id=1, source_target_pairs={{0,1},{1,0},{2,3},{3,2},{4,5},{5,4},{6,7},{7,6},{8,9},{9,8},{10,11... | collective-permute-start | bytes 4718600 | tf_op jit(solution)/shard_map/ppermute | solution.py:480
  81.1 26.2 %collective-permute-start.25 = (bf16[2,64,768]{2,1,0:T(8,128)(2,1)S(1)}, bf16[2,64,768]{2,1,0:T(8,128)(2,1)S(1)}, u32[]{:S(2)}, u32[]{:S(2)}) collective-permute-start(bf16[2,64,768]{2,1,0:T(8,128)(2,1)S(1)} %get-tuple-element.105.refs_0_), channel_id=1, source_target_pairs={{0,1},{1,0},{2,3},{3,2},{4,5},{5,4},{6,7},{7,6},{8,9},{9,8},{10,11... | collective-permute-start | bytes 589832 | tf_op jit(solution)/shard_map/ppermute | solution.py:480
  82.6 25.2 %collective-permute-start.21 = (bf16[2,64,768]{2,1,0:T(8,128)(2,1)S(1)}, bf16[2,64,768]{2,1,0:T(8,128)(2,1)S(1)}, u32[]{:S(2)}, u32[]{:S(2)}) collective-permute-start(bf16[2,64,768]{2,1,0:T(8,128)(2,1)S(1)} %get-tuple-element.112), channel_id=1, source_target_pairs={{0,16},{2,18},{4,20},{6,22},{8,24},{10,26},{12,28},{14,30},{16,0},... | collective-permute-start | bytes 589832 | tf_op jit(solution)/shard_map/ppermute | solution.py:487
  87.8 21.5 %collective-permute-start.22 = (bf16[2,64,768]{2,1,0:T(8,128)(2,1)S(1)}, bf16[2,64,768]{2,1,0:T(8,128)(2,1)S(1)}, u32[]{:S(2)}, u32[]{:S(2)}) collective-permute-start(bf16[2,64,768]{2,1,0:T(8,128)(2,1)S(1)} %get-tuple-element.113), channel_id=1, source_target_pairs={{0,20},{2,22},{4,16},{6,18},{8,28},{10,30},{12,24},{14,26},{16,4},... | collective-permute-start | bytes 589832 | tf_op jit(solution)/shard_map/ppermute | solution.py:487
  94.7 22.3 %collective-permute-start.26 = (bf16[2,64,768]{2,1,0:T(8,128)(2,1)S(1)}, bf16[2,64,768]{2,1,0:T(8,128)(2,1)S(1)}, u32[]{:S(2)}, u32[]{:S(2)}) collective-permute-start(bf16[2,64,768]{2,1,0:T(8,128)(2,1)S(1)} %collective-permute-done.14.refs_1_), channel_id=1, source_target_pairs={{0,1},{1,0},{2,3},{3,2},{4,5},{5,4},{6,7},{7,6},{8,9},{9,8},{10,11... | collective-permute-start | bytes 589832 | tf_op jit(solution)/shard_map/ppermute | solution.py:480
  117.0 22.6 %collective-permute-start.23 = (bf16[2,64,768]{2,1,0:T(8,128)(2,1)S(1)}, bf16[2,64,768]{2,1,0:T(8,128)(2,1)S(1)}, u32[]{:S(2)}, u32[]{:S(2)}) collective-permute-start(bf16[2,64,768]{2,1,0:T(8,128)(2,1)S(1)} %collective-permute-done.21.refs_0_), channel_id=1, source_target_pairs={{0,1},{1,0},{2,3},{3,2},{4,5},{5,4},{6,7},{7,6},{8,9},{9,8},{10,11... | collective-permute-start | bytes 589832 | tf_op jit(solution)/shard_map/ppermute | solution.py:480
  119.9 19.7 %collective-permute-start.24 = (bf16[2,64,768]{2,1,0:T(8,128)(2,1)S(1)}, bf16[2,64,768]{2,1,0:T(8,128)(2,1)S(1)}, u32[]{:S(2)}, u32[]{:S(2)}) collective-permute-start(bf16[2,64,768]{2,1,0:T(8,128)(2,1)S(1)} %collective-permute-done.22.refs_1_), channel_id=1, source_target_pairs={{0,1},{1,0},{2,3},{3,2},{4,5},{5,4},{6,7},{7,6},{8,9},{9,8},{10,11... | collective-permute-start | bytes 589832 | tf_op jit(solution)/shard_map/ppermute | solution.py:480
  122.5 28.4 %collective-permute-start.20 = (bf16[2,64,768]{2,1,0:T(8,128)(2,1)S(1)}, bf16[2,64,768]{2,1,0:T(8,128)(2,1)S(1)}, u32[]{:S(2)}, u32[]{:S(2)}) collective-permute-start(bf16[2,64,768]{2,1,0:T(8,128)(2,1)S(1)} %collective-permute-done.18.refs_1_), channel_id=1, source_target_pairs={{0,1},{1,0},{2,3},{3,2},{4,5},{5,4},{6,7},{7,6},{8,9},{9,8},{10,11... | collective-permute-start | bytes 589832 | tf_op jit(solution)/shard_map/ppermute | solution.py:480
  124.6 26.3 %collective-permute-start.19 = (bf16[2,64,768]{2,1,0:T(8,128)(2,1)S(1)}, bf16[2,64,768]{2,1,0:T(8,128)(2,1)S(1)}, u32[]{:S(2)}, u32[]{:S(2)}) collective-permute-start(bf16[2,64,768]{2,1,0:T(8,128)(2,1)S(1)} %collective-permute-done.17.refs_0_), channel_id=1, source_target_pairs={{0,1},{1,0},{2,3},{3,2},{4,5},{5,4},{6,7},{7,6},{8,9},{9,8},{10,11... | collective-permute-start | bytes 589832 | tf_op jit(solution)/shard_map/ppermute | solution.py:480
  138.1 46.1 %collective-permute-start.31 = (bf16[4,128,768]{2,1,0:T(8,128)(2,1)}, bf16[4,128,768]{2,1,0:T(8,128)(2,1)}, u32[]{:S(2)}, u32[]{:S(2)}) collective-permute-start(bf16[4,128,768]{2,1,0:T(8,128)(2,1)} %get-tuple-element.135), channel_id=1, source_target_pairs={{0,1},{1,0},{2,3},{3,2},{4,5},{5,4},{6,7},{7,6},{8,9},{9,8},{10,11... | collective-permute-start | bytes 2359304 | tf_op jit(solution)/shard_map/ppermute | solution.py:480
  165.6 31.6 %collective-permute-start.36 = (bf16[2,64,768]{2,1,0:T(8,128)(2,1)}, bf16[2,64,768]{2,1,0:T(8,128)(2,1)S(1)}, u32[]{:S(2)}, u32[]{:S(2)}) collective-permute-start(bf16[2,64,768]{2,1,0:T(8,128)(2,1)} %get-tuple-element.142), channel_id=1, source_target_pairs={{0,16},{2,18},{4,20},{6,22},{8,24},{10,26},{12,28},{14,30},{16,0},... | collective-permute-start | bytes 589832 | tf_op jit(solution)/shard_map/ppermute | solution.py:487
  174.5 28.5 %collective-permute-start.37 = (bf16[2,64,768]{2,1,0:T(8,128)(2,1)}, bf16[2,64,768]{2,1,0:T(8,128)(2,1)}, u32[]{:S(2)}, u32[]{:S(2)}) collective-permute-start(bf16[2,64,768]{2,1,0:T(8,128)(2,1)} %get-tuple-element.143), channel_id=1, source_target_pairs={{0,20},{2,22},{4,16},{6,18},{8,28},{10,30},{12,24},{14,26},{16,4},... | collective-permute-start | bytes 589832 | tf_op jit(solution)/shard_map/ppermute | solution.py:487
  180.4 23.8 %collective-permute-start.38 = (bf16[2,64,768]{2,1,0:T(8,128)(2,1)}, bf16[2,64,768]{2,1,0:T(8,128)(2,1)}, u32[]{:S(2)}, u32[]{:S(2)}) collective-permute-start(bf16[2,64,768]{2,1,0:T(8,128)(2,1)} %get-tuple-element.128), channel_id=1, source_target_pairs={{0,24},{2,26},{4,28},{6,30},{8,16},{10,18},{12,20},{14,22},{16,8},... | collective-permute-start | bytes 589832 | tf_op jit(solution)/shard_map/ppermute | solution.py:487
  183.3 20.9 %collective-permute-start.39 = (bf16[2,64,768]{2,1,0:T(8,128)(2,1)}, bf16[2,64,768]{2,1,0:T(8,128)(2,1)}, u32[]{:S(2)}, u32[]{:S(2)}) collective-permute-start(bf16[2,64,768]{2,1,0:T(8,128)(2,1)} %get-tuple-element.129), channel_id=1, source_target_pairs={{0,28},{2,30},{4,24},{6,26},{8,20},{10,22},{12,16},{14,18},{16,12}... | collective-permute-start | bytes 589832 | tf_op jit(solution)/shard_map/ppermute | solution.py:487
  232.5 56.8 %collective-permute-start.30 = (bf16[8,128,768]{2,1,0:T(8,128)(2,1)S(1)}, bf16[8,128,768]{2,1,0:T(8,128)(2,1)S(1)}, u32[]{:S(2)}, u32[]{:S(2)}) collective-permute-start(bf16[8,128,768]{2,1,0:T(8,128)(2,1)S(1)} %get-tuple-element.132), channel_id=1, source_target_pairs={{0,1},{1,0},{2,3},{3,2},{4,5},{5,4},{6,7},{7,6},{8,9},{9,8},{10,11... | collective-permute-start | bytes 4718600 | tf_op jit(solution)/shard_map/ppermute | solution.py:480
  235.1 47.0 %collective-permute-start.48 = (bf16[768,384]{1,0:T(8,128)(2,1)S(1)}, bf16[768,384]{1,0:T(8,128)(2,1)S(1)}, u32[]{:S(2)}, u32[]{:S(2)}) collective-permute-start(bf16[768,384]{1,0:T(8,128)(2,1)S(1)} %get-tuple-element.156), channel_id=1, source_target_pairs={{0,1},{1,0},{2,3},{3,2},{4,5},{5,4},{6,7},{7,6},{8,9},{9,8},{10,11... | collective-permute-start | bytes 1769480 | tf_op jit(solution)/shard_map/ppermute | solution.py:480
  289.3 39.0 %collective-permute-start.49 = (bf16[2,4,4,48,384]{4,3,2,1,0:T(8,128)(2,1)}, bf16[2,4,4,48,384]{4,3,2,1,0:T(8,128)(2,1)}, u32[]{:S(2)}, u32[]{:S(2)}) collective-permute-start(bf16[2,4,4,48,384]{4,3,2,1,0:T(8,128)(2,1)} %get-tuple-element.158), channel_id=1, source_target_pairs={{0,2},{2,0},{4,6},{6,4},{8,10},{10,8},{12,14},{14,12},{16,18},{18,... | collective-permute-start | bytes 3538952 | tf_op jit(solution)/shard_map/ppermute | solution.py:487
  291.4 69.7 %all-to-all-start.1 = ((bf16[16,64,768]{2,1,0:T(8,128)(2,1)}), bf16[16,64,768]{2,1,0:T(8,128)(2,1)}, u32[]{:S(2)}, u32[]{:S(2)}) async-start(bf16[16,64,768]{2,1,0:T(8,128)(2,1)} %copy-done.17), calls=%async_computation.1 | async-start | bytes 3145728 | tf_op jit(solution)/shard_map/all_to_all | solution.py:679
  338.5 19.5 %collective-permute-start.42 = (bf16[512,768]{1,0:T(8,128)(2,1)S(1)}, bf16[512,768]{1,0:T(8,128)(2,1)S(1)}, u32[]{:S(2)}, u32[]{:S(2)}) collective-permute-start(bf16[512,768]{1,0:T(8,128)(2,1)S(1)} %shard_map.229.give_ref), channel_id=1, source_target_pairs={{0,1},{1,0},{2,3},{3,2},{4,5},{5,4},{6,7},{7,6},{8,9},{9,8},{10,11... | collective-permute-start | bytes 2359304 | tf_op jit(solution)/shard_map/ppermute | solution.py:480
  339.9 17.5 %collective-permute-start.47 = (f32[4,768]{1,0:T(4,128)S(1)}, f32[4,768]{1,0:T(4,128)S(1)}, u32[]{:S(2)}, u32[]{:S(2)}) collective-permute-start(f32[4,768]{1,0:T(4,128)S(1)} %add.137), channel_id=1, source_target_pairs={{0,1},{1,0},{2,3},{3,2},{4,5},{5,4},{6,7},{7,6},{8,9},{9,8},{10,11... | collective-permute-start | bytes 36872 | tf_op jit(solution)/shard_map/ppermute | solution.py:480
  (103 other events, 1138.0 us)
where the time goes:
time: 369 us; the launch traced here: 365 us
  waiting for transfers between devices  108 us (29%)
  Pallas kernels  95.5 us (26%)
  starting transfers between devices  95.1 us (26%)
  local copies, waits for them, and re-layouts  42.3 us (11%)
  matrix products  19.4 us (5%)
    pallas_call x24, Pallas kernels, run(): pl.pallas_call(kernel, out_shape=outs, compiler_params=pltpu.CompilerPara...  95.5 us
    ppermute x34, starting transfers between devices, swapped(): return lax.ppermute(values, 'fsdp', [(i, i ^ offset) for i in range(count)])  63.3 us
    ppermute x34, waiting for transfers between devices, swapped(): return lax.ppermute(values, 'fsdp', [(i, i ^ offset) for i in range(count)])  53 us
    ppermute x20, waiting for transfers between devices, across(): return lax.ppermute(values, 'tp', [(0, 1), (1, 0)])  45.4 us
    unnamed x148, local copies, waits for them, and re-layouts  39.2 us
    ppermute x20, starting transfers between devices, across(): return lax.ppermute(values, 'tp', [(0, 1), (1, 0)])  20.5 us
    dot_general x5, matrix products, dot(): return lax.dot_general(left, right, dims, preferred_element_type=wide)  18.7 us
    all_to_all x1, waiting for transfers between devices, shards(): lax.all_to_all(packed_grads.reshape(experts_in_all, capacity, width), 'fs...  9.23 us
  transfers between devices with their start and end apart: 56, of which 23 were waited for; matrix products, arithmetic and copies ran while one was open for 8% of the time, Pallas kernels for 24%

commit v1 on v0

--- a/solution.py
+++ b/solution.py
@@ -1,4 +1,5 @@
 import functools
+import math
 
 import jax
 import jax.numpy as jnp
@@ -28,12 +29,13 @@
 
 def gelu_both(values):
     squared = values * values
-    tangent = jnp.tanh(gelu_root * values * (1.0 + gelu_cubic * squared))
-    half_up = 0.5 * (1.0 + tangent)
-    slope = half_up + 0.5 * values * (1.0 - tangent * tangent) * gelu_root * (
-        1.0 + 3.0 * gelu_cubic * squared
-    )
-    return values * half_up, slope
+    tangent = jnp.tanh(values * (gelu_root + gelu_root * gelu_cubic * squared))
+    half_up = 0.5 + 0.5 * tangent
+    active = values * half_up
+    slope = half_up + active * (1.0 - half_up) * (
+        2.0 * gelu_root + 6.0 * gelu_root * gelu_cubic * squared
+    )
+    return active, slope
 
 
 def normalize(values):
@@ -57,45 +59,98 @@
     return jax.ShapeDtypeStruct(shape, kind)
 
 
-def run(kernel, operands, outs, flops=0, limit=32, **more):
+def kept(shape, kind):
+    return pltpu.HBM(shape, kind)
+
+
+def size_of(x):
+    return math.prod(x.shape) * jnp.dtype(x.dtype).itemsize
+
+
+def run(kernel, operands, outs, flops=0, limit=32, first=(), mark=False, **more):
     if "in_specs" not in more:
         more["in_specs"] = [spec_of(x) for x in operands]
-    moved = sum(x.size * x.dtype.itemsize for x in operands) + sum(
-        x.size * x.dtype.itemsize for x in jax.tree.leaves(outs)
-    )
-    return pl.pallas_call(
-        kernel,
+    operands = [in_hbm(x.values) if isinstance(x, Far) else x for x in operands]
+    alone = not isinstance(outs, list)
+    outs = [outs] if alone else list(outs)
+    count, results = len(operands), len(outs)
+    moved = sum(map(size_of, operands)) + sum(map(size_of, outs))
+    first = tuple(first)
+    more["in_specs"] = list(more["in_specs"]) + [pl.BlockSpec(memory_space=pl.ANY)] * len(first)
+    if mark:
+        outs.append(array((8, LANES), wide))
+    if "out_specs" in more:
+        more["out_specs"] = list(more["out_specs"])
+        if mark:
+            more["out_specs"].append(pl.BlockSpec((8, LANES), lambda *i: (0, 0)))
+
+    def whole(*refs):
+        end = count + len(first) + results
+        if mark:
+            refs[end][...] = jnp.zeros((8, LANES), wide)
+        kernel(*refs[:count], *refs[count + len(first) : end], *refs[end + mark :])
+
+    res = pl.pallas_call(
+        whole,
         out_shape=outs,
         compiler_params=pltpu.CompilerParams(vmem_limit_bytes=limit << 20),
         cost_estimate=pl.CostEstimate(flops=int(flops), bytes_accessed=int(moved), transcendentals=0),
         **more,
-    )(*operands)
+    )(*operands, *first)
+    return res[0] if alone and not mark else res
+
+
+def in_hbm(x):
+    return pltpu.with_memory_space_constraint(x, pltpu.HBM)
+
+
+class Far:
+    def __init__(self, values):
+        self.values = values
 
 
 def spec_of(x):
+    if isinstance(x, Far):
+        shape = x.values.shape
+        return pl.BlockSpec(shape, lambda *i: (0,) * len(shape))
     scalar = x.ndim == 1 and x.dtype == jnp.int32
     return pl.BlockSpec(memory_space=pltpu.SMEM if scalar else pltpu.VMEM)
 
 
-def project_kernel(chips, place_ref, own_ref, other_ref, gain_ref, bias_ref, mine_ref, sibling_ref, full_ref, out_ref):
+def project_kernel(
+    chips, place_ref, own_ref, other_ref, gain_ref, bias_ref, gain2_ref, bias2_ref, mine_ref, sibling_ref,
+    full_ref, last_ref, out_ref, scale_ref
+):
     place, side = place_ref[0], place_ref[1]
+    for n, ref in enumerate((gain_ref, bias_ref, gain2_ref, bias2_ref)):
+        scale_ref[n : n + 1] = ref[...].reshape(1, ref.shape[0])
     if chips:
         rows = mine_ref.shape[2]
         for k in range(chips):
-            source = place ^ (2 * k)
-            full_ref[:, pl.ds(pl.multiple_of(source * rows, rows), rows), :] = mine_ref[k]
-            source = source ^ 1
-            full_ref[:, pl.ds(pl.multiple_of(source * rows, rows), rows), :] = sibling_ref[k]
+            for ref, source in ((mine_ref, place ^ (2 * k)), (sibling_ref, place ^ (2 * k + 1))):
+                block = pl.ds(pl.multiple_of(source * rows, rows), rows)
+                full_ref[:, block, :] = ref[k, :3]
+                last_ref[block, :] = ref[k, 3]
     else:
-        full_ref[...] = mine_ref[...]
+        full_ref[...] = mine_ref[:3]
+        last_ref[...] = mine_ref[3]
     count, width = own_ref.shape[0], mine_ref.shape[-1]
     for ref, first in ((own_ref, side * count), (other_ref, (1 - side) * count)):
         hat, _ = normalize(ref[...].astype(wide))
-        normed = (hat * gain_ref[...] + bias_ref[...]).astype(low)
+        normed = (hat * scale_ref[0:1] + scale_ref[1:2]).astype(low)
         for n in range(3):
             out_ref[pl.ds(pl.multiple_of(first, count), count), n * width : (n + 1) * width] = dot(
                 normed, full_ref[n]
             ).astype(low)
+
+
+def turned_kernel(place_ref, own_ref, other_ref, scale_ref, out_ref):
+    side = place_ref[1]
+    count = own_ref.shape[0]
+    for ref, first in ((own_ref, side * count), (other_ref, (1 - side) * count)):
+        hat, _ = normalize(ref[...].astype(wide))
+        normed = (hat * scale_ref[0:1] + scale_ref[1:2]).T
+        out_ref[:, pl.ds(pl.multiple_of(first, count), count)] = normed.astype(low)
 
 
 def attend_kernel(block, place_ref, q_ref, k_ref, v_ref, unreached_ref, member_ref, out_ref, total_ref, keep_ref, give_ref):
@@ -147,10 +202,10 @@
     fixed = pl.BlockSpec((rows, LANES), lambda p: (0, 0))
     return run(
         functools.partial(attend_kernel, block),
-        (place, projected, projected, projected, unreached, member),
+        (place, in_hbm(projected), in_hbm(projected), in_hbm(projected), unreached, member),
         [
-            array((rows, width // 3), low),
-            array((rows, width // 3), wide),
+            kept((rows, width // 3), low),
+            kept((rows, width // 3), wide),
             array((rows // 2, width // 3), low),
             array((rows // 2, width // 3), low),
         ],
@@ -213,7 +268,7 @@
     res_ref[2] = dv[...].astype(low)
 
 
-def attend_back(place, projected, unreached, member, out, total, mine, more, block=256):
+def attend_back(place, projected, unreached, member, out, total, mine, more, block=256, first=()):
     rows, width = projected.shape
     pairs = width // (3 * LANES)
 
@@ -223,23 +278,27 @@
     fixed = pl.BlockSpec((rows, LANES), lambda p: (0, 0))
     return run(
         functools.partial(attend_back_kernel, block),
-        (place, projected, projected, projected, unreached, member, out, total, mine, more),
-        array((3, rows, width // 3), low),
+        (
+            place, in_hbm(projected), in_hbm(projected), in_hbm(projected), unreached, member,
+            in_hbm(out), in_hbm(total), mine, more,
+        ),
+        [kept((3, rows, width // 3), low)],
         flops=24e9,
+        first=first,
         grid=(pairs,),
         in_specs=[spec_of(place), part(0), part(1), part(2), fixed, fixed, part(0), part(0)]
         + [part(0, rows // 2)] * 2,
-        out_specs=pl.BlockSpec((3, rows, LANES), lambda p: (0, 0, p)),
+        out_specs=[pl.BlockSpec((3, rows, LANES), lambda p: (0, 0, p))],
         scratch_shapes=[pltpu.VMEM((rows, LANES), wide)] * 2 + [pltpu.VMEM((rows, LANES), low)],
     )
 
 
-def branch_kernel(keep_ref, more_ref, weight_ref, other_ref, residual_ref, gain_ref, bias_ref, middle_ref, normed_ref):
+def branch_kernel(keep_ref, more_ref, weight_ref, other_ref, residual_ref, scale_ref, middle_ref, normed_ref):
     branch = dot(keep_ref[...], weight_ref[...], NT) + dot(more_ref[...], other_ref[...], NT)
     middle = residual_ref[...].astype(wide) + branch
     middle_ref[...] = middle
     hat, _ = normalize(middle)
-    normed_ref[...] = (hat * gain_ref[...] + bias_ref[...]).astype(low)
+    normed_ref[...] = (hat * scale_ref[2:3] + scale_ref[3:4]).astype(low)
 
 
 def pack_kernel(own_ref, sibling_ref, own_slot_ref, sibling_slot_ref, *out_refs):
@@ -253,6 +312,12 @@
         packed = dot(chooser, ref[...]).astype(low)
         for k, out_ref in enumerate(out_refs):
             out_ref[source] = packed[k * capacity : (k + 1) * capacity]
+
+
+def straight_pack_kernel(values_ref, slot_ref, out_ref):
+    place = lax.broadcasted_iota(jnp.int32, (out_ref.shape[0], values_ref.shape[0]), 0)
+    chooser = (place == slot_ref[...]).astype(wide).astype(low)
+    out_ref[...] = dot(chooser, values_ref[...]).astype(low)
 
 
 def expert_kernel(first, count, chunk, place_ref, in_ref, out_ref, grads_ref, more_grads_ref, *refs):
@@ -291,7 +356,9 @@
     give_ref[0] = total[rows:].astype(low)
 
 
-def expert_group(place, weight_in, weight_out, grads, more_grads, pieces, more_pieces, buffers, span, chips):
+def expert_group(
+    place, weight_in, weight_out, grads, more_grads, pieces, more_pieces, buffers, span, chips, earlier
+):
     first, stop = span
     count = stop - first
     capacity, width = pieces[0].shape[1:]
@@ -314,10 +381,10 @@
         functools.partial(expert_kernel, first, count, min(512, hidden)),
         operands,
         [
-            array((chips, rows, width), low),
-            array((chips, rows, width), low),
-            array((chips, rows, hidden), low),
-            array((chips, rows, hidden), low),
+            kept((chips, rows, width), low),
+            kept((chips, rows, width), low),
+            kept((chips, rows, hidden), low),
+            kept((chips, rows, hidden), low),
             array((count, rows // 2, width), wide),
             array((count, rows // 2, width), low),
         ],
@@ -333,6 +400,7 @@
             block(rows // 2, width, 0),
         ],
         input_output_aliases=aliases,
+        first=earlier,
     )
     return res[:4], res[4], res[5]
 
@@ -352,10 +420,10 @@
     for source, (slot_ref, out_ref) in enumerate(
         ((own_slot_ref, own_ref), (sibling_slot_ref, sibling_ref))
     ):
-        place = lax.broadcasted_iota(jnp.int32, (slot_ref.shape[0], slots), 1)
+        place = lax.broadcasted_iota(jnp.int32, (slots, out_ref.shape[0]), 0)
         chooser = (place == slot_ref[...]).astype(wide).astype(low)
         values = jnp.concatenate([piece[source] for piece in pieces], axis=0)
-        out_ref[...] = dot(chooser, values).astype(low)
+        out_ref[...] = dot(chooser, values, TN).astype(low)
 
 
 def ffn_kernel(active_ref, weight_ref, keep_ref, give_ref):
@@ -363,6 +431,13 @@
     rows = keep_ref.shape[1]
     keep_ref[0] = values[:rows]
     give_ref[0] = values[rows:].astype(low)
+
+
+def product_kernel(left_ref, right_ref, out_ref):
+    left, right = left_ref[...], right_ref[...]
+    out_ref[...] = dot(
+        left.reshape(-1, left.shape[-1]), right.reshape(-1, right.shape[-1]), TN
+    )
 
 
 def ffn_sum_kernel(place_ref, keep_ref, more_ref, out_ref):
@@ -375,20 +450,20 @@
 
 
 def out_kernel(slot_ref, values_ref, middle_ref, out_ref):
-    place = lax.broadcasted_iota(jnp.int32, (slot_ref.shape[0], values_ref.shape[0]), 1)
+    place = lax.broadcasted_iota(jnp.int32, (values_ref.shape[0], out_ref.shape[0]), 0)
     chooser = (place == slot_ref[...]).astype(wide).astype(low)
-    out_ref[...] = (middle_ref[...] + dot(chooser, values_ref[...])).astype(low)
+    out_ref[...] = (middle_ref[...] + dot(chooser, values_ref[...], TN)).astype(low)
 
 
 def middle_back_kernel(
-    own_ref, more_ref, middle_ref, ct_ref, gain_ref, weight_ref, other_ref,
+    own_ref, more_ref, middle_ref, ct_ref, scale_ref, weight_ref, other_ref,
     grad_ref, branch_ref, mine_ref, give_ref, sums_ref,
 ):
     grad_second = own_ref[...].astype(wide) + more_ref[...].astype(wide)
     hat, inverse = normalize(middle_ref[...])
     sums_ref[0:1] = jnp.sum(grad_second * hat, axis=0, keepdims=True)
     sums_ref[1:2] = jnp.sum(grad_second, axis=0, keepdims=True)
-    grad_middle = ct_ref[...].astype(wide) + norm_back(grad_second, hat, inverse, gain_ref[...])
+    grad_middle = ct_ref[...].astype(wide) + norm_back(grad_second, hat, inverse, scale_ref[2:3])
     grad_ref[...] = grad_middle
     branch = grad_middle.astype(low)
     branch_ref[...] = branch
@@ -401,28 +476,31 @@
     own_ref[...] = dot(branch_ref[...], keep_ref[...], TN)
 
 
-def first_give_kernel(place_ref, grads_ref, full_ref, give_ref):
-    half = give_ref.shape[0]
-    first = pl.multiple_of((1 - place_ref[1]) * half, half)
-    total = None
+def first_kernel(
+    place_ref, grads_ref, full_ref, own_in_ref, other_in_ref, second_ref, give_ref, own_ref, sums_ref
+):
+    half = own_ref.shape[0]
+    side = place_ref[1]
+    sums = None
+    for ref, out_ref, first in ((other_in_ref, give_ref, 1 - side), (own_in_ref, own_ref, side)):
+        rows = pl.ds(pl.multiple_of(first * half, half), half)
+        total = None
+        for n in range(3):
+            term = dot(grads_ref[n, rows], full_ref[n], NT)
+            total = term if total is None else total + term
+        out_ref[...] = total.astype(out_ref.dtype)
+        hat, _ = normalize(ref[...].astype(wide))
+        more = [jnp.sum(total * hat, axis=0, keepdims=True), jnp.sum(total, axis=0, keepdims=True)]
+        sums = more if sums is None else [x + y for x, y in zip(sums, more)]
+    sums_ref[0:1] = sums[0]
+    sums_ref[1:2] = sums[1]
+    sums_ref[2:4] = second_ref[...]
+
+
+def weight_part_kernel(chips, place_ref, turned_ref, grads_ref, part_ref, more_ref, keep_ref, give_ref, parts):
+    place = place_ref[0]
     for n in range(3):
-        term = dot(grads_ref[n, pl.ds(first, half)], full_ref[n], NT)
-        total = term if total is None else total + term
-    give_ref[...] = total.astype(low)
-
-
-def weight_part_kernel(
-    chips, place_ref, own_ref, other_ref, gain_ref, bias_ref, grads_ref, part_ref, more_ref, keep_ref, give_ref, normed, parts
-):
-    place, side = place_ref[0], place_ref[1]
-    count = own_ref.shape[0]
-    for ref, first in ((own_ref, side * count), (other_ref, (1 - side) * count)):
-        hat, _ = normalize(ref[...].astype(wide))
-        normed[pl.ds(pl.multiple_of(first, count), count)] = (
-            hat * gain_ref[...] + bias_ref[...]
-        ).astype(low)
-    for n in range(3):
-        parts[n] = dot(normed[...], grads_ref[n], TN).astype(low)
+        parts[n] = dot(turned_ref[...], grads_ref[n]).astype(low)
     parts[3] = (part_ref[...] + more_ref[...].astype(wide)).astype(low)
     if chips:
         rows = keep_ref.shape[3]
@@ -436,44 +514,70 @@
         give_ref[...] = jnp.zeros(give_ref.shape, low)
 
 
-def first_own_kernel(place_ref, grads_ref, full_ref, give_ref, own_in_ref, other_in_ref, own_ref, sums_ref):
-    half = own_ref.shape[0]
-    first = pl.multiple_of(place_ref[1] * half, half)
-    total = None
+def spread(sums):
+    half = sums.shape[1] // 2
+    rows = []
+    rest = sums
+    for _ in range(3):
+        term = rest.astype(low).astype(wide)
+        rest = rest - term
+        rows += [term[:, :half], term[:, half:]]
+    rows.append(jnp.zeros((8, half), wide))
+    return jnp.concatenate(rows, axis=0).astype(low)
+
+
+def gathered(rows):
+    rows = rows.astype(wide)
+    terms = [
+        jnp.concatenate([rows[8 * n : 8 * n + 4], rows[8 * n + 4 : 8 * n + 8]], axis=1)
+        for n in range(3)
+    ]
+    return (terms[0] + terms[1]) + terms[2]
+
+
+def halves_kernel(keep_ref, more_ref, sums_ref, more_sums_ref, near_ref, far_ref, out_sums_ref):
+    count = near_ref.shape[0]
+    sums = sums_ref[...] + more_sums_ref[...]
+    out_sums_ref[...] = sums
+    far_ref[count:] = spread(sums)
+    for side, ref in ((0, near_ref), (1, far_ref)):
+        total = keep_ref[side].astype(wide) + more_ref[side].astype(wide)
+        ref[:count] = total.reshape(count, total.shape[-1]).astype(low)
+
+
+def quarters_kernel(near_ref, more_ref, sums_ref, own_ref, out_sums_ref, *out_refs):
+    rows = own_ref.shape[0]
+    sums = sums_ref[...] + gathered(more_ref[near_ref.shape[0] :])
+    out_sums_ref[...] = sums
+    packed = spread(sums)
+    for n, ref in enumerate((own_ref, *out_refs)):
+        block = slice(n * rows, (n + 1) * rows)
+        total = near_ref[block].astype(wide) + more_ref[block].astype(wide)
+        ref[:rows] = total.astype(ref.dtype)
+        if n:
+            ref[rows:] = packed
+
+
+def total_kernel(own_ref, sums_ref, *refs):
+    aways, (in_ref, out_ref, out_sums_ref) = refs[:-3], refs[-3:]
+    rows = out_ref.shape[0]
+    sums = [sums_ref[...]]
+    total = own_ref[...]
+    for ref in aways:
+        total = total + ref[: own_ref.shape[0]].astype(wide)
+        sums.append(gathered(ref[own_ref.shape[0] :]))
+    while len(sums) > 1:
+        sums = [x + y for x, y in zip(sums[0::2], sums[1::2])]
+    out_sums_ref[...] = sums[0]
     for n in range(3):
-        term = dot(grads_ref[n, pl.ds(first, half)], full_ref[n], NT)
-        total = term if total is None else total + term
-    own_ref[...] = total
-    hat, _ = normalize(own_in_ref[...].astype(wide))
-    more_hat, _ = normalize(other_in_ref[...].astype(wide))
-    more = give_ref[...].astype(wide)
-    sums_ref[0:1] = jnp.sum(total * hat + more * more_hat, axis=0, keepdims=True)
-    sums_ref[1:2] = jnp.sum(total + more, axis=0, keepdims=True)
-
-
-def halves_kernel(keep_ref, more_ref, near_ref, far_ref):
-    near_ref[...] = (keep_ref[0].astype(wide) + more_ref[0].astype(wide)).astype(low)
-    far_ref[...] = (keep_ref[1].astype(wide) + more_ref[1].astype(wide)).astype(low)
-
-
-def quarters_kernel(keep_ref, more_ref, own_ref, *out_refs):
-    own_ref[...] = keep_ref[0].astype(wide) + more_ref[0].astype(wide)
-    for n, out_ref in enumerate(out_refs):
-        out_ref[...] = (keep_ref[n + 1].astype(wide) + more_ref[n + 1].astype(wide)).astype(low)
-
-
-def total_kernel(own_ref, *refs):
-    total = own_ref[...]
-    for ref in refs[:-2]:
-        total = total + ref[...].astype(wide)
-    refs[-2][...] = total[:3]
-    refs[-1][...] = total[3]
-
-
-def input_grad_kernel(grad_ref, own_ref, more_ref, input_ref, gain_ref, out_ref):
+        in_ref[n] = total[n * rows : (n + 1) * rows]
+    out_ref[...] = total[3 * rows :]
+
+
+def input_grad_kernel(grad_ref, own_ref, more_ref, input_ref, scale_ref, out_ref):
     hat, inverse = normalize(input_ref[...].astype(wide))
     upstream = own_ref[...] + more_ref[...].astype(wide)
-    out_ref[...] = grad_ref[...] + norm_back(upstream, hat, inverse, gain_ref[...])
+    out_ref[...] = grad_ref[...] + norm_back(upstream, hat, inverse, scale_ref[0:1])
 
 
 def across(values):
@@ -485,10 +589,6 @@
         return values
     count = lax.axis_size("fsdp")
     return lax.ppermute(values, "fsdp", [(i, i ^ offset) for i in range(count)])
-
-
-def after(values, *earlier):
-    return lax.optimization_barrier((values, earlier))[0]
 
 
 def reduce_blocks(blocks, index, count):
@@ -557,8 +657,7 @@
     side = lax.axis_index("tp")
     place = jnp.stack([index, side]).astype(jnp.int32)
     in_kernel = shard_rows % 16 == 0
-    first_gain, first_bias = first_gain[None], first_bias[None]
-    second_gain, second_bias = second_gain[None], second_bias[None]
+    scales = [first_gain, first_bias, second_gain, second_bias]
 
     other_inputs = across(inputs)
     shard = jnp.concatenate([input_weight, output_weight.T[None]])
@@ -588,8 +687,13 @@
     own_place, sibling_place = chip_slot(own_slot), chip_slot(sibling_slot)
 
     slot_count = experts_in_all * capacity
-    straight = (own_slot[None, :] == jnp.arange(slot_count)[:, None]).astype(low)
-    packed_grads = after(dot(straight, cotangent).astype(low), mine)
+    packed_grads = run(
+        straight_pack_kernel,
+        (cotangent, own_slot[None]),
+        kept((slot_count, width), low),
+        flops=2 * slot_count * own_count * width,
+        first=(mine, other_inputs),
+    )
     slot_grads = lax.all_to_all(
         packed_grads.reshape(experts_in_all, capacity, width), "fsdp", 0, 0, tiled=True
     )
@@ -604,21 +708,25 @@
             [lax.dynamic_index_in_dim(both, index ^ n, 0, False) for n in range(experts_in_all)], axis=1
         )
         weights = (full, full[:1, :16])
-    full_weight, projected = run(
+    full_weight, out_weight, projected, scales = run(
         functools.partial(project_kernel, chips if in_kernel else 0),
-        (place, inputs, other_inputs, first_gain, first_bias, *weights),
-        [array((4, width, local_width), low), array((tree_size, 3 * local_width), low)],
+        (place, inputs, other_inputs, *scales, *weights),
+        [
+            kept((3, width, local_width), low),
+            array((width, local_width), low),
+            kept((tree_size, 3 * local_width), low),
+            array((4, width), wide),
+        ],
         flops=2 * tree_size * width * 3 * local_width,
     )
-    out_weight = full_weight[3]
     other_out_weight = across(out_weight)
     unreached, member = tree_masks(segment_lengths[0], segment_parents[0], tree_size)
     attended, totals, attended_keep, attended_give = attend(place, projected, unreached, member)
     attended_more = across(attended_give)
     middle, second_normed = run(
         branch_kernel,
-        (attended_keep, attended_more, out_weight, other_out_weight, inputs, second_gain, second_bias),
-        [array((own_count, width), wide), array((own_count, width), low)],
+        (attended_keep, attended_more, out_weight, other_out_weight, inputs, scales),
+        [kept((own_count, width), wide), array((own_count, width), low)],
         flops=2 * own_count * width * width,
     )
 
@@ -628,44 +736,47 @@
         pack_kernel,
         (second_normed, sibling_normed, own_place[None], sibling_place[None]),
         [piece] * chips,
+        first=(slot_grads,),
         flops=4 * own_count * own_count * width,
     )
-    packed = after(packed, slot_grads)
-    spans = [(0, chips // 2), (chips // 2, 3 * chips // 4), (3 * chips // 4, chips)]
+    quarter = chips // 4
+    near, next_near, far, next_far = [(n * quarter, (n + 1) * quarter) for n in range(4)]
     arrived = {}
-    for k in range(*spans[1]):
+    for span in (far, near, next_near):
+        for k in range(*span):
+            arrived[k] = swapped(packed[k], 2 * k)
+    for k in range(*next_far):
         arrived[k] = swapped(packed[k], 2 * k)
-    for k in range(*spans[0]):
-        arrived[k] = swapped(packed[k], 2 * k)
-    for k in range(*spans[2]):
-        arrived[k] = swapped(after(packed[k], *[arrived[n] for n in range(*spans[0])]), 2 * k)
-    more_arrived = {k: across(arrived[k]) for k in range(chips)}
+    spans = (near, far, next_far, next_near)
+    more_arrived = {k: across(arrived[k]) for span in spans for k in range(*span)}
 
     weight_in, weight_out = expert_in[0], expert_out[0]
     buffers = None
-    returned = []
-    for span in spans:
+    returned = {}
+    done = []
+    back = []
+    for turn, span in enumerate(spans):
+        own_pieces = [arrived[k] for k in range(*span)]
         buffers, keep, give = expert_group(
             place, weight_in, weight_out, slot_grads, more_slot_grads,
-            [arrived[k] for k in range(*span)], [more_arrived[k] for k in range(*span)],
-            buffers, span, chips,
+            own_pieces, [more_arrived[k] for k in range(*span)], buffers, span, chips,
+            [more_arrived[k] for later in spans[turn + 1 : turn + 2] for k in range(*later)]
+            + ([arrived[k] for k in range(1, chips)] if turn == 0 else []),
         )
-        sums = run(pieces_kernel, (keep, across(give)), [piece] * (span[1] - span[0]))
-        returned += [swapped(sums[k - span[0]], 2 * k) for k in range(*span)]
-    own_part, sibling_part = run(
-        unpack_kernel,
-        (own_place[:, None], sibling_place[:, None], *returned),
-        [array((own_count, width), low)] * 2,
-        flops=4 * own_count * own_count * width,
-    )
-    sibling_part = swapped(sibling_part, 1)
-    slot_rows, grad_rows, actives, grad_pres = after(buffers, *sums)
+        *sums, token = run(pieces_kernel, (keep, across(give)), [piece] * quarter, mark=True)
+        done.append(token)
+        for k in range(*span):
+            returned[k] = swapped(sums[k - span[0]], 2 * k)
+        back.append([returned[k] for k in range(*span)])
+    slot_rows, grad_rows, actives, grad_pres = buffers
     rows = 4 * capacity
-    ffn_keep, ffn_give = run(
+    ffn_keep, ffn_give, ffn_done = run(
         ffn_kernel,
-        (actives, weight_out),
+        (in_hbm(actives), weight_out),
         [array((chips, rows // 2, width), wide), array((chips, rows // 2, width), low)],
         flops=2 * chips * rows * width * hidden,
+        first=done[2:3],
+        mark=True,
         grid=(chips,),
         in_specs=[
             pl.BlockSpec((1, rows, hidden), lambda i: (i, 0, 0)),
@@ -673,102 +784,165 @@
         ],
         out_specs=[pl.BlockSpec((1, rows // 2, width), lambda i: (i, 0, 0))] * 2,
     )
-    ffn_sums = run(
-        ffn_sum_kernel, (place, ffn_keep, across(ffn_give)), array((experts_in_all, capacity, width), low)
+    ffn_more = across(ffn_give)
+    tile = min(512, hidden)
+    stripe = pl.BlockSpec((chips, rows, tile), lambda i: (0, 0, i))
+    fixed = pl.BlockSpec((chips, rows, width), lambda i: (0, 0, 0))
+    expert_out_grad, out_done = run(
+        product_kernel,
+        (in_hbm(actives), in_hbm(grad_rows)),
+        array((hidden, width), wide),
+        flops=2 * chips * rows * width * hidden,
+        first=(ffn_done, done[3], *back[0], *back[1]),
+        mark=True,
+        grid=(hidden // tile,),
+        in_specs=[stripe, fixed],
+        out_specs=[pl.BlockSpec((tile, width), lambda i: (i, 0))],
+    )
+    expert_in_grad, in_done = run(
+        product_kernel,
+        (in_hbm(slot_rows), in_hbm(grad_pres)),
+        array((width, hidden), wide),
+        flops=2 * chips * rows * width * hidden,
+        first=(out_done, *back[2]),
+        mark=True,
+        grid=(hidden // tile,),
+        in_specs=[fixed, stripe],
+        out_specs=[pl.BlockSpec((width, tile), lambda i: (0, i))],
+    )
+    own_part, sibling_part = run(
+        unpack_kernel,
+        (own_place[None], sibling_place[None], *[returned[k] for k in range(chips)]),
+        [array((own_count, width), low)] * 2,
+        first=(in_done,),
+        flops=4 * own_count * own_count * width,
+    )
+    sibling_part = swapped(sibling_part, 1)
+    ffn_sums, sums_done = run(
+        ffn_sum_kernel,
+        (place, ffn_keep, ffn_more),
+        kept((experts_in_all, capacity, width), low),
+        mark=True,
     )
     ffn_back = lax.all_to_all(ffn_sums, "fsdp", 0, 0, tiled=True)
-    grad_rows, slot_rows = grad_rows.reshape(-1, width), slot_rows.reshape(-1, width)
-    expert_out_grad = dot(actives.reshape(-1, hidden), grad_rows, TN)
-    expert_in_grad = dot(slot_rows, grad_pres.reshape(-1, hidden), TN)
 
     grad_middle, grad_branch, grad_mine, grad_give, second_sums = run(
         middle_back_kernel,
-        (own_part, sibling_part, middle, cotangent, second_gain, out_weight, other_out_weight),
+        (
+            own_part, sibling_part, Far(middle), Far(cotangent), scales,
+            Far(out_weight), Far(other_out_weight),
+        ),
         [
-            array((own_count, width), wide),
+            kept((own_count, width), wide),
             array((own_count, width), low),
             array((own_count, local_width), low),
             array((own_count, local_width), low),
             array((2, width), wide),
         ],
+        first=(sums_done,),
         flops=2 * own_count * width * width,
     )
     grad_more = across(grad_give)
-    output_own, output_give = run(
+    output_own, output_give, output_done = run(
         output_part_kernel,
-        (grad_branch, attended_keep, attended_more),
-        [array((width, local_width), wide), array((width, local_width), low)],
+        (grad_branch, Far(attended_keep), Far(attended_more)),
+        [kept((width, local_width), wide), array((width, local_width), low)],
+        mark=True,
         flops=2 * own_count * width * width,
     )
     output_more = across(output_give)
-    grad_projected = attend_back(
-        place, projected, unreached, member, attended, totals, grad_mine, grad_more
-    )
-
-    first_give = run(
-        first_give_kernel,
-        (place, grad_projected, full_weight),
-        array((own_count, width), low),
-        flops=2 * own_count * width * 3 * local_width,
-    )
+    turned, turned_done = run(
+        turned_kernel,
+        (place, Far(inputs), Far(other_inputs), scales),
+        kept((width, tree_size), low),
+        mark=True,
+    )
+    (grad_projected,) = attend_back(
+        place, projected, unreached, member, attended, totals, grad_mine, grad_more,
+        first=(turned_done, output_done),
+    )
+
+    first_give, first_own, norm_sums, give_done = run(
+        first_kernel,
+        (
+            place, Far(grad_projected), Far(full_weight), Far(inputs), Far(other_inputs), second_sums,
+        ),
+        [array((own_count, width), low), array((own_count, width), wide), array((4, width), wide)],
+        mark=True,
+        first=(ffn_back,),
+        flops=2 * tree_size * width * 3 * local_width,
+    )
+    norm_more = across(norm_sums)
+    norm_sums = norm_sums + norm_more
     first_more = across(first_give)
     if in_kernel:
         block = array((2, chips // 2, 4, shard_rows, local_width), low)
         part_outs = [block, block]
     else:
         part_outs = [array((4, width, local_width), low), array((8, LANES), low)]
-    part_keep, part_give = run(
+    part_keep, part_give, part_done = run(
         functools.partial(weight_part_kernel, chips if in_kernel else 0),
-        (place, inputs, other_inputs, first_gain, first_bias, grad_projected, output_own, output_more),
+        (place, Far(turned), Far(grad_projected), Far(output_own), output_more),
         part_outs,
+        mark=True,
+        first=(give_done, norm_more),
         flops=2 * tree_size * width * 3 * local_width,
-        scratch_shapes=[
-            pltpu.VMEM((tree_size, width), low),
-            pltpu.VMEM((4, width, local_width), low),
-        ],
+        scratch_shapes=[pltpu.VMEM((4, width, local_width), low)],
     )
     if in_kernel:
         part_more = swapped(part_give, 1)
-        quarter = array((chips // 2, 4, shard_rows, local_width), low)
-        near, far = run(halves_kernel, (part_keep, part_more), [quarter, quarter])
-        shape = (4, shard_rows, local_width)
-        own_sum, *away = run(
+        rows = 4 * shard_rows
+        near_sum, far_sum, norm_sums = run(
+            halves_kernel,
+            (part_keep, part_more, norm_sums, swapped(norm_sums, 1)),
+            [
+                array((chips // 2 * rows, local_width), low),
+                array((chips // 2 * rows + 32, local_width), low),
+                array((4, width), wide),
+            ],
+        )
+        own_sum, norm_sums, *away = run(
             quarters_kernel,
-            (near, swapped(far, 2)),
-            [array(shape, wide)] + [array(shape, low)] * (chips // 2 - 1),
+            (near_sum, swapped(far_sum, 2), norm_sums),
+            [array((rows, local_width), wide), array((4, width), wide)]
+            + [array((rows + 32, local_width), low)] * (chips // 2 - 1),
+            first=(first_more,),
         )
         away = [swapped(away[k - 1], 4 * k) for k in range(1, chips // 2)]
-        input_weight_grad, output_weight_grad = run(
-            total_kernel, (own_sum, *away), [array((3, *shape[1:]), wide), array(shape[1:], wide)]
-        )
     else:
         blocks = part_keep.reshape(4, experts_in_all, shard_rows, local_width).transpose(1, 0, 2, 3)
         summed = reduce_blocks(blocks, index, experts_in_all)
+        bit = 1
+        while bit < experts_in_all:
+            norm_sums = norm_sums + swapped(norm_sums, bit)
+            bit *= 2
+    input_grad, input_done = run(
+        input_grad_kernel,
+        (Far(grad_middle), first_own, first_more, Far(inputs), scales),
+        array((own_count, width), wide),
+        mark=True,
+    )
+    out_block, out_done = run(
+        out_kernel,
+        (own_slot[None], ffn_back.reshape(slot_count, width), Far(middle)),
+        array((own_count, width), low),
+        mark=True,
+        flops=2 * own_count * slot_count * width,
+    )
+    if in_kernel:
+        input_weight_grad, output_weight_grad, norm_sums = run(
+            total_kernel,
+            (own_sum, norm_sums, *away),
+            [
+                array((3, shard_rows, local_width), wide),
+                array((shard_rows, local_width), wide),
+                array((4, width), wide),
+            ],
+            first=(input_done, out_done),
+        )
+    else:
         input_weight_grad, output_weight_grad = summed[:3], summed[3]
     output_weight_grad = output_weight_grad.T
-    first_own, first_sums = run(
-        first_own_kernel,
-        (place, grad_projected, full_weight, first_give, inputs, other_inputs),
-        [array((own_count, width), wide), array((2, width), wide)],
-        flops=2 * own_count * width * 3 * local_width,
-    )
-    norm_sums = jnp.concatenate([first_sums, second_sums])
-    bit = 1
-    while bit < experts_in_all:
-        norm_sums = norm_sums + swapped(norm_sums, bit)
-        bit *= 2
-    norm_sums = norm_sums + across(norm_sums)
-    input_grad = run(
-        input_grad_kernel,
-        (grad_middle, first_own, first_more, inputs, first_gain),
-        array((own_count, width), wide),
-    )
-    out_block = run(
-        out_kernel,
-        (own_slot[:, None], ffn_back.reshape(slot_count, width), middle),
-        array((own_count, width), low),
-        flops=2 * own_count * slot_count * width,
-    )
     return (
         out_block,
         input_grad,

time: 369 us -> 315 us (0.85)
  local copies, waits for them, and re-layouts: 42.3 us -> 7.39 us
  Pallas kernels: 95.5 us -> 129 us
  waiting for transfers between devices: 108 us -> 79.4 us
  matrix products: 19.4 us -> 2.51 us
  starting transfers between devices: 95.1 us -> 86.3 us
    pallas_call x24 -> x29, Pallas kernels: 95.5 us -> 129 us  [run(): pl.pallas_call(whole, out_shape=outs, compiler_params=pltpu.CompilerParam...]
    unnamed x148 -> x50, local copies, waits for them, and re-layouts: 39.2 us -> 6.03 us
    ppermute x34 -> x31, waiting for transfers between devices: 53 us -> 34.3 us  [swapped(): return lax.ppermute(values, 'fsdp', [(i, i ^ offset) for i in range(count)])]
    dot_general x5 -> x2, matrix products: 18.7 us -> 1.72 us  [dot(): return lax.dot_general(left, right, dims, preferred_element_type=wide)]
    ppermute x20 -> x21, waiting for transfers between devices: 45.4 us -> 32.3 us  [across(): return lax.ppermute(values, 'tp', [(0, 1), (1, 0)])]
    ppermute x34 -> x31, starting transfers between devices: 63.3 us -> 54.4 us  [swapped(): return lax.ppermute(values, 'fsdp', [(i, i ^ offset) for i in range(count)])]
    ppermute x20 -> x21, starting transfers between devices: 20.5 us -> 18.5 us  [across(): return lax.ppermute(values, 'tp', [(0, 1), (1, 0)])]
  transfers between devices with their start and end apart: 56 -> 54, of which waited for: 23 -> 19; matrix products, arithmetic and copies ran while one was open for 8% -> 3% of each run, Pallas kernels for 24% -> 39%
where the time goes in v1:
time: 315 us; the launch traced here: 310 us
  Pallas kernels  129 us (41%)
  starting transfers between devices  86.3 us (27%)
  waiting for transfers between devices  79.4 us (25%)
  local copies, waits for them, and re-layouts  7.39 us (2%)
  other arithmetic  4.42 us (1%)
    pallas_call x29, Pallas kernels, run(): pl.pallas_call(whole, out_shape=outs, compiler_params=pltpu.CompilerParam...  129 us
    ppermute x31, starting transfers between devices, swapped(): return lax.ppermute(values, 'fsdp', [(i, i ^ offset) for i in range(count)])  54.4 us
    ppermute x31, waiting for transfers between devices, swapped(): return lax.ppermute(values, 'fsdp', [(i, i ^ offset) for i in range(count)])  34.3 us
    ppermute x21, waiting for transfers between devices, across(): return lax.ppermute(values, 'tp', [(0, 1), (1, 0)])  32.3 us
    ppermute x21, starting transfers between devices, across(): return lax.ppermute(values, 'tp', [(0, 1), (1, 0)])  18.5 us
    all_to_all x1, waiting for transfers between devices, shards(): lax.all_to_all(packed_grads.reshape(experts_in_all, capacity, width), 'fs...  12.7 us
    all_to_all x1, starting transfers between devices, shards(): ffn_back = lax.all_to_all(ffn_sums, 'fsdp', 0, 0, tiled=True)  7.97 us
  transfers between devices with their start and end apart: 54, of which 19 were waited for; matrix products, arithmetic and copies ran while one was open for 3% of the time, Pallas kernels for 39%

profile of v1, /device:TPU:0, one launch (start us, length us, event | category | flops | bytes accessed | tf_op | source)
XLA Modules:
  0.0 310.1 jit_solution(14284260791938646078)
XLA Ops:
  29.6 5.5 %all-to-all-start = ((bf16[16,64,768]{2,1,0:T(8,128)(2,1)}), bf16[16,64,768]{2,1,0:T(8,128)(2,1)S(1)}, u32[]{:S(2)}, u32[]{:S(2)}) async-start(bf16[16,64,768]{2,1,0:T(8,128)(2,1)} %bitcast.60), calls=%async_computation | async-start | bytes 3145728 | tf_op jit(solution)/shard_map/all_to_all | solution.py:697
  36.5 6.4 %shard_map.214 = (bf16[3,768,384]{2,1,0:T(8,128)(2,1)}, bf16[768,384]{1,0:T(8,128)(2,1)}, bf16[1024,1152]{1,0:T(8,128)(2,1)}, f32[4,768]{1,0:T(4,128)S(1)}) custom-call(s32[2]{0:T(128)S(1)} %pad_add_fusion.refs_0_, bf16[512,768]{1,0:T(8,128)(2,1)S(1)} %copy-done.2, bf16[512,768]{1,0:T(8,128)(2,1)S(1)} %collective-permute-done.7.refs_3_.refs_2_.refs_4_, ...), custom_call_target="tpu_custom_call" | custom-call | flops 1811939328 | bytes 8675336 | tf_op jit(solution)/shard_map/pallas_call | solution.py:93
  44.3 9.5 %shard_map.215 = (bf16[1024,384]{1,0:T(8,128)(2,1)}, f32[1024,384]{1,0:T(8,128)}, bf16[512,384]{1,0:T(8,128)(2,1)S(1)}, bf16[512,384]{1,0:T(8,128)(2,1)}) custom-call(s32[2]{0:T(128)S(1)} %pad_add_fusion.refs_0_, bf16[1024,1152]{1,0:T(8,128)(2,1)} %get-tuple-element.104.refs_1_.refs_2_.refs_3_, ...), custom_call_target="tpu_custom_call" | custom-call | flops 12000000000 | bytes 10747912 | tf_op jit(solution)/shard_map/pallas_call | solution.py:93
  54.3 12.7 %all-to-all-done.refs_4_.refs_3_ = bf16[16,64,768]{2,1,0:T(8,128)(2,1)S(1)} async-done(((bf16[16,64,768]{2,1,0:T(8,128)(2,1)}), bf16[16,64,768]{2,1,0:T(8,128)(2,1)S(1)}, u32[]{:S(2)}, u32[]{:S(2)}) %all-to-all-start) | async-done | bytes 1572896 | tf_op jit(solution)/shard_map/all_to_all | solution.py:697
  75.7 7.2 %collective-permute-start.22 = (bf16[2,64,768]{2,1,0:T(8,128)(2,1)S(1)}, bf16[2,64,768]{2,1,0:T(8,128)(2,1)S(1)}, u32[]{:S(2)}, u32[]{:S(2)}) collective-permute-start(bf16[2,64,768]{2,1,0:T(8,128)(2,1)S(1)} %get-tuple-element.114), channel_id=1, source_target_pairs={{0,16},{2,18},{4,20},{6,22},{8,24},{10,26},{12,28},{14,30},{16,0},... | collective-permute-start | bytes 589832 | tf_op jit(solution)/shard_map/ppermute | solution.py:591
  85.5 11.1 %collective-permute-done.22.refs_14_.refs_5_ = bf16[2,64,768]{2,1,0:T(8,128)(2,1)S(1)} collective-permute-done((bf16[2,64,768]{2,1,0:T(8,128)(2,1)S(1)}, bf16[2,64,768]{2,1,0:T(8,128)(2,1)S(1)}, u32[]{:S(2)}, u32[]{:S(2)}) %collective-permute-start.22) | collective-permute-done | bytes 196640 | tf_op jit(solution)/shard_map/ppermute | solution.py:591
  110.1 4.5 %collective-permute-done.19.refs_17_.refs_6_ = bf16[2,64,768]{2,1,0:T(8,128)(2,1)S(1)} collective-permute-done((bf16[2,64,768]{2,1,0:T(8,128)(2,1)S(1)}, bf16[2,64,768]{2,1,0:T(8,128)(2,1)S(1)}, u32[]{:S(2)}, u32[]{:S(2)}) %collective-permute-start.19) | collective-permute-done | bytes 196640 | tf_op jit(solution)/shard_map/ppermute | solution.py:591
  126.5 6.3 %shard_map.218 = (bf16[8,256,768]{2,1,0:T(8,128)(2,1)}, bf16[8,256,768]{2,1,0:T(8,128)(2,1)}, bf16[8,256,1536]{2,1,0:T(8,128)(2,1)}, bf16[8,256,1536]{2,1,0:T(8,...) custom-call(s32[2]{0:T(128)S(1)} %copy-done.12, bf16[768,1536]{1,0:T(8,128)(2,1)S(1)} %bitcast.45, ...), custom_call_target="tpu_custom_call" | custom-call | flops 3623878656 | bytes 28704776 | tf_op jit(solution)/shard_map/pallas_call | solution.py:93
  134.4 6.6 %shard_map.219 = (bf16[8,256,768]{2,1,0:T(8,128)(2,1)}, bf16[8,256,768]{2,1,0:T(8,128)(2,1)}, bf16[8,256,1536]{2,1,0:T(8,128)(2,1)}, bf16[8,256,1536]{2,1,0:T(8,...) custom-call(s32[2]{0:T(128)S(1)} %copy-done.12, ...), custom_call_target="tpu_custom_call", output_to_operand_aliasing={{0}: (9, {}), {1}: (10, {}), {2}: (11, {}), {3}: (12, {})} | custom-call | flops 3623878656 | bytes 47579144 | tf_op jit(solution)/shard_map/pallas_call | solution.py:93
  143.0 6.5 %shard_map.220 = (bf16[8,256,768]{2,1,0:T(8,128)(2,1)}, bf16[8,256,768]{2,1,0:T(8,128)(2,1)}, bf16[8,256,1536]{2,1,0:T(8,128)(2,1)}, bf16[8,256,1536]{2,1,0:T(8,...) custom-call(s32[2]{0:T(128)S(1)} %copy-done.12, ...), custom_call_target="tpu_custom_call", output_to_operand_aliasing={{0}: (9, {}), {1}: (10, {}), {2}: (11, {}), {3}: (12, {})} | custom-call | flops 3623878656 | bytes 47579144 | tf_op jit(solution)/shard_map/pallas_call | solution.py:93
  150.0 6.4 %shard_map.221 = (bf16[8,256,768]{2,1,0:T(8,128)(2,1)}, bf16[8,256,768]{2,1,0:T(8,128)(2,1)}, bf16[8,256,1536]{2,1,0:T(8,128)(2,1)}, bf16[8,256,1536]{2,1,0:T(8,...) custom-call(s32[2]{0:T(128)S(1)} %copy-done.12, ...), custom_call_target="tpu_custom_call", output_to_operand_aliasing={{0}: (9, {}), {1}: (10, {}), {2}: (11, {}), {3}: (12, {})} | custom-call | flops 3623878656 | bytes 47579144 | tf_op jit(solution)/shard_map/pallas_call | solution.py:93
  160.6 5.3 %collective-permute-start.38 = (bf16[2,64,768]{2,1,0:T(8,128)(2,1)S(1)}, bf16[2,64,768]{2,1,0:T(8,128)(2,1)S(1)}, u32[]{:S(2)}, u32[]{:S(2)}) collective-permute-start(bf16[2,64,768]{2,1,0:T(8,128)(2,1)S(1)} %get-tuple-element.150), channel_id=1, source_target_pairs={{0,20},{2,22},{4,16},{6,18},{8,28},{10,30},{12,24},{14,26},{16,4},... | collective-permute-start | bytes 589832 | tf_op jit(solution)/shard_map/ppermute | solution.py:591
  170.0 8.7 %shard_map.223 = (f32[8,128,768]{2,1,0:T(8,128)S(1)}, bf16[8,128,768]{2,1,0:T(8,128)(2,1)S(1)}, f32[8,128]{1,0:T(8,128)S(1)}) custom-call(bf16[8,256,1536]{2,1,0:T(8,128)(2,1)} %get-tuple-element.130.refs_0_, bf16[1536,768]{1,0:T(8,128)(2,1)S(1)} %bitcast.53, f32[8,128]{1,0:T(8,128)S(1)} %get-tuple-element.133.refs_2_), custom_call_target="tpu_custom_call" | custom-call | flops 4831838208 | bytes 13369344 | tf_op jit(solution)/shard_map/pallas_call | solution.py:93
  179.2 6.3 %collective-permute-start.39 = (bf16[2,64,768]{2,1,0:T(8,128)(2,1)S(1)}, bf16[2,64,768]{2,1,0:T(8,128)(2,1)S(1)}, u32[]{:S(2)}, u32[]{:S(2)}) collective-permute-start(bf16[2,64,768]{2,1,0:T(8,128)(2,1)S(1)} %get-tuple-element.151), channel_id=1, source_target_pairs={{0,24},{2,26},{4,28},{6,30},{8,16},{10,18},{12,20},{14,22},{16,8},... | collective-permute-start | bytes 589832 | tf_op jit(solution)/shard_map/ppermute | solution.py:591
  188.6 9.5 %shard_map.229 = (f32[1536,768]{1,0:T(8,128)}, f32[8,128]{1,0:T(8,128)S(1)}) custom-call(bf16[8,256,1536]{2,1,0:T(8,128)(2,1)} %get-tuple-element.130.refs_0_, bf16[8,256,768]{2,1,0:T(8,128)(2,1)} %get-tuple-element.155.refs_1_, f32[8,128]{1,0:T(8,128)S(1)} %get-tuple-element.156.refs_2_, f32[8,128]{1,0:T(8,128)S(1)} %get-tuple-element.157.refs_3_, ...), custom_call_target="tpu_custom_call" | custom-call | flops 4831838208 | bytes 14155776 | tf_op jit(solution)/shard_map/pallas_call | solution.py:93
  198.1 9.5 %shard_map.230 = (f32[768,1536]{1,0:T(8,128)}, f32[8,128]{1,0:T(8,128)S(1)}) custom-call(bf16[8,256,768]{2,1,0:T(8,128)(2,1)} %get-tuple-element.153.refs_0_, bf16[8,256,1536]{2,1,0:T(8,128)(2,1)} %get-tuple-element.154.refs_1_, f32[8,128]{1,0:T(8,128)S(1)} %get-tuple-element.158.refs_2_, bf16[2,64,768]{2,1,0:T(8,128)(2,1)S(1)} %collective-permute-done.39.refs_3_.refs_8_, ...), custom_call_target="tpu_custom_call" | custom-call | flops 4831838208 | bytes 14155776 | tf_op jit(solution)/shard_map/pallas_call | solution.py:93
  211.6 8.0 %all-to-all-start.1 = ((bf16[16,64,768]{2,1,0:T(8,128)(2,1)}), bf16[16,64,768]{2,1,0:T(8,128)(2,1)S(1)}, u32[]{:S(2)}, u32[]{:S(2)}) async-start(bf16[16,64,768]{2,1,0:T(8,128)(2,1)} %get-tuple-element.136), calls=%async_computation.1 | async-start | bytes 3145728 | tf_op jit(solution)/shard_map/all_to_all | solution.py:827
  219.6 4.6 %shard_map.232 = (f32[512,768]{1,0:T(8,128)}, bf16[512,768]{1,0:T(8,128)(2,1)S(1)}, bf16[512,384]{1,0:T(8,128)(2,1)S(1)}, bf16[512,384]{1,0:T(8,128)(2,1)S(1)}, f32[2,768]{1,0:T(2,128)S(1)}) custom-call(bf16[512,768]{1,0:T(8,128)(2,1)S(1)} %get-tuple-element.160.refs_0_, bf16[512,768]{1,0:T(8,128)(2,1)S(1)} %collective-permute-done.41.refs_1_, ...), custom_call_target="tpu_custom_call" | custom-call | flops 603979776 | bytes 8275968 | tf_op jit(solution)/shard_map/pallas_call | solution.py:93
  236.1 15.6 %shard_map.235.refs_1_.refs_2_ = bf16[3,1024,384]{2,1,0:T(8,128)(2,1)} custom-call(s32[2]{0:T(128)S(1)} %copy-done.13, bf16[1024,1152]{1,0:T(8,128)(2,1)} %get-tuple-element.104.refs_1_.refs_2_.refs_3_, bf16[1024,1152]{1,0:T(8,128)(2,1)} %get-tuple-element.104.refs_1_.refs_2_.refs_3_, bf16[1024,1152]{1,0:T(8,128)(2,1)} %get-tuple-element.104.refs_1_.refs_2_.refs_3_, ...), custom_call_target="tpu_custom_call" | custom-call | flops 24000000000 | bytes 13107208 | tf_op jit(solution)/shard_map/pallas_call | solution.py:93
  251.8 5.7 %shard_map.236 = (bf16[512,768]{1,0:T(8,128)(2,1)S(1)}, f32[512,768]{1,0:T(8,128)S(1)}, f32[4,768]{1,0:T(4,128)S(1)}, f32[8,128]{1,0:T(8,128)S(1)}) custom-call(s32[2]{0:T(128)S(1)} %copy-done.13, bf16[3,1024,384]{2,1,0:T(8,128)(2,1)} %shard_map.235.refs_1_.refs_2_, bf16[3,768,384]{2,1,0:T(8,128)(2,1)} %get-tuple-element.171.refs_2_, ...), custom_call_target="tpu_custom_call" | custom-call | flops 1811939328 | bytes 8079368 | tf_op jit(solution)/shard_map/pallas_call | solution.py:93
  262.3 5.9 %shard_map.238 = (bf16[2,4,4,48,384]{4,3,2,1,0:T(8,128)(2,1)S(1)}, bf16[2,4,4,48,384]{4,3,2,1,0:T(8,128)(2,1)S(1)}, f32[8,128]{1,0:T(8,128)}) custom-call(s32[2]{0:T(128)S(1)} %copy-done.13, bf16[768,1024]{1,0:T(8,128)(2,1)} %get-tuple-element.176.refs_1_, bf16[3,1024,384]{2,1,0:T(8,128)(2,1)} %shard_map.235.refs_1_.refs_2_, ...), custom_call_target="tpu_custom_call" | custom-call | flops 1811939328 | bytes 8060936 | tf_op jit(solution)/shard_map/pallas_call | solution.py:93
  273.9 14.3 %collective-permute-done.43.refs_2_.refs_3_ = bf16[512,768]{1,0:T(8,128)(2,1)S(1)} collective-permute-done((bf16[512,768]{1,0:T(8,128)(2,1)S(1)}, bf16[512,768]{1,0:T(8,128)(2,1)S(1)}, u32[]{:S(2)}, u32[]{:S(2)}) %collective-permute-start.43) | collective-permute-done | bytes 786464 | tf_op jit(solution)/shard_map/ppermute | solution.py:584
  288.4 4.7 %collective-permute-start.49 = (bf16[224,384]{1,0:T(8,128)(2,1)S(1)}, bf16[224,384]{1,0:T(8,128)(2,1)S(1)}, u32[]{:S(2)}, u32[]{:S(2)}) collective-permute-start(bf16[224,384]{1,0:T(8,128)(2,1)S(1)} %get-tuple-element.188), channel_id=1, source_target_pairs={{0,8},{2,10},{4,12},{6,14},{8,0},{10,2},{12,4},{14,6},{16,24},{18,... | collective-permute-start | bytes 516104 | tf_op jit(solution)/shard_map/ppermute | solution.py:591
  304.1 4.3 %collective-permute-done.51.refs_4_ = bf16[224,384]{1,0:T(8,128)(2,1)S(1)} collective-permute-done((bf16[224,384]{1,0:T(8,128)(2,1)S(1)}, bf16[224,384]{1,0:T(8,128)(2,1)S(1)}, u32[]{:S(2)}, u32[]{:S(2)}) %collective-permute-start.51) | collective-permute-done | bytes 172064 | tf_op jit(solution)/shard_map/ppermute | solution.py:591
  (184 shorter events, 123.6 us)
Async XLA Ops:
  1.6 20.5 %collective-permute-start = (bf16[4,48,384]{2,1,0:T(8,128)(2,1)S(1)}, bf16[4,48,384]{2,1,0:T(8,128)(2,1)S(1)}, u32[]{:S(2)}, u32[]{:S(2)}) collective-permute-start(bf16[4,48,384]{2,1,0:T(8,128)(2,1)S(1)} %pad_maximum_fusion), channel_id=1, source_target_pairs={{0,4},{2,6},{4,0},{6,2},{8,12},{10,14},{12,8},{14,10},{16,20},{18,... | collective-permute-start | bytes 442376 | tf_op jit(solution)/shard_map/ppermute | solution.py:591
  9.0 18.5 %collective-permute-start.7 = (bf16[512,768]{1,0:T(8,128)(2,1)}, bf16[512,768]{1,0:T(8,128)(2,1)S(1)}, u32[]{:S(2)}, u32[]{:S(2)}) collective-permute-start(bf16[512,768]{1,0:T(8,128)(2,1)} %refs_3_.7), channel_id=1, source_target_pairs={{0,1},{1,0},{2,3},{3,2},{4,5},{5,4},{6,7},{7,6},{8,9},{9,8},{10,11... | collective-permute-start | bytes 2359304 | tf_op jit(solution)/shard_map/ppermute | solution.py:584
  29.6 37.5 %all-to-all-start = ((bf16[16,64,768]{2,1,0:T(8,128)(2,1)}), bf16[16,64,768]{2,1,0:T(8,128)(2,1)S(1)}, u32[]{:S(2)}, u32[]{:S(2)}) async-start(bf16[16,64,768]{2,1,0:T(8,128)(2,1)} %bitcast.60), calls=%async_computation | async-start | bytes 3145728 | tf_op jit(solution)/shard_map/all_to_all | solution.py:697
  42.8 25.8 %collective-permute-start.11 = (bf16[768,384]{1,0:T(8,128)(2,1)}, bf16[768,384]{1,0:T(8,128)(2,1)S(1)}, u32[]{:S(2)}, u32[]{:S(2)}) collective-permute-start(bf16[768,384]{1,0:T(8,128)(2,1)} %get-tuple-element.107.refs_2_.refs_5_), channel_id=1, source_target_pairs={{0,1},{1,0},{2,3},{3,2},{4,5},{5,4},{6,7},{7,6},{8,9},{9,8},{10,11... | collective-permute-start | bytes 1769480 | tf_op jit(solution)/shard_map/ppermute | solution.py:584
  67.1 59.4 %collective-permute-start.8 = (bf16[16,64,768]{2,1,0:T(8,128)(2,1)S(1)}, bf16[16,64,768]{2,1,0:T(8,128)(2,1)S(1)}, u32[]{:S(2)}, u32[]{:S(2)}) collective-permute-start(bf16[16,64,768]{2,1,0:T(8,128)(2,1)S(1)} %all-to-all-done.refs_4_.refs_3_), channel_id=1, source_target_pairs={{0,1},{1,0},{2,3},{3,2},{4,5},{5,4},{6,7},{7,6},{8,9},{9,8},{10,11... | collective-permute-start | bytes 4718600 | tf_op jit(solution)/shard_map/ppermute | solution.py:584
  75.7 20.8 %collective-permute-start.22 = (bf16[2,64,768]{2,1,0:T(8,128)(2,1)S(1)}, bf16[2,64,768]{2,1,0:T(8,128)(2,1)S(1)}, u32[]{:S(2)}, u32[]{:S(2)}) collective-permute-start(bf16[2,64,768]{2,1,0:T(8,128)(2,1)S(1)} %get-tuple-element.114), channel_id=1, source_target_pairs={{0,16},{2,18},{4,20},{6,22},{8,24},{10,26},{12,28},{14,30},{16,0},... | collective-permute-start | bytes 589832 | tf_op jit(solution)/shard_map/ppermute | solution.py:591
  82.9 20.7 %collective-permute-start.26 = (bf16[2,64,768]{2,1,0:T(8,128)(2,1)S(1)}, bf16[2,64,768]{2,1,0:T(8,128)(2,1)S(1)}, u32[]{:S(2)}, u32[]{:S(2)}) collective-permute-start(bf16[2,64,768]{2,1,0:T(8,128)(2,1)S(1)} %get-tuple-element.117), channel_id=1, source_target_pairs={{0,4},{2,6},{4,0},{6,2},{8,12},{10,14},{12,8},{14,10},{16,20},{18,... | collective-permute-start | bytes 589832 | tf_op jit(solution)/shard_map/ppermute | solution.py:591
  84.4 21.1 %collective-permute-start.14 = (bf16[2,64,768]{2,1,0:T(8,128)(2,1)S(1)}, bf16[2,64,768]{2,1,0:T(8,128)(2,1)S(1)}, u32[]{:S(2)}, u32[]{:S(2)}) collective-permute-start(bf16[2,64,768]{2,1,0:T(8,128)(2,1)S(1)} %get-tuple-element.110), channel_id=1, source_target_pairs={{0,8},{2,10},{4,12},{6,14},{8,0},{10,2},{12,4},{14,6},{16,24},{18,... | collective-permute-start | bytes 589832 | tf_op jit(solution)/shard_map/ppermute | solution.py:591
  115.1 17.7 %collective-permute-start.20 = (bf16[2,64,768]{2,1,0:T(8,128)(2,1)S(1)}, bf16[2,64,768]{2,1,0:T(8,128)(2,1)S(1)}, u32[]{:S(2)}, u32[]{:S(2)}) collective-permute-start(bf16[2,64,768]{2,1,0:T(8,128)(2,1)S(1)} %collective-permute-done.18.refs_16_.refs_5_), channel_id=1, source_target_pairs={{0,1},{1,0},{2,3},{3,2},{4,5},{5,4},{6,7},{7,6},{8,9},{9,8},{10,11... | collective-permute-start | bytes 589832 | tf_op jit(solution)/shard_map/ppermute | solution.py:584
  121.8 21.2 %collective-permute-start.16 = (bf16[2,64,768]{2,1,0:T(8,128)(2,1)S(1)}, bf16[2,64,768]{2,1,0:T(8,128)(2,1)S(1)}, u32[]{:S(2)}, u32[]{:S(2)}) collective-permute-start(bf16[2,64,768]{2,1,0:T(8,128)(2,1)S(1)} %collective-permute-done.14.refs_12_.refs_5_), channel_id=1, source_target_pairs={{0,1},{1,0},{2,3},{3,2},{4,5},{5,4},{6,7},{7,6},{8,9},{9,8},{10,11... | collective-permute-start | bytes 589832 | tf_op jit(solution)/shard_map/ppermute | solution.py:584
  126.0 17.0 %collective-permute-start.17 = (bf16[2,64,768]{2,1,0:T(8,128)(2,1)S(1)}, bf16[2,64,768]{2,1,0:T(8,128)(2,1)S(1)}, u32[]{:S(2)}, u32[]{:S(2)}) collective-permute-start(bf16[2,64,768]{2,1,0:T(8,128)(2,1)S(1)} %collective-permute-done.15.refs_13_.refs_6_), channel_id=1, source_target_pairs={{0,1},{1,0},{2,3},{3,2},{4,5},{5,4},{6,7},{7,6},{8,9},{9,8},{10,11... | collective-permute-start | bytes 589832 | tf_op jit(solution)/shard_map/ppermute | solution.py:584
  141.5 24.4 %collective-permute-start.31 = (bf16[2,128,768]{2,1,0:T(8,128)(2,1)S(1)}, bf16[2,128,768]{2,1,0:T(8,128)(2,1)S(1)}, u32[]{:S(2)}, u32[]{:S(2)}) collective-permute-start(bf16[2,128,768]{2,1,0:T(8,128)(2,1)S(1)} %get-tuple-element.140), channel_id=1, source_target_pairs={{0,1},{1,0},{2,3},{3,2},{4,5},{5,4},{6,7},{7,6},{8,9},{9,8},{10,11... | collective-permute-start | bytes 1179656 | tf_op jit(solution)/shard_map/ppermute | solution.py:584
  149.5 20.4 %collective-permute-start.29 = (bf16[2,128,768]{2,1,0:T(8,128)(2,1)S(1)}, bf16[2,128,768]{2,1,0:T(8,128)(2,1)S(1)}, u32[]{:S(2)}, u32[]{:S(2)}) collective-permute-start(bf16[2,128,768]{2,1,0:T(8,128)(2,1)S(1)} %get-tuple-element.132), channel_id=1, source_target_pairs={{0,1},{1,0},{2,3},{3,2},{4,5},{5,4},{6,7},{7,6},{8,9},{9,8},{10,11... | collective-permute-start | bytes 1179656 | tf_op jit(solution)/shard_map/ppermute | solution.py:584
  156.4 22.8 %collective-permute-start.33 = (bf16[2,128,768]{2,1,0:T(8,128)(2,1)S(1)}, bf16[2,128,768]{2,1,0:T(8,128)(2,1)S(1)}, u32[]{:S(2)}, u32[]{:S(2)}) collective-permute-start(bf16[2,128,768]{2,1,0:T(8,128)(2,1)S(1)} %get-tuple-element.144), channel_id=1, source_target_pairs={{0,1},{1,0},{2,3},{3,2},{4,5},{5,4},{6,7},{7,6},{8,9},{9,8},{10,11... | collective-permute-start | bytes 1179656 | tf_op jit(solution)/shard_map/ppermute | solution.py:584
  158.6 27.0 %collective-permute-start.37 = (bf16[2,64,768]{2,1,0:T(8,128)(2,1)S(1)}, bf16[2,64,768]{2,1,0:T(8,128)(2,1)S(1)}, u32[]{:S(2)}, u32[]{:S(2)}) collective-permute-start(bf16[2,64,768]{2,1,0:T(8,128)(2,1)S(1)} %get-tuple-element.149), channel_id=1, source_target_pairs={{0,16},{2,18},{4,20},{6,22},{8,24},{10,26},{12,28},{14,30},{16,0},... | collective-permute-start | bytes 589832 | tf_op jit(solution)/shard_map/ppermute | solution.py:591
  160.6 27.0 %collective-permute-start.38 = (bf16[2,64,768]{2,1,0:T(8,128)(2,1)S(1)}, bf16[2,64,768]{2,1,0:T(8,128)(2,1)S(1)}, u32[]{:S(2)}, u32[]{:S(2)}) collective-permute-start(bf16[2,64,768]{2,1,0:T(8,128)(2,1)S(1)} %get-tuple-element.150), channel_id=1, source_target_pairs={{0,20},{2,22},{4,16},{6,18},{8,28},{10,30},{12,24},{14,26},{16,4},... | collective-permute-start | bytes 589832 | tf_op jit(solution)/shard_map/ppermute | solution.py:591
  166.6 21.1 %collective-permute-start.32 = (bf16[2,64,768]{2,1,0:T(8,128)(2,1)S(1)}, bf16[2,64,768]{2,1,0:T(8,128)(2,1)S(1)}, u32[]{:S(2)}, u32[]{:S(2)}) collective-permute-start(bf16[2,64,768]{2,1,0:T(8,128)(2,1)S(1)} %get-tuple-element.142), channel_id=1, source_target_pairs={{0,4},{2,6},{4,0},{6,2},{8,12},{10,14},{12,8},{14,10},{16,20},{18,... | collective-permute-start | bytes 589832 | tf_op jit(solution)/shard_map/ppermute | solution.py:591
  178.7 30.9 %collective-permute-start.30 = (bf16[8,128,768]{2,1,0:T(8,128)(2,1)S(1)}, bf16[8,128,768]{2,1,0:T(8,128)(2,1)S(1)}, u32[]{:S(2)}, u32[]{:S(2)}) collective-permute-start(bf16[8,128,768]{2,1,0:T(8,128)(2,1)S(1)} %get-tuple-element.135), channel_id=1, source_target_pairs={{0,1},{1,0},{2,3},{3,2},{4,5},{5,4},{6,7},{7,6},{8,9},{9,8},{10,11... | collective-permute-start | bytes 4718600 | tf_op jit(solution)/shard_map/ppermute | solution.py:584
  179.2 18.9 %collective-permute-start.39 = (bf16[2,64,768]{2,1,0:T(8,128)(2,1)S(1)}, bf16[2,64,768]{2,1,0:T(8,128)(2,1)S(1)}, u32[]{:S(2)}, u32[]{:S(2)}) collective-permute-start(bf16[2,64,768]{2,1,0:T(8,128)(2,1)S(1)} %get-tuple-element.151), channel_id=1, source_target_pairs={{0,24},{2,26},{4,28},{6,30},{8,16},{10,18},{12,20},{14,22},{16,8},... | collective-permute-start | bytes 589832 | tf_op jit(solution)/shard_map/ppermute | solution.py:591
  187.6 20.0 %collective-permute-start.34 = (bf16[2,64,768]{2,1,0:T(8,128)(2,1)S(1)}, bf16[2,64,768]{2,1,0:T(8,128)(2,1)S(1)}, u32[]{:S(2)}, u32[]{:S(2)}) collective-permute-start(bf16[2,64,768]{2,1,0:T(8,128)(2,1)S(1)} %get-tuple-element.145), channel_id=1, source_target_pairs={{0,8},{2,10},{4,12},{6,14},{8,0},{10,2},{12,4},{14,6},{16,24},{18,... | collective-permute-start | bytes 589832 | tf_op jit(solution)/shard_map/ppermute | solution.py:591
  187.6 20.0 %collective-permute-start.35 = (bf16[2,64,768]{2,1,0:T(8,128)(2,1)S(1)}, bf16[2,64,768]{2,1,0:T(8,128)(2,1)S(1)}, u32[]{:S(2)}, u32[]{:S(2)}) collective-permute-start(bf16[2,64,768]{2,1,0:T(8,128)(2,1)S(1)} %get-tuple-element.146), channel_id=1, source_target_pairs={{0,12},{2,14},{4,8},{6,10},{8,4},{10,6},{12,0},{14,2},{16,28},{18,... | collective-permute-start | bytes 589832 | tf_op jit(solution)/shard_map/ppermute | solution.py:591
  211.6 40.1 %all-to-all-start.1 = ((bf16[16,64,768]{2,1,0:T(8,128)(2,1)}), bf16[16,64,768]{2,1,0:T(8,128)(2,1)S(1)}, u32[]{:S(2)}, u32[]{:S(2)}) async-start(bf16[16,64,768]{2,1,0:T(8,128)(2,1)} %get-tuple-element.136), calls=%async_computation.1 | async-start | bytes 3145728 | tf_op jit(solution)/shard_map/all_to_all | solution.py:827
  231.8 26.0 %collective-permute-start.44 = (bf16[768,384]{1,0:T(8,128)(2,1)S(1)}, bf16[768,384]{1,0:T(8,128)(2,1)S(1)}, u32[]{:S(2)}, u32[]{:S(2)}) collective-permute-start(bf16[768,384]{1,0:T(8,128)(2,1)S(1)} %get-tuple-element.178), channel_id=1, source_target_pairs={{0,1},{1,0},{2,3},{3,2},{4,5},{5,4},{6,7},{7,6},{8,9},{9,8},{10,11... | collective-permute-start | bytes 1769480 | tf_op jit(solution)/shard_map/ppermute | solution.py:584
  268.2 20.0 %collective-permute-start.43 = (bf16[512,768]{1,0:T(8,128)(2,1)S(1)}, bf16[512,768]{1,0:T(8,128)(2,1)S(1)}, u32[]{:S(2)}, u32[]{:S(2)}) collective-permute-start(bf16[512,768]{1,0:T(8,128)(2,1)S(1)} %get-tuple-element.174), channel_id=1, source_target_pairs={{0,1},{1,0},{2,3},{3,2},{4,5},{5,4},{6,7},{7,6},{8,9},{9,8},{10,11... | collective-permute-start | bytes 2359304 | tf_op jit(solution)/shard_map/ppermute | solution.py:584
  (52 other events, 598.1 us)

commit v2 on v1

--- a/solution.py
+++ b/solution.py
@@ -67,7 +67,7 @@
     return math.prod(x.shape) * jnp.dtype(x.dtype).itemsize
 
 
-def run(kernel, operands, outs, flops=0, limit=32, first=(), mark=False, **more):
+def run(kernel, operands, outs, flops=0, limit=32, first=(), mark=False, light=False, **more):
     if "in_specs" not in more:
         more["in_specs"] = [spec_of(x) for x in operands]
     operands = [in_hbm(x.values) if isinstance(x, Far) else x for x in operands]
@@ -75,6 +75,8 @@
     outs = [outs] if alone else list(outs)
     count, results = len(operands), len(outs)
     moved = sum(map(size_of, operands)) + sum(map(size_of, outs))
+    if light:
+        flops = moved = 0
     first = tuple(first)
     more["in_specs"] = list(more["in_specs"]) + [pl.BlockSpec(memory_space=pl.ANY)] * len(first)
     if mark:
@@ -217,9 +219,12 @@
 
 
 def attend_back_kernel(
-    block, place_ref, q_ref, k_ref, v_ref, unreached_ref, member_ref, out_ref, total_ref, mine_ref, more_ref, res_ref, dk, dv, grads
+    chips, block, place_ref, q_ref, k_ref, v_ref, unreached_ref, member_ref, out_ref, total_ref, mine_ref, more_ref,
+    turned_ref, weight_ref, scale_ref, second_ref,
+    res_ref, keep_ref, give_ref, sums_ref, dk, dv, grads, parts, products, columns,
 ):
-    side = place_ref[1]
+    place, side = place_ref[0], place_ref[1]
+    step = pl.program_id(0)
     rows = q_ref.shape[0]
     half = rows // 2
     grads[pl.ds(pl.multiple_of(side * half, half), half)] = mine_ref[...]
@@ -267,29 +272,87 @@
     res_ref[1] = dk[...].astype(low)
     res_ref[2] = dv[...].astype(low)
 
-
-def attend_back(place, projected, unreached, member, out, total, mine, more, block=256, first=()):
+    pair = dot(turned_ref[...], jnp.concatenate([res_ref[0], res_ref[1]], axis=1))
+    grads_in = (pair[:, :LANES], pair[:, LANES:], dot(turned_ref[...], res_ref[2]))
+    product = column = None
+    for n, grad_in in enumerate(grads_in):
+        weight = weight_ref[n].astype(wide)
+        total = jnp.sum(res_ref[n].astype(wide), axis=0, keepdims=True)
+        terms = weight * grad_in, weight * total
+        product = terms[0] if n == 0 else product + terms[0]
+        column = terms[1] if n == 0 else column + terms[1]
+        parts[n] = grad_in.astype(low)
+
+    @pl.when(step == 0)
+    def _():
+        products[...] = product
+        columns[...] = column
+
+    @pl.when(step > 0)
+    def _():
+        products[...] += product
+        columns[...] += column
+
+    lanes = pl.ds(pl.multiple_of(step * LANES, LANES), LANES)
+    if chips:
+        height = keep_ref.shape[3]
+        for k in range(chips):
+            for ref, target in ((keep_ref, place ^ (2 * k)), (give_ref, place ^ (2 * k + 1))):
+                ref[k % 2, k // 2, :, :, lanes] = parts[
+                    :, pl.ds(pl.multiple_of(target * height, height), height)
+                ]
+    else:
+        keep_ref[:, :, lanes] = parts[...]
+        give_ref[...] = jnp.zeros(give_ref.shape, low)
+
+    @pl.when(step == pl.num_programs(0) - 1)
+    def _():
+        bias_grad = jnp.sum(columns[...].T, axis=0, keepdims=True)
+        whole = jnp.sum(products[...].T, axis=0, keepdims=True)
+        sums_ref[0:1] = (whole - scale_ref[1:2] * bias_grad) / scale_ref[0:1]
+        sums_ref[1:2] = bias_grad
+        sums_ref[2:4] = second_ref[...]
+
+
+def attend_back(
+    place, projected, unreached, member, out, total, mine, more, turned, weight, scales, second,
+    chips, block=256, first=(),
+):
     rows, width = projected.shape
     pairs = width // (3 * LANES)
+    features = turned.shape[0]
 
     def part(n, height=rows):
         return pl.BlockSpec((height, LANES), lambda p: (0, n * pairs + p))
 
-    fixed = pl.BlockSpec((rows, LANES), lambda p: (0, 0))
+    def fixed(shape):
+        return pl.BlockSpec(shape, lambda p: (0,) * len(shape))
+
+    if chips:
+        shape = (2, chips // 2, 3, features // (2 * chips), width // 3)
+        shapes = [shape, shape]
+    else:
+        shapes = [(3, features, width // 3), (8, LANES)]
+    triple = pl.BlockSpec((3, rows, LANES), lambda p: (0, 0, p))
     return run(
-        functools.partial(attend_back_kernel, block),
+        functools.partial(attend_back_kernel, chips, block),
         (
             place, in_hbm(projected), in_hbm(projected), in_hbm(projected), unreached, member,
-            in_hbm(out), in_hbm(total), mine, more,
+            in_hbm(out), in_hbm(total), mine, more, in_hbm(turned), in_hbm(weight), scales, second,
         ),
-        [kept((3, rows, width // 3), low)],
-        flops=24e9,
+        [kept((3, rows, width // 3), low), *[array(x, low) for x in shapes], array((4, features), wide)],
+        flops=30e9,
+        limit=44,
         first=first,
         grid=(pairs,),
-        in_specs=[spec_of(place), part(0), part(1), part(2), fixed, fixed, part(0), part(0)]
-        + [part(0, rows // 2)] * 2,
-        out_specs=[pl.BlockSpec((3, rows, LANES), lambda p: (0, 0, p))],
-        scratch_shapes=[pltpu.VMEM((rows, LANES), wide)] * 2 + [pltpu.VMEM((rows, LANES), low)],
+        in_specs=[spec_of(place), part(0), part(1), part(2), fixed(unreached.shape), fixed(member.shape)]
+        + [part(0), part(0), part(0, rows // 2), part(0, rows // 2), fixed(turned.shape)]
+        + [pl.BlockSpec((3, features, LANES), lambda p: (0, 0, p)), fixed(scales.shape)]
+        + [fixed(second.shape)],
+        out_specs=[triple, fixed(shapes[0]), fixed(shapes[1]), fixed((4, features))],
+        scratch_shapes=[pltpu.VMEM((rows, LANES), wide)] * 2
+        + [pltpu.VMEM((rows, LANES), low), pltpu.VMEM((3, features, LANES), low)]
+        + [pltpu.VMEM((features, LANES), wide)] * 2,
     )
 
 
@@ -471,47 +534,37 @@
     mine_ref[...] = dot(branch, weight_ref[...]).astype(low)
 
 
-def output_part_kernel(branch_ref, keep_ref, more_ref, own_ref, give_ref):
-    give_ref[...] = dot(branch_ref[...], more_ref[...], TN).astype(low)
-    own_ref[...] = dot(branch_ref[...], keep_ref[...], TN)
-
-
-def first_kernel(
-    place_ref, grads_ref, full_ref, own_in_ref, other_in_ref, second_ref, give_ref, own_ref, sums_ref
-):
+def output_part_kernel(chips, place_ref, branch_ref, keep_ref, more_ref, own_ref, give_ref, parts):
+    place = place_ref[0]
+    parts[0] = dot(branch_ref[...], keep_ref[...], TN)
+    parts[1] = dot(branch_ref[...], more_ref[...], TN)
+    if chips:
+        rows = own_ref.shape[2]
+        for k in range(chips):
+            block = pl.ds(pl.multiple_of((place ^ (2 * k)) * rows, rows), rows)
+            own_ref[:, k] = parts[:, block]
+            block = pl.ds(pl.multiple_of((place ^ (2 * k + 1)) * rows, rows), rows)
+            give_ref[:, k] = parts[:, block].astype(low)
+    else:
+        own_ref[...] = parts[0]
+        give_ref[...] = parts[1].astype(low)
+
+
+def output_sum_kernel(own_ref, more_ref, keep_ref, give_ref):
+    keep_ref[...] = own_ref[0] + more_ref[0].astype(wide)
+    give_ref[...] = (own_ref[1] + more_ref[1].astype(wide)).astype(low)
+
+
+def first_kernel(place_ref, grads_ref, full_ref, give_ref, own_ref):
     half = own_ref.shape[0]
     side = place_ref[1]
-    sums = None
-    for ref, out_ref, first in ((other_in_ref, give_ref, 1 - side), (own_in_ref, own_ref, side)):
+    for out_ref, first in ((give_ref, 1 - side), (own_ref, side)):
         rows = pl.ds(pl.multiple_of(first * half, half), half)
         total = None
         for n in range(3):
             term = dot(grads_ref[n, rows], full_ref[n], NT)
             total = term if total is None else total + term
         out_ref[...] = total.astype(out_ref.dtype)
-        hat, _ = normalize(ref[...].astype(wide))
-        more = [jnp.sum(total * hat, axis=0, keepdims=True), jnp.sum(total, axis=0, keepdims=True)]
-        sums = more if sums is None else [x + y for x, y in zip(sums, more)]
-    sums_ref[0:1] = sums[0]
-    sums_ref[1:2] = sums[1]
-    sums_ref[2:4] = second_ref[...]
-
-
-def weight_part_kernel(chips, place_ref, turned_ref, grads_ref, part_ref, more_ref, keep_ref, give_ref, parts):
-    place = place_ref[0]
-    for n in range(3):
-        parts[n] = dot(turned_ref[...], grads_ref[n]).astype(low)
-    parts[3] = (part_ref[...] + more_ref[...].astype(wide)).astype(low)
-    if chips:
-        rows = keep_ref.shape[3]
-        for k in range(chips):
-            target = place ^ (2 * k)
-            keep_ref[k % 2, k // 2] = parts[:, pl.ds(pl.multiple_of(target * rows, rows), rows)]
-            target = target ^ 1
-            give_ref[k % 2, k // 2] = parts[:, pl.ds(pl.multiple_of(target * rows, rows), rows)]
-    else:
-        keep_ref[...] = parts[...]
-        give_ref[...] = jnp.zeros(give_ref.shape, low)
 
 
 def spread(sums):
@@ -535,14 +588,23 @@
     return (terms[0] + terms[1]) + terms[2]
 
 
-def halves_kernel(keep_ref, more_ref, sums_ref, more_sums_ref, near_ref, far_ref, out_sums_ref):
-    count = near_ref.shape[0]
-    sums = sums_ref[...] + more_sums_ref[...]
+def halves_kernel(
+    keep_ref, more_ref, output_ref, more_output_ref, sums_ref, core_ref, across_ref, both_ref,
+    near_ref, far_ref, out_sums_ref,
+):
+    count, size = near_ref.shape
+    pieces = keep_ref.shape[1]
+    height = count // pieces
+    sums = (sums_ref[...] + core_ref[...]) + (across_ref[...] + both_ref[...])
     out_sums_ref[...] = sums
     far_ref[count:] = spread(sums)
     for side, ref in ((0, near_ref), (1, far_ref)):
-        total = keep_ref[side].astype(wide) + more_ref[side].astype(wide)
-        ref[:count] = total.reshape(count, total.shape[-1]).astype(low)
+        for k in range(pieces):
+            total = keep_ref[side, k].astype(wide) + more_ref[side, k].astype(wide)
+            total = total.reshape(-1, size).astype(low)
+            ref[k * height : k * height + total.shape[0]] = total
+            rest = output_ref[2 * k + side] + more_output_ref[2 * k + side].astype(wide)
+            ref[k * height + total.shape[0] : (k + 1) * height] = rest.astype(low)
 
 
 def quarters_kernel(near_ref, more_ref, sums_ref, own_ref, out_sums_ref, *out_refs):
@@ -750,6 +812,14 @@
     spans = (near, far, next_far, next_near)
     more_arrived = {k: across(arrived[k]) for span in spans for k in range(*span)}
 
+    turned, turned_done = run(
+        turned_kernel,
+        (place, Far(inputs), Far(other_inputs), scales),
+        kept((width, tree_size), low),
+        mark=True,
+        first=(packed[0],),
+    )
+
     weight_in, weight_out = expert_in[0], expert_out[0]
     buffers = None
     returned = {}
@@ -760,8 +830,7 @@
         buffers, keep, give = expert_group(
             place, weight_in, weight_out, slot_grads, more_slot_grads,
             own_pieces, [more_arrived[k] for k in range(*span)], buffers, span, chips,
-            [more_arrived[k] for later in spans[turn + 1 : turn + 2] for k in range(*later)]
-            + ([arrived[k] for k in range(1, chips)] if turn == 0 else []),
+            [turned_done] + [arrived[k] for k in range(1, chips)] if turn == 0 else [],
         )
         *sums, token = run(pieces_kernel, (keep, across(give)), [piece] * quarter, mark=True)
         done.append(token)
@@ -777,6 +846,7 @@
         flops=2 * chips * rows * width * hidden,
         first=done[2:3],
         mark=True,
+        light=True,
         grid=(chips,),
         in_specs=[
             pl.BlockSpec((1, rows, hidden), lambda i: (i, 0, 0)),
@@ -799,34 +869,15 @@
         in_specs=[stripe, fixed],
         out_specs=[pl.BlockSpec((tile, width), lambda i: (i, 0))],
     )
-    expert_in_grad, in_done = run(
-        product_kernel,
-        (in_hbm(slot_rows), in_hbm(grad_pres)),
-        array((width, hidden), wide),
-        flops=2 * chips * rows * width * hidden,
-        first=(out_done, *back[2]),
-        mark=True,
-        grid=(hidden // tile,),
-        in_specs=[fixed, stripe],
-        out_specs=[pl.BlockSpec((width, tile), lambda i: (0, i))],
-    )
     own_part, sibling_part = run(
         unpack_kernel,
         (own_place[None], sibling_place[None], *[returned[k] for k in range(chips)]),
         [array((own_count, width), low)] * 2,
-        first=(in_done,),
+        first=(out_done, *back[2]),
         flops=4 * own_count * own_count * width,
     )
     sibling_part = swapped(sibling_part, 1)
-    ffn_sums, sums_done = run(
-        ffn_sum_kernel,
-        (place, ffn_keep, ffn_more),
-        kept((experts_in_all, capacity, width), low),
-        mark=True,
-    )
-    ffn_back = lax.all_to_all(ffn_sums, "fsdp", 0, 0, tiled=True)
-
-    grad_middle, grad_branch, grad_mine, grad_give, second_sums = run(
+    grad_middle, grad_branch, grad_mine, grad_give, second_sums, middle_done = run(
         middle_back_kernel,
         (
             own_part, sibling_part, Far(middle), Far(cotangent), scales,
@@ -839,94 +890,121 @@
             array((own_count, local_width), low),
             array((2, width), wide),
         ],
-        first=(sums_done,),
-        flops=2 * own_count * width * width,
-    )
-    grad_more = across(grad_give)
-    output_own, output_give, output_done = run(
-        output_part_kernel,
-        (grad_branch, Far(attended_keep), Far(attended_more)),
-        [kept((width, local_width), wide), array((width, local_width), low)],
+        first=(ffn_more,),
         mark=True,
         flops=2 * own_count * width * width,
     )
+    grad_more = across(grad_give)
+    ffn_sums, sums_done = run(
+        ffn_sum_kernel,
+        (place, ffn_keep, ffn_more),
+        kept((experts_in_all, capacity, width), low),
+        mark=True,
+        first=(middle_done,),
+    )
+    ffn_back = lax.all_to_all(ffn_sums, "fsdp", 0, 0, tiled=True)
+
+    if in_kernel:
+        blocks = (2, chips, shard_rows, local_width)
+        outs = [array(blocks, wide), array(blocks, low)]
+    else:
+        outs = [array((width, local_width), wide), array((width, local_width), low)]
+    output_own, output_give = run(
+        functools.partial(output_part_kernel, chips if in_kernel else 0),
+        (place, grad_branch, Far(attended_keep), Far(attended_more)),
+        outs,
+        scratch_shapes=[pltpu.VMEM((2, width, local_width), wide)],
+        flops=2 * own_count * width * width,
+    )
+    if in_kernel:
+        output_own, output_give, output_done = run(
+            output_sum_kernel,
+            (output_own, swapped(output_give, 1)),
+            [array(blocks[1:], wide), array(blocks[1:], low)],
+            mark=True,
+        )
+    else:
+        output_done = middle_done
     output_more = across(output_give)
-    turned, turned_done = run(
-        turned_kernel,
-        (place, Far(inputs), Far(other_inputs), scales),
-        kept((width, tree_size), low),
-        mark=True,
-    )
-    (grad_projected,) = attend_back(
+    grad_projected, part_keep, part_give, norm_sums = attend_back(
         place, projected, unreached, member, attended, totals, grad_mine, grad_more,
-        first=(turned_done, output_done),
-    )
-
-    first_give, first_own, norm_sums, give_done = run(
-        first_kernel,
-        (
-            place, Far(grad_projected), Far(full_weight), Far(inputs), Far(other_inputs), second_sums,
-        ),
-        [array((own_count, width), low), array((own_count, width), wide), array((4, width), wide)],
-        mark=True,
-        first=(ffn_back,),
-        flops=2 * tree_size * width * 3 * local_width,
-    )
-    norm_more = across(norm_sums)
-    norm_sums = norm_sums + norm_more
-    first_more = across(first_give)
-    if in_kernel:
-        block = array((2, chips // 2, 4, shard_rows, local_width), low)
-        part_outs = [block, block]
-    else:
-        part_outs = [array((4, width, local_width), low), array((8, LANES), low)]
-    part_keep, part_give, part_done = run(
-        functools.partial(weight_part_kernel, chips if in_kernel else 0),
-        (place, Far(turned), Far(grad_projected), Far(output_own), output_more),
-        part_outs,
-        mark=True,
-        first=(give_done, norm_more),
-        flops=2 * tree_size * width * 3 * local_width,
-        scratch_shapes=[pltpu.VMEM((4, width, local_width), low)],
-    )
+        turned, full_weight, scales, second_sums,
+        chips if in_kernel else 0, first=(sums_done, output_done),
+    )
+
     if in_kernel:
         part_more = swapped(part_give, 1)
         rows = 4 * shard_rows
-        near_sum, far_sum, norm_sums = run(
+        near_sum, far_sum, norm_sums, half_done = run(
             halves_kernel,
-            (part_keep, part_more, norm_sums, swapped(norm_sums, 1)),
+            (
+                part_keep, part_more, output_own, output_more,
+                norm_sums, swapped(norm_sums, 1), across(norm_sums),
+                lax.ppermute(norm_sums, ("fsdp", "tp"), [(i, i ^ 3) for i in range(2 * experts_in_all)]),
+            ),
             [
-                array((chips // 2 * rows, local_width), low),
-                array((chips // 2 * rows + 32, local_width), low),
+                kept((chips // 2 * rows, local_width), low),
+                kept((chips // 2 * rows + 32, local_width), low),
                 array((4, width), wide),
             ],
+            mark=True,
         )
+    else:
+        half_done = norm_sums
+    first_give, first_own, give_done = run(
+        first_kernel,
+        (place, Far(grad_projected), Far(full_weight)),
+        [array((own_count, width), low), array((own_count, width), wide)],
+        mark=True,
+        first=(half_done,),
+        light=True,
+        flops=2 * tree_size * width * 3 * local_width,
+    )
+    first_more = across(first_give)
+    expert_in_grad, in_done = run(
+        product_kernel,
+        (in_hbm(slot_rows), in_hbm(grad_pres)),
+        array((width, hidden), wide),
+        flops=2 * chips * capacity * 4 * width * hidden,
+        first=(give_done,),
+        mark=True,
+        light=True,
+        grid=(hidden // tile,),
+        in_specs=[fixed, stripe],
+        out_specs=[pl.BlockSpec((width, tile), lambda i: (0, i))],
+    )
+    if in_kernel:
         own_sum, norm_sums, *away = run(
             quarters_kernel,
-            (near_sum, swapped(far_sum, 2), norm_sums),
+            (Far(near_sum), Far(swapped(far_sum, 2)), norm_sums),
             [array((rows, local_width), wide), array((4, width), wide)]
             + [array((rows + 32, local_width), low)] * (chips // 2 - 1),
-            first=(first_more,),
+            first=(in_done, ffn_back),
         )
         away = [swapped(away[k - 1], 4 * k) for k in range(1, chips // 2)]
     else:
-        blocks = part_keep.reshape(4, experts_in_all, shard_rows, local_width).transpose(1, 0, 2, 3)
+        output_part = (output_own + output_more.astype(wide)).astype(low)
+        blocks = jnp.concatenate([part_keep, output_part[None]])
+        blocks = blocks.reshape(4, experts_in_all, shard_rows, local_width).transpose(1, 0, 2, 3)
         summed = reduce_blocks(blocks, index, experts_in_all)
         bit = 1
         while bit < experts_in_all:
             norm_sums = norm_sums + swapped(norm_sums, bit)
             bit *= 2
+        norm_sums = norm_sums + across(norm_sums)
     input_grad, input_done = run(
         input_grad_kernel,
         (Far(grad_middle), first_own, first_more, Far(inputs), scales),
         array((own_count, width), wide),
         mark=True,
+        light=True,
     )
     out_block, out_done = run(
         out_kernel,
         (own_slot[None], ffn_back.reshape(slot_count, width), Far(middle)),
         array((own_count, width), low),
         mark=True,
+        light=True,
         flops=2 * own_count * slot_count * width,
     )
     if in_kernel:

time: 315 us -> 303 us (0.962)
  starting transfers between devices: 86.3 us -> 73.6 us
    ppermute x31 -> x32, starting transfers between devices: 54.4 us -> 45.5 us  [swapped(): return lax.ppermute(values, 'fsdp', [(i, i ^ offset) for i in range(count)])]
    ppermute x31 -> x32, waiting for transfers between devices: 34.3 us -> 40.7 us  [swapped(): return lax.ppermute(values, 'fsdp', [(i, i ^ offset) for i in range(count)])]
    all_to_all x1, starting transfers between devices: 7.97 us -> 3.77 us  [shards(): ffn_back = lax.all_to_all(ffn_sums, 'fsdp', 0, 0, tiled=True)]
  transfers between devices with their start and end apart: 54 -> 56, of which waited for: 19 -> 21; matrix products, arithmetic and copies ran while one was open for 3% -> 4% of each run, Pallas kernels for 39% -> 40%
where the time goes in v2:
time: 303 us; the launch traced here: 299 us
  Pallas kernels  129 us (43%)
  waiting for transfers between devices  81.6 us (27%)
  starting transfers between devices  73.6 us (24%)
  local copies, waits for them, and re-layouts  6.45 us (2%)
  other arithmetic  4.41 us (1%)
  matrix products  3.21 us (1%)
    pallas_call x29, Pallas kernels, run(): pl.pallas_call(whole, out_shape=outs, compiler_params=pltpu.CompilerParam...  129 us
    ppermute x32, starting transfers between devices, swapped(): return lax.ppermute(values, 'fsdp', [(i, i ^ offset) for i in range(count)])  45.5 us
    ppermute x32, waiting for transfers between devices, swapped(): return lax.ppermute(values, 'fsdp', [(i, i ^ offset) for i in range(count)])  40.7 us
    ppermute x21, waiting for transfers between devices, across(): return lax.ppermute(values, 'tp', [(0, 1), (1, 0)])  29.8 us
    ppermute x21, starting transfers between devices, across(): return lax.ppermute(values, 'tp', [(0, 1), (1, 0)])  19 us
    all_to_all x1, waiting for transfers between devices, shards(): lax.all_to_all(packed_grads.reshape(experts_in_all, capacity, width), 'fs...  11.1 us
  transfers between devices with their start and end apart: 56, of which 21 were waited for; matrix products, arithmetic and copies ran while one was open for 4% of the time, Pallas kernels for 40%

profile of v2, /device:TPU:0, one launch (start us, length us, event | category | flops | bytes accessed | tf_op | source)
XLA Modules:
  0.0 299.2 jit_solution(3450229414615677654)
XLA Ops:
  15.9 4.1 %collective-permute-done.3 = bf16[4,48,384]{2,1,0:T(8,128)(2,1)S(1)} collective-permute-done((bf16[4,48,384]{2,1,0:T(8,128)(2,1)S(1)}, bf16[4,48,384]{2,1,0:T(8,128)(2,1)S(1)}, u32[]{:S(2)}, u32[]{:S(2)}) %collective-permute-start.3) | collective-permute-done | bytes 147488 | tf_op jit(solution)/shard_map/ppermute | solution.py:653
  29.6 5.2 %all-to-all-start = ((bf16[16,64,768]{2,1,0:T(8,128)(2,1)}), bf16[16,64,768]{2,1,0:T(8,128)(2,1)S(1)}, u32[]{:S(2)}, u32[]{:S(2)}) async-start(bf16[16,64,768]{2,1,0:T(8,128)(2,1)} %bitcast.60), calls=%async_computation | async-start | bytes 3145728 | tf_op jit(solution)/shard_map/all_to_all | solution.py:759
  37.8 6.3 %shard_map.214 = (bf16[3,768,384]{2,1,0:T(8,128)(2,1)}, bf16[768,384]{1,0:T(8,128)(2,1)}, bf16[1024,1152]{1,0:T(8,128)(2,1)}, f32[4,768]{1,0:T(4,128)S(1)}) custom-call(s32[2]{0:T(128)S(1)} %pad_add_fusion.refs_0_, bf16[512,768]{1,0:T(8,128)(2,1)S(1)} %copy-done.2, bf16[512,768]{1,0:T(8,128)(2,1)S(1)} %collective-permute-done.7.refs_3_.refs_2_, ...), custom_call_target="tpu_custom_call" | custom-call | flops 1811939328 | bytes 8675336 | tf_op jit(solution)/shard_map/pallas_call | solution.py:95
  45.6 9.5 %shard_map.215 = (bf16[1024,384]{1,0:T(8,128)(2,1)}, f32[1024,384]{1,0:T(8,128)}, bf16[512,384]{1,0:T(8,128)(2,1)S(1)}, bf16[512,384]{1,0:T(8,128)(2,1)}) custom-call(s32[2]{0:T(128)S(1)} %pad_add_fusion.refs_0_, bf16[1024,1152]{1,0:T(8,128)(2,1)} %get-tuple-element.109.refs_1_.refs_2_.refs_3_, ...), custom_call_target="tpu_custom_call" | custom-call | flops 12000000000 | bytes 10747912 | tf_op jit(solution)/shard_map/pallas_call | solution.py:95
  55.7 11.1 %all-to-all-done.refs_4_.refs_3_ = bf16[16,64,768]{2,1,0:T(8,128)(2,1)S(1)} async-done(((bf16[16,64,768]{2,1,0:T(8,128)(2,1)}), bf16[16,64,768]{2,1,0:T(8,128)(2,1)S(1)}, u32[]{:S(2)}, u32[]{:S(2)}) %all-to-all-start) | async-done | bytes 1572896 | tf_op jit(solution)/shard_map/all_to_all | solution.py:759
  78.1 4.6 %collective-permute-start.14 = (bf16[2,64,768]{2,1,0:T(8,128)(2,1)S(1)}, bf16[2,64,768]{2,1,0:T(8,128)(2,1)S(1)}, u32[]{:S(2)}, u32[]{:S(2)}) collective-permute-start(bf16[2,64,768]{2,1,0:T(8,128)(2,1)S(1)} %get-tuple-element.115), channel_id=1, source_target_pairs={{0,8},{2,10},{4,12},{6,14},{8,0},{10,2},{12,4},{14,6},{16,24},{18,... | collective-permute-start | bytes 589832 | tf_op jit(solution)/shard_map/ppermute | solution.py:653
  85.5 4.5 %collective-permute-start.19 = (bf16[2,64,768]{2,1,0:T(8,128)(2,1)S(1)}, bf16[2,64,768]{2,1,0:T(8,128)(2,1)S(1)}, u32[]{:S(2)}, u32[]{:S(2)}) collective-permute-start(bf16[2,64,768]{2,1,0:T(8,128)(2,1)S(1)} %get-tuple-element.118), channel_id=1, source_target_pairs={{0,28},{2,30},{4,24},{6,26},{8,20},{10,22},{12,16},{14,18},{16,12}... | collective-permute-start | bytes 589832 | tf_op jit(solution)/shard_map/ppermute | solution.py:653
  99.1 5.4 %collective-permute-done.19.refs_16_.refs_6_ = bf16[2,64,768]{2,1,0:T(8,128)(2,1)S(1)} collective-permute-done((bf16[2,64,768]{2,1,0:T(8,128)(2,1)S(1)}, bf16[2,64,768]{2,1,0:T(8,128)(2,1)S(1)}, u32[]{:S(2)}, u32[]{:S(2)}) %collective-permute-start.19) | collective-permute-done | bytes 196640 | tf_op jit(solution)/shard_map/ppermute | solution.py:653
  108.8 8.9 %collective-permute-done.22.refs_13_.refs_5_ = bf16[2,64,768]{2,1,0:T(8,128)(2,1)S(1)} collective-permute-done((bf16[2,64,768]{2,1,0:T(8,128)(2,1)S(1)}, bf16[2,64,768]{2,1,0:T(8,128)(2,1)S(1)}, u32[]{:S(2)}, u32[]{:S(2)}) %collective-permute-start.22) | collective-permute-done | bytes 196640 | tf_op jit(solution)/shard_map/ppermute | solution.py:653
  125.4 6.4 %shard_map.219 = (bf16[8,256,768]{2,1,0:T(8,128)(2,1)}, bf16[8,256,768]{2,1,0:T(8,128)(2,1)}, bf16[8,256,1536]{2,1,0:T(8,128)(2,1)}, bf16[8,256,1536]{2,1,0:T(8,...) custom-call(s32[2]{0:T(128)S(1)} %pad_add_fusion.refs_0_, bf16[768,1536]{1,0:T(8,128)(2,1)S(1)} %bitcast.50, ...), custom_call_target="tpu_custom_call" | custom-call | flops 3623878656 | bytes 28704776 | tf_op jit(solution)/shard_map/pallas_call | solution.py:95
  132.4 6.2 %shard_map.220 = (bf16[8,256,768]{2,1,0:T(8,128)(2,1)}, bf16[8,256,768]{2,1,0:T(8,128)(2,1)}, bf16[8,256,1536]{2,1,0:T(8,128)(2,1)}, bf16[8,256,1536]{2,1,0:T(8,...) custom-call(s32[2]{0:T(128)S(1)} %pad_add_fusion.refs_0_, ...), custom_call_target="tpu_custom_call", output_to_operand_aliasing={{0}: (9, {}), {1}: (10, {}), {2}: (11, {}), {3}: (12, {})} | custom-call | flops 3623878656 | bytes 47579144 | tf_op jit(solution)/shard_map/pallas_call | solution.py:95
  140.2 6.3 %shard_map.221 = (bf16[8,256,768]{2,1,0:T(8,128)(2,1)}, bf16[8,256,768]{2,1,0:T(8,128)(2,1)}, bf16[8,256,1536]{2,1,0:T(8,128)(2,1)}, bf16[8,256,1536]{2,1,0:T(8,...) custom-call(s32[2]{0:T(128)S(1)} %pad_add_fusion.refs_0_, ...), custom_call_target="tpu_custom_call", output_to_operand_aliasing={{0}: (9, {}), {1}: (10, {}), {2}: (11, {}), {3}: (12, {})} | custom-call | flops 3623878656 | bytes 47579144 | tf_op jit(solution)/shard_map/pallas_call | solution.py:95
  148.5 6.3 %shard_map.222 = (bf16[8,256,768]{2,1,0:T(8,128)(2,1)}, bf16[8,256,768]{2,1,0:T(8,128)(2,1)}, bf16[8,256,1536]{2,1,0:T(8,128)(2,1)}, bf16[8,256,1536]{2,1,0:T(8,...) custom-call(s32[2]{0:T(128)S(1)} %pad_add_fusion.refs_0_, ...), custom_call_target="tpu_custom_call", output_to_operand_aliasing={{0}: (9, {}), {1}: (10, {}), {2}: (11, {}), {3}: (12, {})} | custom-call | flops 3623878656 | bytes 47579144 | tf_op jit(solution)/shard_map/pallas_call | solution.py:95
  155.3 7.6 %collective-permute-done.29.refs_1_ = bf16[2,128,768]{2,1,0:T(8,128)(2,1)S(1)} collective-permute-done((bf16[2,128,768]{2,1,0:T(8,128)(2,1)S(1)}, bf16[2,128,768]{2,1,0:T(8,128)(2,1)S(1)}, u32[]{:S(2)}, u32[]{:S(2)}) %collective-permute-start.29) | collective-permute-done | bytes 393248 | tf_op jit(solution)/shard_map/ppermute | solution.py:646
  163.0 8.7 %shard_map.224 = (f32[8,128,768]{2,1,0:T(8,128)S(1)}, bf16[8,128,768]{2,1,0:T(8,128)(2,1)S(1)}, f32[8,128]{1,0:T(8,128)S(1)}) custom-call(bf16[8,256,1536]{2,1,0:T(8,128)(2,1)} %get-tuple-element.136.refs_0_, bf16[1536,768]{1,0:T(8,128)(2,1)S(1)} %bitcast.49, f32[8,128]{1,0:T(8,128)S(1)} %get-tuple-element.139.refs_2_), custom_call_target="tpu_custom_call" | custom-call | tf_op jit(solution)/shard_map/pallas_call | solution.py:95
  181.2 4.1 %collective-permute-done.37.refs_6_ = bf16[2,64,768]{2,1,0:T(8,128)(2,1)S(1)} collective-permute-done((bf16[2,64,768]{2,1,0:T(8,128)(2,1)S(1)}, bf16[2,64,768]{2,1,0:T(8,128)(2,1)S(1)}, u32[]{:S(2)}, u32[]{:S(2)}) %collective-permute-start.37) | collective-permute-done | bytes 196640 | tf_op jit(solution)/shard_map/ppermute | solution.py:653
  185.3 4.6 %collective-permute-done.38.refs_7_ = bf16[2,64,768]{2,1,0:T(8,128)(2,1)S(1)} collective-permute-done((bf16[2,64,768]{2,1,0:T(8,128)(2,1)S(1)}, bf16[2,64,768]{2,1,0:T(8,128)(2,1)S(1)}, u32[]{:S(2)}, u32[]{:S(2)}) %collective-permute-start.38) | collective-permute-done | bytes 196640 | tf_op jit(solution)/shard_map/ppermute | solution.py:653
  194.6 9.9 %shard_map.228 = (f32[1536,768]{1,0:T(8,128)}, f32[8,128]{1,0:T(8,128)S(1)}) custom-call(bf16[8,256,1536]{2,1,0:T(8,128)(2,1)} %get-tuple-element.136.refs_0_, bf16[8,256,768]{2,1,0:T(8,128)(2,1)} %get-tuple-element.156.refs_1_, f32[8,128]{1,0:T(8,128)S(1)} %get-tuple-element.157.refs_2_, f32[8,128]{1,0:T(8,128)S(1)} %get-tuple-element.158.refs_3_, ...), custom_call_target="tpu_custom_call" | custom-call | flops 4831838208 | bytes 14155776 | tf_op jit(solution)/shard_map/pallas_call | solution.py:95
  211.9 4.7 %shard_map.230 = (f32[512,768]{1,0:T(8,128)}, bf16[512,768]{1,0:T(8,128)(2,1)S(1)}, bf16[512,384]{1,0:T(8,128)(2,1)S(1)}, bf16[512,384]{1,0:T(8,128)(2,1)}, f32[2,768]{1,0:T(2,128)S(1)}, /*index=5*/f32[8,128]{1,0:T(8,128)S(1)}) custom-call(bf16[512,768]{1,0:T(8,128)(2,1)S(1)} %get-tuple-element.160.refs_0_, ...), custom_call_target="tpu_custom_call" | custom-call | flops 603979776 | bytes 8275968 | tf_op jit(solution)/shard_map/pallas_call | solution.py:95
  226.2 5.5 %collective-permute-done.42.refs_9_ = bf16[512,384]{1,0:T(8,128)(2,1)} collective-permute-done((bf16[512,384]{1,0:T(8,128)(2,1)}, bf16[512,384]{1,0:T(8,128)(2,1)}, u32[]{:S(2)}, u32[]{:S(2)}) %collective-permute-start.42) | collective-permute-done | bytes 393248 | tf_op jit(solution)/shard_map/ppermute | solution.py:646
  231.7 20.0 %shard_map.235 = (bf16[3,1024,384]{2,1,0:T(8,128)(2,1)}, bf16[2,4,3,48,384]{4,3,2,1,0:T(8,128)(2,1)S(1)}, bf16[2,4,3,48,384]{4,3,2,1,0:T(8,128)(2,1)S(1)}, f32[4,768]{1,0:T(4,128)S(1)}) custom-call(s32[2]{0:T(128)S(1)} %pad_add_fusion.refs_0_, bf16[1024,1152]{1,0:T(8,128)(2,1)} %get-tuple-element.109.refs_1_.refs_2_.refs_3_, ...), custom_call_target="tpu_custom_call" | custom-call | flops 30000001024 | bytes 18249736 | tf_op jit(solution)/shard_map/pallas_call | solution.py:95
  254.1 7.4 %collective-permute-done.47.refs_6_ = f32[4,768]{1,0:T(4,128)S(1)} collective-permute-done((f32[4,768]{1,0:T(4,128)S(1)}, f32[4,768]{1,0:T(4,128)S(1)}, u32[]{:S(2)}, u32[]{:S(2)}) %collective-permute-start.47) | collective-permute-done | bytes 12320 | tf_op jit(solution)/shard_map/ppermute | solution.py:646
  263.3 5.6 %shard_map.237 = (bf16[512,768]{1,0:T(8,128)(2,1)}, f32[512,768]{1,0:T(8,128)S(1)}, f32[8,128]{1,0:T(8,128)S(1)}) custom-call(s32[2]{0:T(128)S(1)} %pad_add_fusion.refs_0_, bf16[3,1024,384]{2,1,0:T(8,128)(2,1)} %get-tuple-element.179.refs_1_, bf16[3,768,384]{2,1,0:T(8,128)(2,1)} %get-tuple-element.172.refs_11_.refs_2_, f32[8,128]{1,0:T(8,128)S(1)} %get-tuple-element.185.refs_3_), custom_call_target="tpu_custom_call" | custom-call | tf_op jit(solution)/shard_map/pallas_call | solution.py:95
  269.4 9.6 %shard_map.239 = (f32[768,1536]{1,0:T(8,128)}, f32[8,128]{1,0:T(8,128)S(1)}) custom-call(bf16[8,256,768]{2,1,0:T(8,128)(2,1)} %get-tuple-element.192.refs_0_, bf16[8,256,1536]{2,1,0:T(8,128)(2,1)} %get-tuple-element.193.refs_1_, f32[8,128]{1,0:T(8,128)S(1)} %get-tuple-element.194.refs_2_), custom_call_target="tpu_custom_call" | custom-call | tf_op jit(solution)/shard_map/pallas_call | solution.py:95
  (181 shorter events, 125.4 us)
Async XLA Ops:
  1.6 20.5 %collective-permute-start = (bf16[4,48,384]{2,1,0:T(8,128)(2,1)S(1)}, bf16[4,48,384]{2,1,0:T(8,128)(2,1)S(1)}, u32[]{:S(2)}, u32[]{:S(2)}) collective-permute-start(bf16[4,48,384]{2,1,0:T(8,128)(2,1)S(1)} %pad_maximum_fusion), channel_id=1, source_target_pairs={{0,4},{2,6},{4,0},{6,2},{8,12},{10,14},{12,8},{14,10},{16,20},{18,... | collective-permute-start | bytes 442376 | tf_op jit(solution)/shard_map/ppermute | solution.py:653
  9.0 18.5 %collective-permute-start.7 = (bf16[512,768]{1,0:T(8,128)(2,1)}, bf16[512,768]{1,0:T(8,128)(2,1)S(1)}, u32[]{:S(2)}, u32[]{:S(2)}) collective-permute-start(bf16[512,768]{1,0:T(8,128)(2,1)} %refs_3_.5), channel_id=1, source_target_pairs={{0,1},{1,0},{2,3},{3,2},{4,5},{5,4},{6,7},{7,6},{8,9},{9,8},{10,11... | collective-permute-start | bytes 2359304 | tf_op jit(solution)/shard_map/ppermute | solution.py:646
  29.6 37.2 %all-to-all-start = ((bf16[16,64,768]{2,1,0:T(8,128)(2,1)}), bf16[16,64,768]{2,1,0:T(8,128)(2,1)S(1)}, u32[]{:S(2)}, u32[]{:S(2)}) async-start(bf16[16,64,768]{2,1,0:T(8,128)(2,1)} %bitcast.60), calls=%async_computation | async-start | bytes 3145728 | tf_op jit(solution)/shard_map/all_to_all | solution.py:759
  44.1 24.5 %collective-permute-start.11 = (bf16[768,384]{1,0:T(8,128)(2,1)}, bf16[768,384]{1,0:T(8,128)(2,1)S(1)}, u32[]{:S(2)}, u32[]{:S(2)}) collective-permute-start(bf16[768,384]{1,0:T(8,128)(2,1)} %get-tuple-element.112.refs_2_.refs_5_), channel_id=1, source_target_pairs={{0,1},{1,0},{2,3},{3,2},{4,5},{5,4},{6,7},{7,6},{8,9},{9,8},{10,11... | collective-permute-start | bytes 1769480 | tf_op jit(solution)/shard_map/ppermute | solution.py:646
  66.7 57.2 %collective-permute-start.8 = (bf16[16,64,768]{2,1,0:T(8,128)(2,1)S(1)}, bf16[16,64,768]{2,1,0:T(8,128)(2,1)S(1)}, u32[]{:S(2)}, u32[]{:S(2)}) collective-permute-start(bf16[16,64,768]{2,1,0:T(8,128)(2,1)S(1)} %all-to-all-done.refs_4_.refs_3_), channel_id=1, source_target_pairs={{0,1},{1,0},{2,3},{3,2},{4,5},{5,4},{6,7},{7,6},{8,9},{9,8},{10,11... | collective-permute-start | bytes 4718600 | tf_op jit(solution)/shard_map/ppermute | solution.py:646
  85.5 19.0 %collective-permute-start.19 = (bf16[2,64,768]{2,1,0:T(8,128)(2,1)S(1)}, bf16[2,64,768]{2,1,0:T(8,128)(2,1)S(1)}, u32[]{:S(2)}, u32[]{:S(2)}) collective-permute-start(bf16[2,64,768]{2,1,0:T(8,128)(2,1)S(1)} %get-tuple-element.118), channel_id=1, source_target_pairs={{0,28},{2,30},{4,24},{6,26},{8,20},{10,22},{12,16},{14,18},{16,12}... | collective-permute-start | bytes 589832 | tf_op jit(solution)/shard_map/ppermute | solution.py:653
  90.0 27.8 %collective-permute-start.22 = (bf16[2,64,768]{2,1,0:T(8,128)(2,1)S(1)}, bf16[2,64,768]{2,1,0:T(8,128)(2,1)S(1)}, u32[]{:S(2)}, u32[]{:S(2)}) collective-permute-start(bf16[2,64,768]{2,1,0:T(8,128)(2,1)S(1)} %get-tuple-element.119), channel_id=1, source_target_pairs={{0,16},{2,18},{4,20},{6,22},{8,24},{10,26},{12,28},{14,30},{16,0},... | collective-permute-start | bytes 589832 | tf_op jit(solution)/shard_map/ppermute | solution.py:653
  92.7 28.6 %collective-permute-start.23 = (bf16[2,64,768]{2,1,0:T(8,128)(2,1)S(1)}, bf16[2,64,768]{2,1,0:T(8,128)(2,1)S(1)}, u32[]{:S(2)}, u32[]{:S(2)}) collective-permute-start(bf16[2,64,768]{2,1,0:T(8,128)(2,1)S(1)} %get-tuple-element.120), channel_id=1, source_target_pairs={{0,20},{2,22},{4,16},{6,18},{8,28},{10,30},{12,24},{14,26},{16,4},... | collective-permute-start | bytes 589832 | tf_op jit(solution)/shard_map/ppermute | solution.py:653
  98.5 23.3 %collective-permute-start.27 = (bf16[2,64,768]{2,1,0:T(8,128)(2,1)S(1)}, bf16[2,64,768]{2,1,0:T(8,128)(2,1)S(1)}, u32[]{:S(2)}, u32[]{:S(2)}) collective-permute-start(bf16[2,64,768]{2,1,0:T(8,128)(2,1)S(1)} %get-tuple-element.121.refs_4_.refs_5_), channel_id=1, source_target_pairs={{0,1},{1,0},{2,3},{3,2},{4,5},{5,4},{6,7},{7,6},{8,9},{9,8},{10,11... | collective-permute-start | bytes 589832 | tf_op jit(solution)/shard_map/ppermute | solution.py:646
  104.4 19.0 %collective-permute-start.28 = (bf16[2,64,768]{2,1,0:T(8,128)(2,1)S(1)}, bf16[2,64,768]{2,1,0:T(8,128)(2,1)S(1)}, u32[]{:S(2)}, u32[]{:S(2)}) collective-permute-start(bf16[2,64,768]{2,1,0:T(8,128)(2,1)S(1)} %collective-permute-done.26.refs_6_.refs_10_), channel_id=1, source_target_pairs={{0,1},{1,0},{2,3},{3,2},{4,5},{5,4},{6,7},{7,6},{8,9},{9,8},{10,11... | collective-permute-start | bytes 589832 | tf_op jit(solution)/shard_map/ppermute | solution.py:646
  121.9 18.3 %collective-permute-start.20 = (bf16[2,64,768]{2,1,0:T(8,128)(2,1)S(1)}, bf16[2,64,768]{2,1,0:T(8,128)(2,1)S(1)}, u32[]{:S(2)}, u32[]{:S(2)}) collective-permute-start(bf16[2,64,768]{2,1,0:T(8,128)(2,1)S(1)} %collective-permute-done.18.refs_15_.refs_5_), channel_id=1, source_target_pairs={{0,1},{1,0},{2,3},{3,2},{4,5},{5,4},{6,7},{7,6},{8,9},{9,8},{10,11... | collective-permute-start | bytes 589832 | tf_op jit(solution)/shard_map/ppermute | solution.py:646
  123.4 16.8 %collective-permute-start.21 = (bf16[2,64,768]{2,1,0:T(8,128)(2,1)S(1)}, bf16[2,64,768]{2,1,0:T(8,128)(2,1)S(1)}, u32[]{:S(2)}, u32[]{:S(2)}) collective-permute-start(bf16[2,64,768]{2,1,0:T(8,128)(2,1)S(1)} %collective-permute-done.19.refs_16_.refs_6_), channel_id=1, source_target_pairs={{0,1},{1,0},{2,3},{3,2},{4,5},{5,4},{6,7},{7,6},{8,9},{9,8},{10,11... | collective-permute-start | bytes 589832 | tf_op jit(solution)/shard_map/ppermute | solution.py:646
  123.9 24.6 %collective-permute-start.16 = (bf16[2,64,768]{2,1,0:T(8,128)(2,1)S(1)}, bf16[2,64,768]{2,1,0:T(8,128)(2,1)S(1)}, u32[]{:S(2)}, u32[]{:S(2)}) collective-permute-start(bf16[2,64,768]{2,1,0:T(8,128)(2,1)S(1)} %collective-permute-done.14.refs_11_.refs_5_), channel_id=1, source_target_pairs={{0,1},{1,0},{2,3},{3,2},{4,5},{5,4},{6,7},{7,6},{8,9},{9,8},{10,11... | collective-permute-start | bytes 589832 | tf_op jit(solution)/shard_map/ppermute | solution.py:646
  131.8 16.7 %collective-permute-start.17 = (bf16[2,64,768]{2,1,0:T(8,128)(2,1)S(1)}, bf16[2,64,768]{2,1,0:T(8,128)(2,1)S(1)}, u32[]{:S(2)}, u32[]{:S(2)}) collective-permute-start(bf16[2,64,768]{2,1,0:T(8,128)(2,1)S(1)} %collective-permute-done.15.refs_12_.refs_6_), channel_id=1, source_target_pairs={{0,1},{1,0},{2,3},{3,2},{4,5},{5,4},{6,7},{7,6},{8,9},{9,8},{10,11... | collective-permute-start | bytes 589832 | tf_op jit(solution)/shard_map/ppermute | solution.py:646
  138.7 33.5 %collective-permute-start.36 = (bf16[2,128,768]{2,1,0:T(8,128)(2,1)S(1)}, bf16[2,128,768]{2,1,0:T(8,128)(2,1)S(1)}, u32[]{:S(2)}, u32[]{:S(2)}) collective-permute-start(bf16[2,128,768]{2,1,0:T(8,128)(2,1)S(1)} %get-tuple-element.151), channel_id=1, source_target_pairs={{0,1},{1,0},{2,3},{3,2},{4,5},{5,4},{6,7},{7,6},{8,9},{9,8},{10,11... | collective-permute-start | bytes 1179656 | tf_op jit(solution)/shard_map/ppermute | solution.py:646
  146.5 16.4 %collective-permute-start.29 = (bf16[2,128,768]{2,1,0:T(8,128)(2,1)S(1)}, bf16[2,128,768]{2,1,0:T(8,128)(2,1)S(1)}, u32[]{:S(2)}, u32[]{:S(2)}) collective-permute-start(bf16[2,128,768]{2,1,0:T(8,128)(2,1)S(1)} %get-tuple-element.138), channel_id=1, source_target_pairs={{0,1},{1,0},{2,3},{3,2},{4,5},{5,4},{6,7},{7,6},{8,9},{9,8},{10,11... | collective-permute-start | bytes 1179656 | tf_op jit(solution)/shard_map/ppermute | solution.py:646
  147.0 29.2 %collective-permute-start.31 = (bf16[2,128,768]{2,1,0:T(8,128)(2,1)S(1)}, bf16[2,128,768]{2,1,0:T(8,128)(2,1)S(1)}, u32[]{:S(2)}, u32[]{:S(2)}) collective-permute-start(bf16[2,128,768]{2,1,0:T(8,128)(2,1)S(1)} %get-tuple-element.143), channel_id=1, source_target_pairs={{0,1},{1,0},{2,3},{3,2},{4,5},{5,4},{6,7},{7,6},{8,9},{9,8},{10,11... | collective-permute-start | bytes 1179656 | tf_op jit(solution)/shard_map/ppermute | solution.py:646
  154.8 25.0 %collective-permute-start.33 = (bf16[2,128,768]{2,1,0:T(8,128)(2,1)S(1)}, bf16[2,128,768]{2,1,0:T(8,128)(2,1)S(1)}, u32[]{:S(2)}, u32[]{:S(2)}) collective-permute-start(bf16[2,128,768]{2,1,0:T(8,128)(2,1)S(1)} %get-tuple-element.147), channel_id=1, source_target_pairs={{0,1},{1,0},{2,3},{3,2},{4,5},{5,4},{6,7},{7,6},{8,9},{9,8},{10,11... | collective-permute-start | bytes 1179656 | tf_op jit(solution)/shard_map/ppermute | solution.py:646
  171.6 40.2 %collective-permute-start.30 = (bf16[8,128,768]{2,1,0:T(8,128)(2,1)S(1)}, bf16[8,128,768]{2,1,0:T(8,128)(2,1)S(1)}, u32[]{:S(2)}, u32[]{:S(2)}) collective-permute-start(bf16[8,128,768]{2,1,0:T(8,128)(2,1)S(1)} %get-tuple-element.141), channel_id=1, source_target_pairs={{0,1},{1,0},{2,3},{3,2},{4,5},{5,4},{6,7},{7,6},{8,9},{9,8},{10,11... | collective-permute-start | bytes 4718600 | tf_op jit(solution)/shard_map/ppermute | solution.py:646
  179.8 24.7 %collective-permute-start.34 = (bf16[2,64,768]{2,1,0:T(8,128)(2,1)S(1)}, bf16[2,64,768]{2,1,0:T(8,128)(2,1)S(1)}, u32[]{:S(2)}, u32[]{:S(2)}) collective-permute-start(bf16[2,64,768]{2,1,0:T(8,128)(2,1)S(1)} %get-tuple-element.148), channel_id=1, source_target_pairs={{0,8},{2,10},{4,12},{6,14},{8,0},{10,2},{12,4},{14,6},{16,24},{18,... | collective-permute-start | bytes 589832 | tf_op jit(solution)/shard_map/ppermute | solution.py:653
  185.3 19.2 %collective-permute-start.35 = (bf16[2,64,768]{2,1,0:T(8,128)(2,1)S(1)}, bf16[2,64,768]{2,1,0:T(8,128)(2,1)S(1)}, u32[]{:S(2)}, u32[]{:S(2)}) collective-permute-start(bf16[2,64,768]{2,1,0:T(8,128)(2,1)S(1)} %get-tuple-element.149), channel_id=1, source_target_pairs={{0,12},{2,14},{4,8},{6,10},{8,4},{10,6},{12,0},{14,2},{16,28},{18,... | collective-permute-start | bytes 589832 | tf_op jit(solution)/shard_map/ppermute | solution.py:653
  222.3 56.8 %all-to-all-start.1 = ((bf16[16,64,768]{2,1,0:T(8,128)(2,1)}), bf16[16,64,768]{2,1,0:T(8,128)(2,1)S(1)}, u32[]{:S(2)}, u32[]{:S(2)}) async-start(bf16[16,64,768]{2,1,0:T(8,128)(2,1)} %get-tuple-element.164), calls=%async_computation.1 | async-start | bytes 3145728 | tf_op jit(solution)/shard_map/all_to_all | solution.py:905
  262.7 16.4 %collective-permute-start.50 = (bf16[800,384]{1,0:T(8,128)(2,1)}, bf16[800,384]{1,0:T(8,128)(2,1)}, u32[]{:S(2)}, u32[]{:S(2)}) collective-permute-start(bf16[800,384]{1,0:T(8,128)(2,1)} %get-tuple-element.190), channel_id=1, source_target_pairs={{0,4},{2,6},{4,0},{6,2},{8,12},{10,14},{12,8},{14,10},{16,20},{18,... | collective-permute-start | bytes 1843208 | tf_op jit(solution)/shard_map/ppermute | solution.py:653
  268.9 19.6 %collective-permute-start.49 = (bf16[512,768]{1,0:T(8,128)(2,1)}, bf16[512,768]{1,0:T(8,128)(2,1)}, u32[]{:S(2)}, u32[]{:S(2)}) collective-permute-start(bf16[512,768]{1,0:T(8,128)(2,1)} %get-tuple-element.187), channel_id=1, source_target_pairs={{0,1},{1,0},{2,3},{3,2},{4,5},{5,4},{6,7},{7,6},{8,9},{9,8},{10,11... | collective-permute-start | bytes 2359304 | tf_op jit(solution)/shard_map/ppermute | solution.py:646
  (51 other events, 548.4 us)

commit v3 on v2

--- a/solution.py
+++ b/solution.py
@@ -163,32 +163,36 @@
     ones = jnp.ones((rows, LANES), low)
     keys = jnp.concatenate([k_ref[...], member_ref[...]], axis=1)
     values = jnp.concatenate([v_ref[...], ones], axis=1)
-    causal = lax.broadcasted_iota(jnp.int32, (block, block), 1) <= lax.broadcasted_iota(
-        jnp.int32, (block, block), 0
-    )
+    row = lax.rem(lax.broadcasted_iota(jnp.int32, (2 * block, block), 0), block)
+    causal = lax.broadcasted_iota(jnp.int32, (2 * block, block), 1) <= row
     for start in range(0, rows, block):
         stop = start + block
         query = q_ref[start:stop] * HD**-0.5
+        zero = jnp.zeros_like(query)
         unreached = unreached_ref[start:stop]
-        halves = []
-        for own in (first_head, ~first_head):
-            left = jnp.concatenate([jnp.where(own, query, 0).astype(low), unreached], axis=1)
-            scores = dot(left, keys[:stop], NT)
-            near = jnp.where(causal, scores[:, start:], masked_score)
-            top = jnp.max(near, axis=1, keepdims=True)
-            if start:
-                far = scores[:, :start]
-                top = jnp.maximum(top, jnp.max(far, axis=1, keepdims=True))
-                weights = jnp.concatenate(
-                    [jnp.exp(far - top).astype(low), jnp.exp(near - top).astype(low)], axis=1
-                )
-            else:
-                weights = jnp.exp(near - top).astype(low)
-            sums = dot(weights, values[:stop], NN)
-            total = sums[:, LANES:]
-            halves.append((sums[:, :LANES] / total, top + jnp.log(total)))
-        out_ref[start:stop] = jnp.where(first_head, halves[0][0], halves[1][0]).astype(low)
-        total_ref[start:stop] = jnp.where(first_head, halves[0][1], halves[1][1])
+        left = jnp.concatenate(
+            [
+                jnp.concatenate([jnp.where(first_head, query, zero), unreached], axis=1),
+                jnp.concatenate([jnp.where(first_head, zero, query), unreached], axis=1),
+            ]
+        ).astype(low)
+        scores = dot(left, keys[:stop], NT)
+        near = jnp.where(causal, scores[:, start:], masked_score)
+        top = jnp.max(near, axis=1, keepdims=True)
+        if start:
+            far = scores[:, :start]
+            top = jnp.maximum(top, jnp.max(far, axis=1, keepdims=True))
+            weights = jnp.concatenate(
+                [jnp.exp(far - top).astype(low), jnp.exp(near - top).astype(low)], axis=1
+            )
+        else:
+            weights = jnp.exp(near - top).astype(low)
+        sums = dot(weights, values[:stop], NN)
+        total = sums[:, LANES:]
+        attended = sums[:, :LANES] / total
+        total = top + jnp.log(total)
+        out_ref[start:stop] = jnp.where(first_head, attended[:block], attended[block:]).astype(low)
+        total_ref[start:stop] = jnp.where(first_head, total[:block], total[block:])
     half = rows // 2
     keep_ref[...] = out_ref[pl.ds(pl.multiple_of(side * half, half), half)]
     give_ref[...] = out_ref[pl.ds(pl.multiple_of((1 - side) * half, half), half)]
@@ -519,8 +523,8 @@
 
 
 def middle_back_kernel(
-    own_ref, more_ref, middle_ref, ct_ref, scale_ref, weight_ref, other_ref,
-    grad_ref, branch_ref, mine_ref, give_ref, sums_ref,
+    chips, place_ref, own_ref, more_ref, middle_ref, ct_ref, scale_ref, weight_ref, other_ref, keep_ref, attended_ref,
+    grad_ref, mine_ref, give_ref, sums_ref, output_ref, output_give_ref, parts,
 ):
     grad_second = own_ref[...].astype(wide) + more_ref[...].astype(wide)
     hat, inverse = normalize(middle_ref[...])
@@ -529,25 +533,23 @@
     grad_middle = ct_ref[...].astype(wide) + norm_back(grad_second, hat, inverse, scale_ref[2:3])
     grad_ref[...] = grad_middle
     branch = grad_middle.astype(low)
-    branch_ref[...] = branch
     give_ref[...] = dot(branch, other_ref[...]).astype(low)
     mine_ref[...] = dot(branch, weight_ref[...]).astype(low)
 
-
-def output_part_kernel(chips, place_ref, branch_ref, keep_ref, more_ref, own_ref, give_ref, parts):
     place = place_ref[0]
-    parts[0] = dot(branch_ref[...], keep_ref[...], TN)
-    parts[1] = dot(branch_ref[...], more_ref[...], TN)
+    turned = branch.astype(wide).T.astype(low)
+    parts[0] = dot(turned, keep_ref[...])
+    parts[1] = dot(turned, attended_ref[...])
     if chips:
-        rows = own_ref.shape[2]
+        rows = output_ref.shape[2]
         for k in range(chips):
             block = pl.ds(pl.multiple_of((place ^ (2 * k)) * rows, rows), rows)
-            own_ref[:, k] = parts[:, block]
+            output_ref[:, k] = parts[:, block]
             block = pl.ds(pl.multiple_of((place ^ (2 * k + 1)) * rows, rows), rows)
-            give_ref[:, k] = parts[:, block].astype(low)
+            output_give_ref[:, k] = parts[:, block].astype(low)
     else:
-        own_ref[...] = parts[0]
-        give_ref[...] = parts[1].astype(low)
+        output_ref[...] = parts[0]
+        output_give_ref[...] = parts[1].astype(low)
 
 
 def output_sum_kernel(own_ref, more_ref, keep_ref, give_ref):
@@ -621,7 +623,7 @@
 
 
 def total_kernel(own_ref, sums_ref, *refs):
-    aways, (in_ref, out_ref, out_sums_ref) = refs[:-3], refs[-3:]
+    aways, (in_ref, out_ref), sums_refs = refs[:-6], refs[-6:-4], refs[-4:]
     rows = out_ref.shape[0]
     sums = [sums_ref[...]]
     total = own_ref[...]
@@ -630,7 +632,8 @@
         sums.append(gathered(ref[own_ref.shape[0] :]))
     while len(sums) > 1:
         sums = [x + y for x, y in zip(sums[0::2], sums[1::2])]
-    out_sums_ref[...] = sums[0]
+    for n, ref in enumerate(sums_refs):
+        ref[...] = sums[0][n : n + 1].reshape(ref.shape)
     for n in range(3):
         in_ref[n] = total[n * rows : (n + 1) * rows]
     out_ref[...] = total[3 * rows :]
@@ -877,22 +880,28 @@
         flops=4 * own_count * own_count * width,
     )
     sibling_part = swapped(sibling_part, 1)
-    grad_middle, grad_branch, grad_mine, grad_give, second_sums, middle_done = run(
-        middle_back_kernel,
+    if in_kernel:
+        blocks = (2, chips, shard_rows, local_width)
+        output_outs = [array(blocks, wide), array(blocks, low)]
+    else:
+        output_outs = [array((width, local_width), wide), array((width, local_width), low)]
+    grad_middle, grad_mine, grad_give, second_sums, output_own, output_give, middle_done = run(
+        functools.partial(middle_back_kernel, chips if in_kernel else 0),
         (
-            own_part, sibling_part, Far(middle), Far(cotangent), scales,
-            Far(out_weight), Far(other_out_weight),
+            place, own_part, sibling_part, Far(middle), Far(cotangent), scales,
+            Far(out_weight), Far(other_out_weight), Far(attended_keep), Far(attended_more),
         ),
         [
             kept((own_count, width), wide),
-            array((own_count, width), low),
             array((own_count, local_width), low),
             array((own_count, local_width), low),
             array((2, width), wide),
+            *output_outs,
         ],
         first=(ffn_more,),
         mark=True,
-        flops=2 * own_count * width * width,
+        scratch_shapes=[pltpu.VMEM((2, width, local_width), wide)],
+        flops=4 * own_count * width * width,
     )
     grad_more = across(grad_give)
     ffn_sums, sums_done = run(
@@ -904,18 +913,6 @@
     )
     ffn_back = lax.all_to_all(ffn_sums, "fsdp", 0, 0, tiled=True)
 
-    if in_kernel:
-        blocks = (2, chips, shard_rows, local_width)
-        outs = [array(blocks, wide), array(blocks, low)]
-    else:
-        outs = [array((width, local_width), wide), array((width, local_width), low)]
-    output_own, output_give = run(
-        functools.partial(output_part_kernel, chips if in_kernel else 0),
-        (place, grad_branch, Far(attended_keep), Far(attended_more)),
-        outs,
-        scratch_shapes=[pltpu.VMEM((2, width, local_width), wide)],
-        flops=2 * own_count * width * width,
-    )
     if in_kernel:
         output_own, output_give, output_done = run(
             output_sum_kernel,
@@ -1008,13 +1005,13 @@
         flops=2 * own_count * slot_count * width,
     )
     if in_kernel:
-        input_weight_grad, output_weight_grad, norm_sums = run(
+        input_weight_grad, output_weight_grad, *norm_sums = run(
             total_kernel,
             (own_sum, norm_sums, *away),
             [
                 array((3, shard_rows, local_width), wide),
                 array((shard_rows, local_width), wide),
-                array((4, width), wide),
+                *[array((width,), wide)] * 4,
             ],
             first=(input_done, out_done),
         )

time: 303 us -> 300 us (0.990)
    pallas_call x29 -> x28, Pallas kernels: 129 us -> 126 us  [run(): pl.pallas_call(whole, out_shape=outs, compiler_params=pltpu.CompilerParam...]
where the time goes in v3:
time: 300 us; the launch traced here: 297 us
  Pallas kernels  126 us (42%)
  waiting for transfers between devices  82 us (27%)
  starting transfers between devices  73.6 us (25%)
  local copies, waits for them, and re-layouts  5.83 us (2%)
  other arithmetic  4.41 us (1%)
  matrix products  3.21 us (1%)
    pallas_call x28, Pallas kernels, run(): pl.pallas_call(whole, out_shape=outs, compiler_params=pltpu.CompilerParam...  126 us
    ppermute x32, starting transfers between devices, swapped(): return lax.ppermute(values, 'fsdp', [(i, i ^ offset) for i in range(count)])  45.5 us
    ppermute x32, waiting for transfers between devices, swapped(): return lax.ppermute(values, 'fsdp', [(i, i ^ offset) for i in range(count)])  40.7 us
    ppermute x21, waiting for transfers between devices, across(): return lax.ppermute(values, 'tp', [(0, 1), (1, 0)])  29.7 us
    ppermute x21, starting transfers between devices, across(): return lax.ppermute(values, 'tp', [(0, 1), (1, 0)])  19 us
    all_to_all x1, waiting for transfers between devices, shards(): lax.all_to_all(packed_grads.reshape(experts_in_all, capacity, width), 'fs...  11.5 us
  transfers between devices with their start and end apart: 56, of which 21 were waited for; matrix products, arithmetic and copies ran while one was open for 4% of the time, Pallas kernels for 40%

profile of v3, /device:TPU:0, one launch (start us, length us, event | category | flops | bytes accessed | tf_op | source)
XLA Modules:
  0.0 296.8 jit_solution(9798637116677063869)
XLA Ops:
  15.9 4.1 %collective-permute-done.3 = bf16[4,48,384]{2,1,0:T(8,128)(2,1)S(1)} collective-permute-done((bf16[4,48,384]{2,1,0:T(8,128)(2,1)S(1)}, bf16[4,48,384]{2,1,0:T(8,128)(2,1)S(1)}, u32[]{:S(2)}, u32[]{:S(2)}) %collective-permute-start.3) | collective-permute-done | bytes 147488 | tf_op jit(solution)/shard_map/ppermute | solution.py:656
  29.6 5.2 %all-to-all-start = ((bf16[16,64,768]{2,1,0:T(8,128)(2,1)}), bf16[16,64,768]{2,1,0:T(8,128)(2,1)S(1)}, u32[]{:S(2)}, u32[]{:S(2)}) async-start(bf16[16,64,768]{2,1,0:T(8,128)(2,1)} %bitcast.60), calls=%async_computation | async-start | bytes 3145728 | tf_op jit(solution)/shard_map/all_to_all | solution.py:762
  37.8 6.3 %shard_map.214 = (bf16[3,768,384]{2,1,0:T(8,128)(2,1)}, bf16[768,384]{1,0:T(8,128)(2,1)}, bf16[1024,1152]{1,0:T(8,128)(2,1)}, f32[4,768]{1,0:T(4,128)S(1)}) custom-call(s32[2]{0:T(128)S(1)} %pad_add_fusion.refs_0_, bf16[512,768]{1,0:T(8,128)(2,1)S(1)} %copy-done.2, bf16[512,768]{1,0:T(8,128)(2,1)S(1)} %collective-permute-done.7.refs_3_.refs_2_, ...), custom_call_target="tpu_custom_call" | custom-call | flops 1811939328 | bytes 8675336 | tf_op jit(solution)/shard_map/pallas_call | solution.py:95
  45.6 9.1 %shard_map.215 = (bf16[1024,384]{1,0:T(8,128)(2,1)}, f32[1024,384]{1,0:T(8,128)}, bf16[512,384]{1,0:T(8,128)(2,1)S(1)}, bf16[512,384]{1,0:T(8,128)(2,1)}) custom-call(s32[2]{0:T(128)S(1)} %pad_add_fusion.refs_0_, bf16[1024,1152]{1,0:T(8,128)(2,1)} %get-tuple-element.111.refs_1_.refs_2_.refs_3_, ...), custom_call_target="tpu_custom_call" | custom-call | flops 12000000000 | bytes 10747912 | tf_op jit(solution)/shard_map/pallas_call | solution.py:95
  55.3 11.5 %all-to-all-done.refs_4_.refs_3_ = bf16[16,64,768]{2,1,0:T(8,128)(2,1)S(1)} async-done(((bf16[16,64,768]{2,1,0:T(8,128)(2,1)}), bf16[16,64,768]{2,1,0:T(8,128)(2,1)S(1)}, u32[]{:S(2)}, u32[]{:S(2)}) %all-to-all-start) | async-done | bytes 1572896 | tf_op jit(solution)/shard_map/all_to_all | solution.py:762
  78.1 4.6 %collective-permute-start.14 = (bf16[2,64,768]{2,1,0:T(8,128)(2,1)S(1)}, bf16[2,64,768]{2,1,0:T(8,128)(2,1)S(1)}, u32[]{:S(2)}, u32[]{:S(2)}) collective-permute-start(bf16[2,64,768]{2,1,0:T(8,128)(2,1)S(1)} %get-tuple-element.117), channel_id=1, source_target_pairs={{0,8},{2,10},{4,12},{6,14},{8,0},{10,2},{12,4},{14,6},{16,24},{18,... | collective-permute-start | bytes 589832 | tf_op jit(solution)/shard_map/ppermute | solution.py:656
  85.5 4.5 %collective-permute-start.19 = (bf16[2,64,768]{2,1,0:T(8,128)(2,1)S(1)}, bf16[2,64,768]{2,1,0:T(8,128)(2,1)S(1)}, u32[]{:S(2)}, u32[]{:S(2)}) collective-permute-start(bf16[2,64,768]{2,1,0:T(8,128)(2,1)S(1)} %get-tuple-element.120), channel_id=1, source_target_pairs={{0,28},{2,30},{4,24},{6,26},{8,20},{10,22},{12,16},{14,18},{16,12}... | collective-permute-start | bytes 589832 | tf_op jit(solution)/shard_map/ppermute | solution.py:656
  99.0 5.4 %collective-permute-done.19.refs_16_.refs_6_ = bf16[2,64,768]{2,1,0:T(8,128)(2,1)S(1)} collective-permute-done((bf16[2,64,768]{2,1,0:T(8,128)(2,1)S(1)}, bf16[2,64,768]{2,1,0:T(8,128)(2,1)S(1)}, u32[]{:S(2)}, u32[]{:S(2)}) %collective-permute-start.19) | collective-permute-done | bytes 196640 | tf_op jit(solution)/shard_map/ppermute | solution.py:656
  108.8 8.9 %collective-permute-done.22.refs_13_.refs_5_ = bf16[2,64,768]{2,1,0:T(8,128)(2,1)S(1)} collective-permute-done((bf16[2,64,768]{2,1,0:T(8,128)(2,1)S(1)}, bf16[2,64,768]{2,1,0:T(8,128)(2,1)S(1)}, u32[]{:S(2)}, u32[]{:S(2)}) %collective-permute-start.22) | collective-permute-done | bytes 196640 | tf_op jit(solution)/shard_map/ppermute | solution.py:656
  125.4 6.4 %shard_map.219 = (bf16[8,256,768]{2,1,0:T(8,128)(2,1)}, bf16[8,256,768]{2,1,0:T(8,128)(2,1)}, bf16[8,256,1536]{2,1,0:T(8,128)(2,1)}, bf16[8,256,1536]{2,1,0:T(8,...) custom-call(s32[2]{0:T(128)S(1)} %pad_add_fusion.refs_0_, bf16[768,1536]{1,0:T(8,128)(2,1)S(1)} %bitcast.50, ...), custom_call_target="tpu_custom_call" | custom-call | flops 3623878656 | bytes 28704776 | tf_op jit(solution)/shard_map/pallas_call | solution.py:95
  132.4 6.2 %shard_map.220 = (bf16[8,256,768]{2,1,0:T(8,128)(2,1)}, bf16[8,256,768]{2,1,0:T(8,128)(2,1)}, bf16[8,256,1536]{2,1,0:T(8,128)(2,1)}, bf16[8,256,1536]{2,1,0:T(8,...) custom-call(s32[2]{0:T(128)S(1)} %pad_add_fusion.refs_0_, ...), custom_call_target="tpu_custom_call", output_to_operand_aliasing={{0}: (9, {}), {1}: (10, {}), {2}: (11, {}), {3}: (12, {})} | custom-call | flops 3623878656 | bytes 47579144 | tf_op jit(solution)/shard_map/pallas_call | solution.py:95
  140.2 6.3 %shard_map.221 = (bf16[8,256,768]{2,1,0:T(8,128)(2,1)}, bf16[8,256,768]{2,1,0:T(8,128)(2,1)}, bf16[8,256,1536]{2,1,0:T(8,128)(2,1)}, bf16[8,256,1536]{2,1,0:T(8,...) custom-call(s32[2]{0:T(128)S(1)} %pad_add_fusion.refs_0_, ...), custom_call_target="tpu_custom_call", output_to_operand_aliasing={{0}: (9, {}), {1}: (10, {}), {2}: (11, {}), {3}: (12, {})} | custom-call | flops 3623878656 | bytes 47579144 | tf_op jit(solution)/shard_map/pallas_call | solution.py:95
  148.5 6.3 %shard_map.222 = (bf16[8,256,768]{2,1,0:T(8,128)(2,1)}, bf16[8,256,768]{2,1,0:T(8,128)(2,1)}, bf16[8,256,1536]{2,1,0:T(8,128)(2,1)}, bf16[8,256,1536]{2,1,0:T(8,...) custom-call(s32[2]{0:T(128)S(1)} %pad_add_fusion.refs_0_, ...), custom_call_target="tpu_custom_call", output_to_operand_aliasing={{0}: (9, {}), {1}: (10, {}), {2}: (11, {}), {3}: (12, {})} | custom-call | flops 3623878656 | bytes 47579144 | tf_op jit(solution)/shard_map/pallas_call | solution.py:95
  155.3 7.6 %collective-permute-done.29.refs_1_ = bf16[2,128,768]{2,1,0:T(8,128)(2,1)S(1)} collective-permute-done((bf16[2,128,768]{2,1,0:T(8,128)(2,1)S(1)}, bf16[2,128,768]{2,1,0:T(8,128)(2,1)S(1)}, u32[]{:S(2)}, u32[]{:S(2)}) %collective-permute-start.29) | collective-permute-done | bytes 393248 | tf_op jit(solution)/shard_map/ppermute | solution.py:649
  163.0 8.7 %shard_map.224 = (f32[8,128,768]{2,1,0:T(8,128)S(1)}, bf16[8,128,768]{2,1,0:T(8,128)(2,1)S(1)}, f32[8,128]{1,0:T(8,128)S(1)}) custom-call(bf16[8,256,1536]{2,1,0:T(8,128)(2,1)} %get-tuple-element.138.refs_0_, bf16[1536,768]{1,0:T(8,128)(2,1)S(1)} %bitcast.49, f32[8,128]{1,0:T(8,128)S(1)} %get-tuple-element.141.refs_2_), custom_call_target="tpu_custom_call" | custom-call | tf_op jit(solution)/shard_map/pallas_call | solution.py:95
  181.2 4.1 %collective-permute-done.37.refs_6_ = bf16[2,64,768]{2,1,0:T(8,128)(2,1)S(1)} collective-permute-done((bf16[2,64,768]{2,1,0:T(8,128)(2,1)S(1)}, bf16[2,64,768]{2,1,0:T(8,128)(2,1)S(1)}, u32[]{:S(2)}, u32[]{:S(2)}) %collective-permute-start.37) | collective-permute-done | bytes 196640 | tf_op jit(solution)/shard_map/ppermute | solution.py:656
  185.3 4.6 %collective-permute-done.38.refs_7_ = bf16[2,64,768]{2,1,0:T(8,128)(2,1)S(1)} collective-permute-done((bf16[2,64,768]{2,1,0:T(8,128)(2,1)S(1)}, bf16[2,64,768]{2,1,0:T(8,128)(2,1)S(1)}, u32[]{:S(2)}, u32[]{:S(2)}) %collective-permute-start.38) | collective-permute-done | bytes 196640 | tf_op jit(solution)/shard_map/ppermute | solution.py:656
  194.6 9.9 %shard_map.228 = (f32[1536,768]{1,0:T(8,128)}, f32[8,128]{1,0:T(8,128)S(1)}) custom-call(bf16[8,256,1536]{2,1,0:T(8,128)(2,1)} %get-tuple-element.138.refs_0_, bf16[8,256,768]{2,1,0:T(8,128)(2,1)} %get-tuple-element.158.refs_1_, f32[8,128]{1,0:T(8,128)S(1)} %get-tuple-element.159.refs_2_, f32[8,128]{1,0:T(8,128)S(1)} %get-tuple-element.160.refs_3_, ...), custom_call_target="tpu_custom_call" | custom-call | flops 4831838208 | bytes 14155776 | tf_op jit(solution)/shard_map/pallas_call | solution.py:95
  211.9 6.1 %shard_map.230 = (f32[512,768]{1,0:T(8,128)}, bf16[512,384]{1,0:T(8,128)(2,1)S(1)}, bf16[512,384]{1,0:T(8,128)(2,1)}, f32[2,768]{1,0:T(2,128)S(1)}, f32[2,8,48,3...) custom-call(s32[2]{0:T(128)S(1)} %pad_add_fusion.refs_0_, ...), custom_call_target="tpu_custom_call" | custom-call | flops 1207959552 | bytes 10045448 | tf_op jit(solution)/shard_map/pallas_call | solution.py:95
  224.5 5.4 %collective-permute-done.42.refs_9_ = bf16[512,384]{1,0:T(8,128)(2,1)} collective-permute-done((bf16[512,384]{1,0:T(8,128)(2,1)}, bf16[512,384]{1,0:T(8,128)(2,1)}, u32[]{:S(2)}, u32[]{:S(2)}) %collective-permute-start.42) | collective-permute-done | bytes 393248 | tf_op jit(solution)/shard_map/ppermute | solution.py:649
  229.9 20.0 %shard_map.234 = (bf16[3,1024,384]{2,1,0:T(8,128)(2,1)}, bf16[2,4,3,48,384]{4,3,2,1,0:T(8,128)(2,1)S(1)}, bf16[2,4,3,48,384]{4,3,2,1,0:T(8,128)(2,1)S(1)}, f32[4,768]{1,0:T(4,128)S(1)}) custom-call(s32[2]{0:T(128)S(1)} %pad_add_fusion.refs_0_, bf16[1024,1152]{1,0:T(8,128)(2,1)} %get-tuple-element.111.refs_1_.refs_2_.refs_3_, ...), custom_call_target="tpu_custom_call" | custom-call | flops 30000001024 | bytes 18249736 | tf_op jit(solution)/shard_map/pallas_call | solution.py:95
  252.3 7.4 %collective-permute-done.47.refs_6_ = f32[4,768]{1,0:T(4,128)S(1)} collective-permute-done((f32[4,768]{1,0:T(4,128)S(1)}, f32[4,768]{1,0:T(4,128)S(1)}, u32[]{:S(2)}, u32[]{:S(2)}) %collective-permute-start.47) | collective-permute-done | bytes 12320 | tf_op jit(solution)/shard_map/ppermute | solution.py:649
  261.5 5.6 %shard_map.236 = (bf16[512,768]{1,0:T(8,128)(2,1)}, f32[512,768]{1,0:T(8,128)S(1)}, f32[8,128]{1,0:T(8,128)S(1)}) custom-call(s32[2]{0:T(128)S(1)} %pad_add_fusion.refs_0_, bf16[3,1024,384]{2,1,0:T(8,128)(2,1)} %get-tuple-element.180.refs_1_, bf16[3,768,384]{2,1,0:T(8,128)(2,1)} %get-tuple-element.174.refs_11_.refs_2_, f32[8,128]{1,0:T(8,128)S(1)} %get-tuple-element.186.refs_3_), custom_call_target="tpu_custom_call" | custom-call | tf_op jit(solution)/shard_map/pallas_call | solution.py:95
  267.6 9.6 %shard_map.238 = (f32[768,1536]{1,0:T(8,128)}, f32[8,128]{1,0:T(8,128)S(1)}) custom-call(bf16[8,256,768]{2,1,0:T(8,128)(2,1)} %get-tuple-element.193.refs_0_, bf16[8,256,1536]{2,1,0:T(8,128)(2,1)} %get-tuple-element.194.refs_1_, f32[8,128]{1,0:T(8,128)S(1)} %get-tuple-element.195.refs_2_), custom_call_target="tpu_custom_call" | custom-call | tf_op jit(solution)/shard_map/pallas_call | solution.py:95
  (179 shorter events, 121.7 us)
Async XLA Ops:
  1.6 20.5 %collective-permute-start = (bf16[4,48,384]{2,1,0:T(8,128)(2,1)S(1)}, bf16[4,48,384]{2,1,0:T(8,128)(2,1)S(1)}, u32[]{:S(2)}, u32[]{:S(2)}) collective-permute-start(bf16[4,48,384]{2,1,0:T(8,128)(2,1)S(1)} %pad_maximum_fusion), channel_id=1, source_target_pairs={{0,4},{2,6},{4,0},{6,2},{8,12},{10,14},{12,8},{14,10},{16,20},{18,... | collective-permute-start | bytes 442376 | tf_op jit(solution)/shard_map/ppermute | solution.py:656
  9.0 18.5 %collective-permute-start.7 = (bf16[512,768]{1,0:T(8,128)(2,1)}, bf16[512,768]{1,0:T(8,128)(2,1)S(1)}, u32[]{:S(2)}, u32[]{:S(2)}) collective-permute-start(bf16[512,768]{1,0:T(8,128)(2,1)} %refs_3_.3), channel_id=1, source_target_pairs={{0,1},{1,0},{2,3},{3,2},{4,5},{5,4},{6,7},{7,6},{8,9},{9,8},{10,11... | collective-permute-start | bytes 2359304 | tf_op jit(solution)/shard_map/ppermute | solution.py:649
  29.6 37.2 %all-to-all-start = ((bf16[16,64,768]{2,1,0:T(8,128)(2,1)}), bf16[16,64,768]{2,1,0:T(8,128)(2,1)S(1)}, u32[]{:S(2)}, u32[]{:S(2)}) async-start(bf16[16,64,768]{2,1,0:T(8,128)(2,1)} %bitcast.60), calls=%async_computation | async-start | bytes 3145728 | tf_op jit(solution)/shard_map/all_to_all | solution.py:762
  44.1 24.5 %collective-permute-start.11 = (bf16[768,384]{1,0:T(8,128)(2,1)}, bf16[768,384]{1,0:T(8,128)(2,1)S(1)}, u32[]{:S(2)}, u32[]{:S(2)}) collective-permute-start(bf16[768,384]{1,0:T(8,128)(2,1)} %get-tuple-element.114.refs_2_.refs_6_), channel_id=1, source_target_pairs={{0,1},{1,0},{2,3},{3,2},{4,5},{5,4},{6,7},{7,6},{8,9},{9,8},{10,11... | collective-permute-start | bytes 1769480 | tf_op jit(solution)/shard_map/ppermute | solution.py:649
  66.7 57.2 %collective-permute-start.8 = (bf16[16,64,768]{2,1,0:T(8,128)(2,1)S(1)}, bf16[16,64,768]{2,1,0:T(8,128)(2,1)S(1)}, u32[]{:S(2)}, u32[]{:S(2)}) collective-permute-start(bf16[16,64,768]{2,1,0:T(8,128)(2,1)S(1)} %all-to-all-done.refs_4_.refs_3_), channel_id=1, source_target_pairs={{0,1},{1,0},{2,3},{3,2},{4,5},{5,4},{6,7},{7,6},{8,9},{9,8},{10,11... | collective-permute-start | bytes 4718600 | tf_op jit(solution)/shard_map/ppermute | solution.py:649
  85.5 19.0 %collective-permute-start.19 = (bf16[2,64,768]{2,1,0:T(8,128)(2,1)S(1)}, bf16[2,64,768]{2,1,0:T(8,128)(2,1)S(1)}, u32[]{:S(2)}, u32[]{:S(2)}) collective-permute-start(bf16[2,64,768]{2,1,0:T(8,128)(2,1)S(1)} %get-tuple-element.120), channel_id=1, source_target_pairs={{0,28},{2,30},{4,24},{6,26},{8,20},{10,22},{12,16},{14,18},{16,12}... | collective-permute-start | bytes 589832 | tf_op jit(solution)/shard_map/ppermute | solution.py:656
  89.9 27.8 %collective-permute-start.22 = (bf16[2,64,768]{2,1,0:T(8,128)(2,1)S(1)}, bf16[2,64,768]{2,1,0:T(8,128)(2,1)S(1)}, u32[]{:S(2)}, u32[]{:S(2)}) collective-permute-start(bf16[2,64,768]{2,1,0:T(8,128)(2,1)S(1)} %get-tuple-element.121), channel_id=1, source_target_pairs={{0,16},{2,18},{4,20},{6,22},{8,24},{10,26},{12,28},{14,30},{16,0},... | collective-permute-start | bytes 589832 | tf_op jit(solution)/shard_map/ppermute | solution.py:656
  92.7 28.6 %collective-permute-start.23 = (bf16[2,64,768]{2,1,0:T(8,128)(2,1)S(1)}, bf16[2,64,768]{2,1,0:T(8,128)(2,1)S(1)}, u32[]{:S(2)}, u32[]{:S(2)}) collective-permute-start(bf16[2,64,768]{2,1,0:T(8,128)(2,1)S(1)} %get-tuple-element.122), channel_id=1, source_target_pairs={{0,20},{2,22},{4,16},{6,18},{8,28},{10,30},{12,24},{14,26},{16,4},... | collective-permute-start | bytes 589832 | tf_op jit(solution)/shard_map/ppermute | solution.py:656
  98.5 23.3 %collective-permute-start.27 = (bf16[2,64,768]{2,1,0:T(8,128)(2,1)S(1)}, bf16[2,64,768]{2,1,0:T(8,128)(2,1)S(1)}, u32[]{:S(2)}, u32[]{:S(2)}) collective-permute-start(bf16[2,64,768]{2,1,0:T(8,128)(2,1)S(1)} %get-tuple-element.123.refs_4_.refs_5_), channel_id=1, source_target_pairs={{0,1},{1,0},{2,3},{3,2},{4,5},{5,4},{6,7},{7,6},{8,9},{9,8},{10,11... | collective-permute-start | bytes 589832 | tf_op jit(solution)/shard_map/ppermute | solution.py:649
  104.4 19.0 %collective-permute-start.28 = (bf16[2,64,768]{2,1,0:T(8,128)(2,1)S(1)}, bf16[2,64,768]{2,1,0:T(8,128)(2,1)S(1)}, u32[]{:S(2)}, u32[]{:S(2)}) collective-permute-start(bf16[2,64,768]{2,1,0:T(8,128)(2,1)S(1)} %collective-permute-done.26.refs_6_.refs_10_), channel_id=1, source_target_pairs={{0,1},{1,0},{2,3},{3,2},{4,5},{5,4},{6,7},{7,6},{8,9},{9,8},{10,11... | collective-permute-start | bytes 589832 | tf_op jit(solution)/shard_map/ppermute | solution.py:649
  121.9 18.3 %collective-permute-start.20 = (bf16[2,64,768]{2,1,0:T(8,128)(2,1)S(1)}, bf16[2,64,768]{2,1,0:T(8,128)(2,1)S(1)}, u32[]{:S(2)}, u32[]{:S(2)}) collective-permute-start(bf16[2,64,768]{2,1,0:T(8,128)(2,1)S(1)} %collective-permute-done.18.refs_15_.refs_5_), channel_id=1, source_target_pairs={{0,1},{1,0},{2,3},{3,2},{4,5},{5,4},{6,7},{7,6},{8,9},{9,8},{10,11... | collective-permute-start | bytes 589832 | tf_op jit(solution)/shard_map/ppermute | solution.py:649
  123.4 16.8 %collective-permute-start.21 = (bf16[2,64,768]{2,1,0:T(8,128)(2,1)S(1)}, bf16[2,64,768]{2,1,0:T(8,128)(2,1)S(1)}, u32[]{:S(2)}, u32[]{:S(2)}) collective-permute-start(bf16[2,64,768]{2,1,0:T(8,128)(2,1)S(1)} %collective-permute-done.19.refs_16_.refs_6_), channel_id=1, source_target_pairs={{0,1},{1,0},{2,3},{3,2},{4,5},{5,4},{6,7},{7,6},{8,9},{9,8},{10,11... | collective-permute-start | bytes 589832 | tf_op jit(solution)/shard_map/ppermute | solution.py:649
  123.9 24.6 %collective-permute-start.16 = (bf16[2,64,768]{2,1,0:T(8,128)(2,1)S(1)}, bf16[2,64,768]{2,1,0:T(8,128)(2,1)S(1)}, u32[]{:S(2)}, u32[]{:S(2)}) collective-permute-start(bf16[2,64,768]{2,1,0:T(8,128)(2,1)S(1)} %collective-permute-done.14.refs_11_.refs_5_), channel_id=1, source_target_pairs={{0,1},{1,0},{2,3},{3,2},{4,5},{5,4},{6,7},{7,6},{8,9},{9,8},{10,11... | collective-permute-start | bytes 589832 | tf_op jit(solution)/shard_map/ppermute | solution.py:649
  131.8 16.7 %collective-permute-start.17 = (bf16[2,64,768]{2,1,0:T(8,128)(2,1)S(1)}, bf16[2,64,768]{2,1,0:T(8,128)(2,1)S(1)}, u32[]{:S(2)}, u32[]{:S(2)}) collective-permute-start(bf16[2,64,768]{2,1,0:T(8,128)(2,1)S(1)} %collective-permute-done.15.refs_12_.refs_6_), channel_id=1, source_target_pairs={{0,1},{1,0},{2,3},{3,2},{4,5},{5,4},{6,7},{7,6},{8,9},{9,8},{10,11... | collective-permute-start | bytes 589832 | tf_op jit(solution)/shard_map/ppermute | solution.py:649
  138.7 33.5 %collective-permute-start.36 = (bf16[2,128,768]{2,1,0:T(8,128)(2,1)S(1)}, bf16[2,128,768]{2,1,0:T(8,128)(2,1)S(1)}, u32[]{:S(2)}, u32[]{:S(2)}) collective-permute-start(bf16[2,128,768]{2,1,0:T(8,128)(2,1)S(1)} %get-tuple-element.153), channel_id=1, source_target_pairs={{0,1},{1,0},{2,3},{3,2},{4,5},{5,4},{6,7},{7,6},{8,9},{9,8},{10,11... | collective-permute-start | bytes 1179656 | tf_op jit(solution)/shard_map/ppermute | solution.py:649
  146.4 16.4 %collective-permute-start.29 = (bf16[2,128,768]{2,1,0:T(8,128)(2,1)S(1)}, bf16[2,128,768]{2,1,0:T(8,128)(2,1)S(1)}, u32[]{:S(2)}, u32[]{:S(2)}) collective-permute-start(bf16[2,128,768]{2,1,0:T(8,128)(2,1)S(1)} %get-tuple-element.140), channel_id=1, source_target_pairs={{0,1},{1,0},{2,3},{3,2},{4,5},{5,4},{6,7},{7,6},{8,9},{9,8},{10,11... | collective-permute-start | bytes 1179656 | tf_op jit(solution)/shard_map/ppermute | solution.py:649
  147.0 29.2 %collective-permute-start.31 = (bf16[2,128,768]{2,1,0:T(8,128)(2,1)S(1)}, bf16[2,128,768]{2,1,0:T(8,128)(2,1)S(1)}, u32[]{:S(2)}, u32[]{:S(2)}) collective-permute-start(bf16[2,128,768]{2,1,0:T(8,128)(2,1)S(1)} %get-tuple-element.145), channel_id=1, source_target_pairs={{0,1},{1,0},{2,3},{3,2},{4,5},{5,4},{6,7},{7,6},{8,9},{9,8},{10,11... | collective-permute-start | bytes 1179656 | tf_op jit(solution)/shard_map/ppermute | solution.py:649
  154.8 25.0 %collective-permute-start.33 = (bf16[2,128,768]{2,1,0:T(8,128)(2,1)S(1)}, bf16[2,128,768]{2,1,0:T(8,128)(2,1)S(1)}, u32[]{:S(2)}, u32[]{:S(2)}) collective-permute-start(bf16[2,128,768]{2,1,0:T(8,128)(2,1)S(1)} %get-tuple-element.149), channel_id=1, source_target_pairs={{0,1},{1,0},{2,3},{3,2},{4,5},{5,4},{6,7},{7,6},{8,9},{9,8},{10,11... | collective-permute-start | bytes 1179656 | tf_op jit(solution)/shard_map/ppermute | solution.py:649
  171.6 40.2 %collective-permute-start.30 = (bf16[8,128,768]{2,1,0:T(8,128)(2,1)S(1)}, bf16[8,128,768]{2,1,0:T(8,128)(2,1)S(1)}, u32[]{:S(2)}, u32[]{:S(2)}) collective-permute-start(bf16[8,128,768]{2,1,0:T(8,128)(2,1)S(1)} %get-tuple-element.143), channel_id=1, source_target_pairs={{0,1},{1,0},{2,3},{3,2},{4,5},{5,4},{6,7},{7,6},{8,9},{9,8},{10,11... | collective-permute-start | bytes 4718600 | tf_op jit(solution)/shard_map/ppermute | solution.py:649
  179.8 24.7 %collective-permute-start.34 = (bf16[2,64,768]{2,1,0:T(8,128)(2,1)S(1)}, bf16[2,64,768]{2,1,0:T(8,128)(2,1)S(1)}, u32[]{:S(2)}, u32[]{:S(2)}) collective-permute-start(bf16[2,64,768]{2,1,0:T(8,128)(2,1)S(1)} %get-tuple-element.150), channel_id=1, source_target_pairs={{0,8},{2,10},{4,12},{6,14},{8,0},{10,2},{12,4},{14,6},{16,24},{18,... | collective-permute-start | bytes 589832 | tf_op jit(solution)/shard_map/ppermute | solution.py:656
  185.3 19.2 %collective-permute-start.35 = (bf16[2,64,768]{2,1,0:T(8,128)(2,1)S(1)}, bf16[2,64,768]{2,1,0:T(8,128)(2,1)S(1)}, u32[]{:S(2)}, u32[]{:S(2)}) collective-permute-start(bf16[2,64,768]{2,1,0:T(8,128)(2,1)S(1)} %get-tuple-element.151), channel_id=1, source_target_pairs={{0,12},{2,14},{4,8},{6,10},{8,4},{10,6},{12,0},{14,2},{16,28},{18,... | collective-permute-start | bytes 589832 | tf_op jit(solution)/shard_map/ppermute | solution.py:656
  220.5 56.7 %all-to-all-start.1 = ((bf16[16,64,768]{2,1,0:T(8,128)(2,1)}), bf16[16,64,768]{2,1,0:T(8,128)(2,1)S(1)}, u32[]{:S(2)}, u32[]{:S(2)}) async-start(bf16[16,64,768]{2,1,0:T(8,128)(2,1)} %get-tuple-element.166), calls=%async_computation.1 | async-start | bytes 3145728 | tf_op jit(solution)/shard_map/all_to_all | solution.py:914
  260.9 16.4 %collective-permute-start.50 = (bf16[800,384]{1,0:T(8,128)(2,1)}, bf16[800,384]{1,0:T(8,128)(2,1)}, u32[]{:S(2)}, u32[]{:S(2)}) collective-permute-start(bf16[800,384]{1,0:T(8,128)(2,1)} %get-tuple-element.191), channel_id=1, source_target_pairs={{0,4},{2,6},{4,0},{6,2},{8,12},{10,14},{12,8},{14,10},{16,20},{18,... | collective-permute-start | bytes 1843208 | tf_op jit(solution)/shard_map/ppermute | solution.py:656
  267.1 19.6 %collective-permute-start.49 = (bf16[512,768]{1,0:T(8,128)(2,1)}, bf16[512,768]{1,0:T(8,128)(2,1)}, u32[]{:S(2)}, u32[]{:S(2)}) collective-permute-start(bf16[512,768]{1,0:T(8,128)(2,1)} %get-tuple-element.188), channel_id=1, source_target_pairs={{0,1},{1,0},{2,3},{3,2},{4,5},{5,4},{6,7},{7,6},{8,9},{9,8},{10,11... | collective-permute-start | bytes 2359304 | tf_op jit(solution)/shard_map/ppermute | solution.py:649
  (51 other events, 545.8 us)

commit v4 on v3

--- a/solution.py
+++ b/solution.py
@@ -389,7 +389,7 @@
 
 def expert_kernel(first, count, chunk, place_ref, in_ref, out_ref, grads_ref, more_grads_ref, *refs):
     pieces, more_pieces = refs[:count], refs[count : 2 * count]
-    x_ref, ct_ref, active_ref, slope_ref, keep_ref, give_ref = refs[-6:]
+    x_ref, ct_ref, active_ref, slope_ref, ffn_keep_ref, ffn_give_ref, keep_ref, give_ref = refs[-8:]
     step = pl.program_id(0)
     place = place_ref[0]
     capacity = pieces[0].shape[1]
@@ -408,19 +408,24 @@
         ct_ref[0, rows + c * capacity : rows + (c + 1) * capacity] = more_grads_ref[source ^ c]
     x = x_ref[0]
     ct = ct_ref[0]
-    total = None
+    total = ffn = None
     for start in range(0, in_ref.shape[1], chunk):
         stop = start + chunk
         pre = dot(x, in_ref[:, start:stop])
         gains = dot(ct, out_ref[start:stop], NT)
         active, slope = gelu_both(pre)
-        active_ref[0, :, start:stop] = active.astype(low)
+        active = active.astype(low)
+        active_ref[0, :, start:stop] = active
+        more = dot(active, out_ref[start:stop])
+        ffn = more if ffn is None else ffn + more
         grad_pre = (gains * slope).astype(low)
         slope_ref[0, :, start:stop] = grad_pre
         term = dot(grad_pre, in_ref[:, start:stop], NT)
         total = term if total is None else total + term
     keep_ref[0] = total[:rows]
     give_ref[0] = total[rows:].astype(low)
+    ffn_keep_ref[0] = ffn[:rows]
+    ffn_give_ref[0] = ffn[rows:].astype(low)
 
 
 def expert_group(
@@ -437,9 +442,9 @@
     ]
     aliases = {}
     if buffers is not None:
-        aliases = {len(operands) + n: n for n in range(4)}
+        aliases = {len(operands) + n: n for n in range(6)}
         operands += buffers
-        specs += [pl.BlockSpec(memory_space=pl.ANY)] * 4
+        specs += [pl.BlockSpec(memory_space=pl.ANY)] * 6
 
     def block(height, size, offset):
         return pl.BlockSpec((1, height, size), lambda i: (offset + i, 0, 0))
@@ -452,10 +457,12 @@
             kept((chips, rows, width), low),
             kept((chips, rows, hidden), low),
             kept((chips, rows, hidden), low),
+            kept((chips, rows // 2, width), wide),
+            kept((chips, rows // 2, width), low),
             array((count, rows // 2, width), wide),
             array((count, rows // 2, width), low),
         ],
-        flops=6 * count * rows * width * hidden,
+        flops=8 * count * rows * width * hidden,
         grid=(count,),
         in_specs=specs,
         out_specs=[
@@ -463,13 +470,15 @@
             block(rows, width, first),
             block(rows, hidden, first),
             block(rows, hidden, first),
+            block(rows // 2, width, first),
+            block(rows // 2, width, first),
             block(rows // 2, width, 0),
             block(rows // 2, width, 0),
         ],
         input_output_aliases=aliases,
         first=earlier,
     )
-    return res[:4], res[4], res[5]
+    return res[:6], res[6], res[7]
 
 
 def pieces_kernel(keep_ref, more_ref, *out_refs):
@@ -493,11 +502,9 @@
         out_ref[...] = dot(chooser, values, TN).astype(low)
 
 
-def ffn_kernel(active_ref, weight_ref, keep_ref, give_ref):
-    values = dot(active_ref[0], weight_ref[...])
-    rows = keep_ref.shape[1]
-    keep_ref[0] = values[:rows]
-    give_ref[0] = values[rows:].astype(low)
+def last_pieces_kernel(keep_ref, more_ref, ffn_ref, *refs):
+    pieces_kernel(keep_ref, more_ref, *refs[:-1])
+    refs[-1][...] = ffn_ref[...]
 
 
 def product_kernel(left_ref, right_ref, out_ref):
@@ -826,6 +833,7 @@
     weight_in, weight_out = expert_in[0], expert_out[0]
     buffers = None
     returned = {}
+    sent = []
     done = []
     back = []
     for turn, span in enumerate(spans):
@@ -835,28 +843,24 @@
             own_pieces, [more_arrived[k] for k in range(*span)], buffers, span, chips,
             [turned_done] + [arrived[k] for k in range(1, chips)] if turn == 0 else [],
         )
-        *sums, token = run(pieces_kernel, (keep, across(give)), [piece] * quarter, mark=True)
+        sent.append((span, keep, across(give)))
+    slot_rows, grad_rows, actives, grad_pres, ffn_keep, ffn_give = buffers
+    rows = 4 * capacity
+    for turn, (span, keep, more) in enumerate(sent):
+        if turn == 2:
+            *sums, ffn_give, token = run(
+                last_pieces_kernel,
+                (keep, more, Far(ffn_give)),
+                [piece] * quarter + [array(ffn_give.shape, low)],
+                mark=True,
+            )
+        else:
+            *sums, token = run(pieces_kernel, (keep, more), [piece] * quarter, mark=True)
         done.append(token)
         for k in range(*span):
             returned[k] = swapped(sums[k - span[0]], 2 * k)
         back.append([returned[k] for k in range(*span)])
-    slot_rows, grad_rows, actives, grad_pres = buffers
-    rows = 4 * capacity
-    ffn_keep, ffn_give, ffn_done = run(
-        ffn_kernel,
-        (in_hbm(actives), weight_out),
-        [array((chips, rows // 2, width), wide), array((chips, rows // 2, width), low)],
-        flops=2 * chips * rows * width * hidden,
-        first=done[2:3],
-        mark=True,
-        light=True,
-        grid=(chips,),
-        in_specs=[
-            pl.BlockSpec((1, rows, hidden), lambda i: (i, 0, 0)),
-            pl.BlockSpec((hidden, width), lambda i: (0, 0)),
-        ],
-        out_specs=[pl.BlockSpec((1, rows // 2, width), lambda i: (i, 0, 0))] * 2,
-    )
+    ffn_done = done[2]
     ffn_more = across(ffn_give)
     tile = min(512, hidden)
     stripe = pl.BlockSpec((chips, rows, tile), lambda i: (0, 0, i))
@@ -906,7 +910,7 @@
     grad_more = across(grad_give)
     ffn_sums, sums_done = run(
         ffn_sum_kernel,
-        (place, ffn_keep, ffn_more),
+        (place, Far(ffn_keep), ffn_more),
         kept((experts_in_all, capacity, width), low),
         mark=True,
         first=(middle_done,),

time: 300 us -> 300 us (level)
    ppermute x32, waiting for transfers between devices: 40.7 us -> 33.6 us  [swapped(): return lax.ppermute(values, 'fsdp', [(i, i ^ offset) for i in range(count)])]
    ppermute x21, waiting for transfers between devices: 29.7 us -> 35.8 us  [across(): return lax.ppermute(values, 'tp', [(0, 1), (1, 0)])]
    pallas_call x28 -> x27, Pallas kernels: 126 us -> 127 us  [run(): pl.pallas_call(whole, out_shape=outs, compiler_params=pltpu.CompilerParam...]
  transfers between devices with their start and end apart: 56 -> 56, of which waited for: 21 -> 21; matrix products, arithmetic and copies ran while one was open for 4% -> 4% of each run, Pallas kernels for 40% -> 41%
where the time goes in v4:
time: 300 us; the launch traced here: 297 us
  Pallas kernels  127 us (42%)
  waiting for transfers between devices  80.8 us (27%)
  starting transfers between devices  73.8 us (25%)
  local copies, waits for them, and re-layouts  5.83 us (2%)
  other arithmetic  4.41 us (1%)
  matrix products  3.21 us (1%)
    pallas_call x27, Pallas kernels, run(): pl.pallas_call(whole, out_shape=outs, compiler_params=pltpu.CompilerParam...  127 us
    ppermute x32, starting transfers between devices, swapped(): return lax.ppermute(values, 'fsdp', [(i, i ^ offset) for i in range(count)])  45.6 us
    ppermute x21, waiting for transfers between devices, across(): return lax.ppermute(values, 'tp', [(0, 1), (1, 0)])  35.8 us
    ppermute x32, waiting for transfers between devices, swapped(): return lax.ppermute(values, 'fsdp', [(i, i ^ offset) for i in range(count)])  33.6 us
    ppermute x21, starting transfers between devices, across(): return lax.ppermute(values, 'tp', [(0, 1), (1, 0)])  19 us
    all_to_all x1, waiting for transfers between devices, shards(): lax.all_to_all(packed_grads.reshape(experts_in_all, capacity, width), 'fs...  11.4 us
  transfers between devices with their start and end apart: 56, of which 21 were waited for; matrix products, arithmetic and copies ran while one was open for 4% of the time, Pallas kernels for 41%

profile of v4, /device:TPU:0, one launch (start us, length us, event | category | flops | bytes accessed | tf_op | source)
XLA Modules:
  0.0 296.8 jit_solution(6111078404990528364)
XLA Ops:
  15.9 4.1 %collective-permute-done.3 = bf16[4,48,384]{2,1,0:T(8,128)(2,1)S(1)} collective-permute-done((bf16[4,48,384]{2,1,0:T(8,128)(2,1)S(1)}, bf16[4,48,384]{2,1,0:T(8,128)(2,1)S(1)}, u32[]{:S(2)}, u32[]{:S(2)}) %collective-permute-start.3) | collective-permute-done | bytes 147488 | tf_op jit(solution)/shard_map/ppermute | solution.py:663
  29.6 5.2 %all-to-all-start = ((bf16[16,64,768]{2,1,0:T(8,128)(2,1)}), bf16[16,64,768]{2,1,0:T(8,128)(2,1)S(1)}, u32[]{:S(2)}, u32[]{:S(2)}) async-start(bf16[16,64,768]{2,1,0:T(8,128)(2,1)} %bitcast.59), calls=%async_computation | async-start | bytes 3145728 | tf_op jit(solution)/shard_map/all_to_all | solution.py:769
  37.8 6.3 %shard_map.214 = (bf16[3,768,384]{2,1,0:T(8,128)(2,1)}, bf16[768,384]{1,0:T(8,128)(2,1)}, bf16[1024,1152]{1,0:T(8,128)(2,1)}, f32[4,768]{1,0:T(4,128)S(1)}) custom-call(s32[2]{0:T(128)S(1)} %pad_add_fusion.refs_0_, bf16[512,768]{1,0:T(8,128)(2,1)S(1)} %copy-done.2, bf16[512,768]{1,0:T(8,128)(2,1)S(1)} %collective-permute-done.7.refs_3_.refs_2_, ...), custom_call_target="tpu_custom_call" | custom-call | flops 1811939328 | bytes 8675336 | tf_op jit(solution)/shard_map/pallas_call | solution.py:95
  45.6 9.2 %shard_map.215 = (bf16[1024,384]{1,0:T(8,128)(2,1)}, f32[1024,384]{1,0:T(8,128)}, bf16[512,384]{1,0:T(8,128)(2,1)S(1)}, bf16[512,384]{1,0:T(8,128)(2,1)}) custom-call(s32[2]{0:T(128)S(1)} %pad_add_fusion.refs_0_, bf16[1024,1152]{1,0:T(8,128)(2,1)} %get-tuple-element.117.refs_1_.refs_2_.refs_3_, ...), custom_call_target="tpu_custom_call" | custom-call | flops 12000000000 | bytes 10747912 | tf_op jit(solution)/shard_map/pallas_call | solution.py:95
  55.3 11.4 %all-to-all-done.refs_4_.refs_3_ = bf16[16,64,768]{2,1,0:T(8,128)(2,1)S(1)} async-done(((bf16[16,64,768]{2,1,0:T(8,128)(2,1)}), bf16[16,64,768]{2,1,0:T(8,128)(2,1)S(1)}, u32[]{:S(2)}, u32[]{:S(2)}) %all-to-all-start) | async-done | bytes 1572896 | tf_op jit(solution)/shard_map/all_to_all | solution.py:769
  78.1 4.6 %collective-permute-start.14 = (bf16[2,64,768]{2,1,0:T(8,128)(2,1)S(1)}, bf16[2,64,768]{2,1,0:T(8,128)(2,1)S(1)}, u32[]{:S(2)}, u32[]{:S(2)}) collective-permute-start(bf16[2,64,768]{2,1,0:T(8,128)(2,1)S(1)} %get-tuple-element.123), channel_id=1, source_target_pairs={{0,8},{2,10},{4,12},{6,14},{8,0},{10,2},{12,4},{14,6},{16,24},{18,... | collective-permute-start | bytes 589832 | tf_op jit(solution)/shard_map/ppermute | solution.py:663
  85.5 4.5 %collective-permute-start.19 = (bf16[2,64,768]{2,1,0:T(8,128)(2,1)S(1)}, bf16[2,64,768]{2,1,0:T(8,128)(2,1)S(1)}, u32[]{:S(2)}, u32[]{:S(2)}) collective-permute-start(bf16[2,64,768]{2,1,0:T(8,128)(2,1)S(1)} %get-tuple-element.126), channel_id=1, source_target_pairs={{0,28},{2,30},{4,24},{6,26},{8,20},{10,22},{12,16},{14,18},{16,12}... | collective-permute-start | bytes 589832 | tf_op jit(solution)/shard_map/ppermute | solution.py:663
  99.1 5.4 %collective-permute-done.19.refs_16_.refs_6_ = bf16[2,64,768]{2,1,0:T(8,128)(2,1)S(1)} collective-permute-done((bf16[2,64,768]{2,1,0:T(8,128)(2,1)S(1)}, bf16[2,64,768]{2,1,0:T(8,128)(2,1)S(1)}, u32[]{:S(2)}, u32[]{:S(2)}) %collective-permute-start.19) | collective-permute-done | bytes 196640 | tf_op jit(solution)/shard_map/ppermute | solution.py:663
  105.0 3.9 %shard_map.218 = (bf16[768,1024]{1,0:T(8,128)(2,1)}, f32[8,128]{1,0:T(8,128)S(1)}) custom-call(s32[2]{0:T(128)S(1)} %pad_add_fusion.refs_0_, bf16[512,768]{1,0:T(8,128)(2,1)} %refs_3_.3, bf16[512,768]{1,0:T(8,128)(2,1)} %copy-done.3, f32[4,768]{1,0:T(4,128)S(1)} %get-tuple-element.121.refs_5_.refs_3_.refs_12_.refs_4_, ...), custom_call_target="tpu_custom_call" | custom-call | bytes 3158024 | tf_op jit(solution)/shard_map/pallas_call | solution.py:95
  108.8 8.9 %collective-permute-done.22.refs_13_.refs_5_ = bf16[2,64,768]{2,1,0:T(8,128)(2,1)S(1)} collective-permute-done((bf16[2,64,768]{2,1,0:T(8,128)(2,1)S(1)}, bf16[2,64,768]{2,1,0:T(8,128)(2,1)S(1)}, u32[]{:S(2)}, u32[]{:S(2)}) %collective-permute-start.22) | collective-permute-done | bytes 196640 | tf_op jit(solution)/shard_map/ppermute | solution.py:663
  125.5 8.2 %shard_map.219 = (bf16[8,256,768]{2,1,0:T(8,128)(2,1)}, bf16[8,256,768]{2,1,0:T(8,128)(2,1)}, bf16[8,256,1536]{2,1,0:T(8,128)(2,1)}, bf16[8,256,1536]{2,1,0:T(8,...) custom-call(s32[2]{0:T(128)S(1)} %pad_add_fusion.refs_0_, ...), custom_call_target="tpu_custom_call" | custom-call | flops 4831838208 | bytes 33423368 | tf_op jit(solution)/shard_map/pallas_call | solution.py:95
  134.2 8.0 %shard_map.220 = (bf16[8,256,768]{2,1,0:T(8,128)(2,1)}, bf16[8,256,768]{2,1,0:T(8,128)(2,1)}, bf16[8,256,1536]{2,1,0:T(8,128)(2,1)}, bf16[8,256,1536]{2,1,0:T(8,...) custom-call(s32[2]{0:T(128)S(1)} %pad_add_fusion.refs_0_, ...), custom_call_target="tpu_custom_call", output_to_operand_aliasing={{0}: (9, {}), {1}: (10, {}), {2}: (11, {}), {3}: (12, {}), ... | custom-call | flops 4831838208 | bytes 57016328 | tf_op jit(solution)/shard_map/pallas_call | solution.py:95
  143.7 8.0 %shard_map.221 = (bf16[8,256,768]{2,1,0:T(8,128)(2,1)}, bf16[8,256,768]{2,1,0:T(8,128)(2,1)}, bf16[8,256,1536]{2,1,0:T(8,128)(2,1)}, bf16[8,256,1536]{2,1,0:T(8,...) custom-call(s32[2]{0:T(128)S(1)} %pad_add_fusion.refs_0_, ...), custom_call_target="tpu_custom_call", output_to_operand_aliasing={{0}: (9, {}), {1}: (10, {}), {2}: (11, {}), {3}: (12, {}), ... | custom-call | flops 4831838208 | bytes 57016328 | tf_op jit(solution)/shard_map/pallas_call | solution.py:95
  153.7 8.0 %shard_map.222 = (bf16[8,256,768]{2,1,0:T(8,128)(2,1)}, bf16[8,256,768]{2,1,0:T(8,128)(2,1)}, bf16[8,256,1536]{2,1,0:T(8,128)(2,1)}, bf16[8,256,1536]{2,1,0:T(8,...) custom-call(s32[2]{0:T(128)S(1)} %pad_add_fusion.refs_0_, ...), custom_call_target="tpu_custom_call", output_to_operand_aliasing={{0}: (9, {}), {1}: (10, {}), {2}: (11, {}), {3}: (12, {}), ... | custom-call | flops 4831838208 | bytes 57016328 | tf_op jit(solution)/shard_map/pallas_call | solution.py:95
  173.4 7.1 %collective-permute-done.33.refs_1_ = bf16[2,128,768]{2,1,0:T(8,128)(2,1)S(1)} collective-permute-done((bf16[2,128,768]{2,1,0:T(8,128)(2,1)S(1)}, bf16[2,128,768]{2,1,0:T(8,128)(2,1)S(1)}, u32[]{:S(2)}, u32[]{:S(2)}) %collective-permute-start.33) | collective-permute-done | bytes 393248 | tf_op jit(solution)/shard_map/ppermute | solution.py:656
  187.9 9.7 %shard_map.227 = (f32[1536,768]{1,0:T(8,128)}, f32[8,128]{1,0:T(8,128)S(1)}) custom-call(bf16[8,256,1536]{2,1,0:T(8,128)(2,1)} %get-tuple-element.169.refs_0_, bf16[8,256,768]{2,1,0:T(8,128)(2,1)} %get-tuple-element.170.refs_1_, f32[8,128]{1,0:T(8,128)S(1)} %get-tuple-element.171.refs_2_, f32[8,128]{1,0:T(8,128)S(1)} %get-tuple-element.172.refs_3_, ...), custom_call_target="tpu_custom_call" | custom-call | flops 4831838208 | bytes 14155776 | tf_op jit(solution)/shard_map/pallas_call | solution.py:95
  202.6 9.3 %collective-permute-done.30.refs_10_.refs_2_ = bf16[8,128,768]{2,1,0:T(8,128)(2,1)S(1)} collective-permute-done((bf16[8,128,768]{2,1,0:T(8,128)(2,1)S(1)}, bf16[8,128,768]{2,1,0:T(8,128)(2,1)S(1)}, u32[]{:S(2)}, u32[]{:S(2)}) %collective-permute-start.30) | collective-permute-done | bytes 1572896 | tf_op jit(solution)/shard_map/ppermute | solution.py:656
  211.9 6.1 %shard_map.229 = (f32[512,768]{1,0:T(8,128)}, bf16[512,384]{1,0:T(8,128)(2,1)S(1)}, bf16[512,384]{1,0:T(8,128)(2,1)}, f32[2,768]{1,0:T(2,128)S(1)}, f32[2,8,48,3...) custom-call(s32[2]{0:T(128)S(1)} %pad_add_fusion.refs_0_, ...), custom_call_target="tpu_custom_call" | custom-call | flops 1207959552 | bytes 10045448 | tf_op jit(solution)/shard_map/pallas_call | solution.py:95
  225.9 4.0 %collective-permute-done.42.refs_9_ = bf16[512,384]{1,0:T(8,128)(2,1)} collective-permute-done((bf16[512,384]{1,0:T(8,128)(2,1)}, bf16[512,384]{1,0:T(8,128)(2,1)}, u32[]{:S(2)}, u32[]{:S(2)}) %collective-permute-start.42) | collective-permute-done | bytes 393248 | tf_op jit(solution)/shard_map/ppermute | solution.py:656
  229.9 20.0 %shard_map.233 = (bf16[3,1024,384]{2,1,0:T(8,128)(2,1)}, bf16[2,4,3,48,384]{4,3,2,1,0:T(8,128)(2,1)S(1)}, bf16[2,4,3,48,384]{4,3,2,1,0:T(8,128)(2,1)S(1)}, f32[4,768]{1,0:T(4,128)S(1)}) custom-call(s32[2]{0:T(128)S(1)} %pad_add_fusion.refs_0_, bf16[1024,1152]{1,0:T(8,128)(2,1)} %get-tuple-element.117.refs_1_.refs_2_.refs_3_, ...), custom_call_target="tpu_custom_call" | custom-call | flops 30000001024 | bytes 18249736 | tf_op jit(solution)/shard_map/pallas_call | solution.py:95
  252.3 7.4 %collective-permute-done.47.refs_6_ = f32[4,768]{1,0:T(4,128)S(1)} collective-permute-done((f32[4,768]{1,0:T(4,128)S(1)}, f32[4,768]{1,0:T(4,128)S(1)}, u32[]{:S(2)}, u32[]{:S(2)}) %collective-permute-start.47) | collective-permute-done | bytes 12320 | tf_op jit(solution)/shard_map/ppermute | solution.py:656
  261.5 5.6 %shard_map.235 = (bf16[512,768]{1,0:T(8,128)(2,1)}, f32[512,768]{1,0:T(8,128)S(1)}, f32[8,128]{1,0:T(8,128)S(1)}) custom-call(s32[2]{0:T(128)S(1)} %pad_add_fusion.refs_0_, bf16[3,1024,384]{2,1,0:T(8,128)(2,1)} %get-tuple-element.192.refs_1_, bf16[3,768,384]{2,1,0:T(8,128)(2,1)} %get-tuple-element.186.refs_11_.refs_2_, f32[8,128]{1,0:T(8,128)S(1)} %get-tuple-element.198.refs_3_), custom_call_target="tpu_custom_call" | custom-call | tf_op jit(solution)/shard_map/pallas_call | solution.py:95
  267.6 9.7 %shard_map.237 = (f32[768,1536]{1,0:T(8,128)}, f32[8,128]{1,0:T(8,128)S(1)}) custom-call(bf16[8,256,768]{2,1,0:T(8,128)(2,1)} %get-tuple-element.205.refs_0_, bf16[8,256,1536]{2,1,0:T(8,128)(2,1)} %get-tuple-element.206.refs_1_, f32[8,128]{1,0:T(8,128)S(1)} %get-tuple-element.207.refs_2_), custom_call_target="tpu_custom_call" | custom-call | tf_op jit(solution)/shard_map/pallas_call | solution.py:95
  286.7 4.0 %shard_map.236 = (f32[512,768]{1,0:T(8,128)}, f32[8,128]{1,0:T(8,128)S(1)}) custom-call(f32[512,768]{1,0:T(8,128)} %get-tuple-element.180.refs_0_, f32[512,768]{1,0:T(8,128)S(1)} %get-tuple-element.199.refs_1_, bf16[512,768]{1,0:T(8,128)(2,1)} %collective-permute-done.49.refs_2_, bf16[512,768]{1,0:T(8,128)(2,1)} %refs_3_.3, ...), custom_call_target="tpu_custom_call" | custom-call | tf_op jit(solution)/shard_map/pallas_call | solution.py:95
  (178 shorter events, 117.0 us)
Async XLA Ops:
  1.6 20.5 %collective-permute-start = (bf16[4,48,384]{2,1,0:T(8,128)(2,1)S(1)}, bf16[4,48,384]{2,1,0:T(8,128)(2,1)S(1)}, u32[]{:S(2)}, u32[]{:S(2)}) collective-permute-start(bf16[4,48,384]{2,1,0:T(8,128)(2,1)S(1)} %pad_maximum_fusion), channel_id=1, source_target_pairs={{0,4},{2,6},{4,0},{6,2},{8,12},{10,14},{12,8},{14,10},{16,20},{18,... | collective-permute-start | bytes 442376 | tf_op jit(solution)/shard_map/ppermute | solution.py:663
  9.0 18.5 %collective-permute-start.7 = (bf16[512,768]{1,0:T(8,128)(2,1)}, bf16[512,768]{1,0:T(8,128)(2,1)S(1)}, u32[]{:S(2)}, u32[]{:S(2)}) collective-permute-start(bf16[512,768]{1,0:T(8,128)(2,1)} %refs_3_.3), channel_id=1, source_target_pairs={{0,1},{1,0},{2,3},{3,2},{4,5},{5,4},{6,7},{7,6},{8,9},{9,8},{10,11... | collective-permute-start | bytes 2359304 | tf_op jit(solution)/shard_map/ppermute | solution.py:656
  29.6 37.2 %all-to-all-start = ((bf16[16,64,768]{2,1,0:T(8,128)(2,1)}), bf16[16,64,768]{2,1,0:T(8,128)(2,1)S(1)}, u32[]{:S(2)}, u32[]{:S(2)}) async-start(bf16[16,64,768]{2,1,0:T(8,128)(2,1)} %bitcast.59), calls=%async_computation | async-start | bytes 3145728 | tf_op jit(solution)/shard_map/all_to_all | solution.py:769
  44.1 24.5 %collective-permute-start.11 = (bf16[768,384]{1,0:T(8,128)(2,1)}, bf16[768,384]{1,0:T(8,128)(2,1)S(1)}, u32[]{:S(2)}, u32[]{:S(2)}) collective-permute-start(bf16[768,384]{1,0:T(8,128)(2,1)} %get-tuple-element.120.refs_2_.refs_6_), channel_id=1, source_target_pairs={{0,1},{1,0},{2,3},{3,2},{4,5},{5,4},{6,7},{7,6},{8,9},{9,8},{10,11... | collective-permute-start | bytes 1769480 | tf_op jit(solution)/shard_map/ppermute | solution.py:656
  66.8 57.2 %collective-permute-start.8 = (bf16[16,64,768]{2,1,0:T(8,128)(2,1)S(1)}, bf16[16,64,768]{2,1,0:T(8,128)(2,1)S(1)}, u32[]{:S(2)}, u32[]{:S(2)}) collective-permute-start(bf16[16,64,768]{2,1,0:T(8,128)(2,1)S(1)} %all-to-all-done.refs_4_.refs_3_), channel_id=1, source_target_pairs={{0,1},{1,0},{2,3},{3,2},{4,5},{5,4},{6,7},{7,6},{8,9},{9,8},{10,11... | collective-permute-start | bytes 4718600 | tf_op jit(solution)/shard_map/ppermute | solution.py:656
  85.5 19.0 %collective-permute-start.19 = (bf16[2,64,768]{2,1,0:T(8,128)(2,1)S(1)}, bf16[2,64,768]{2,1,0:T(8,128)(2,1)S(1)}, u32[]{:S(2)}, u32[]{:S(2)}) collective-permute-start(bf16[2,64,768]{2,1,0:T(8,128)(2,1)S(1)} %get-tuple-element.126), channel_id=1, source_target_pairs={{0,28},{2,30},{4,24},{6,26},{8,20},{10,22},{12,16},{14,18},{16,12}... | collective-permute-start | bytes 589832 | tf_op jit(solution)/shard_map/ppermute | solution.py:663
  90.0 27.8 %collective-permute-start.22 = (bf16[2,64,768]{2,1,0:T(8,128)(2,1)S(1)}, bf16[2,64,768]{2,1,0:T(8,128)(2,1)S(1)}, u32[]{:S(2)}, u32[]{:S(2)}) collective-permute-start(bf16[2,64,768]{2,1,0:T(8,128)(2,1)S(1)} %get-tuple-element.127), channel_id=1, source_target_pairs={{0,16},{2,18},{4,20},{6,22},{8,24},{10,26},{12,28},{14,30},{16,0},... | collective-permute-start | bytes 589832 | tf_op jit(solution)/shard_map/ppermute | solution.py:663
  92.7 28.6 %collective-permute-start.23 = (bf16[2,64,768]{2,1,0:T(8,128)(2,1)S(1)}, bf16[2,64,768]{2,1,0:T(8,128)(2,1)S(1)}, u32[]{:S(2)}, u32[]{:S(2)}) collective-permute-start(bf16[2,64,768]{2,1,0:T(8,128)(2,1)S(1)} %get-tuple-element.128), channel_id=1, source_target_pairs={{0,20},{2,22},{4,16},{6,18},{8,28},{10,30},{12,24},{14,26},{16,4},... | collective-permute-start | bytes 589832 | tf_op jit(solution)/shard_map/ppermute | solution.py:663
  98.6 23.3 %collective-permute-start.27 = (bf16[2,64,768]{2,1,0:T(8,128)(2,1)S(1)}, bf16[2,64,768]{2,1,0:T(8,128)(2,1)S(1)}, u32[]{:S(2)}, u32[]{:S(2)}) collective-permute-start(bf16[2,64,768]{2,1,0:T(8,128)(2,1)S(1)} %get-tuple-element.129.refs_4_.refs_5_), channel_id=1, source_target_pairs={{0,1},{1,0},{2,3},{3,2},{4,5},{5,4},{6,7},{7,6},{8,9},{9,8},{10,11... | collective-permute-start | bytes 589832 | tf_op jit(solution)/shard_map/ppermute | solution.py:656
  104.5 19.0 %collective-permute-start.28 = (bf16[2,64,768]{2,1,0:T(8,128)(2,1)S(1)}, bf16[2,64,768]{2,1,0:T(8,128)(2,1)S(1)}, u32[]{:S(2)}, u32[]{:S(2)}) collective-permute-start(bf16[2,64,768]{2,1,0:T(8,128)(2,1)S(1)} %collective-permute-done.26.refs_6_.refs_10_), channel_id=1, source_target_pairs={{0,1},{1,0},{2,3},{3,2},{4,5},{5,4},{6,7},{7,6},{8,9},{9,8},{10,11... | collective-permute-start | bytes 589832 | tf_op jit(solution)/shard_map/ppermute | solution.py:656
  121.9 21.8 %collective-permute-start.20 = (bf16[2,64,768]{2,1,0:T(8,128)(2,1)S(1)}, bf16[2,64,768]{2,1,0:T(8,128)(2,1)S(1)}, u32[]{:S(2)}, u32[]{:S(2)}) collective-permute-start(bf16[2,64,768]{2,1,0:T(8,128)(2,1)S(1)} %collective-permute-done.18.refs_15_.refs_5_), channel_id=1, source_target_pairs={{0,1},{1,0},{2,3},{3,2},{4,5},{5,4},{6,7},{7,6},{8,9},{9,8},{10,11... | collective-permute-start | bytes 589832 | tf_op jit(solution)/shard_map/ppermute | solution.py:656
  123.4 20.3 %collective-permute-start.21 = (bf16[2,64,768]{2,1,0:T(8,128)(2,1)S(1)}, bf16[2,64,768]{2,1,0:T(8,128)(2,1)S(1)}, u32[]{:S(2)}, u32[]{:S(2)}) collective-permute-start(bf16[2,64,768]{2,1,0:T(8,128)(2,1)S(1)} %collective-permute-done.19.refs_16_.refs_6_), channel_id=1, source_target_pairs={{0,1},{1,0},{2,3},{3,2},{4,5},{5,4},{6,7},{7,6},{8,9},{9,8},{10,11... | collective-permute-start | bytes 589832 | tf_op jit(solution)/shard_map/ppermute | solution.py:656
  124.0 29.7 %collective-permute-start.16 = (bf16[2,64,768]{2,1,0:T(8,128)(2,1)S(1)}, bf16[2,64,768]{2,1,0:T(8,128)(2,1)S(1)}, u32[]{:S(2)}, u32[]{:S(2)}) collective-permute-start(bf16[2,64,768]{2,1,0:T(8,128)(2,1)S(1)} %collective-permute-done.14.refs_11_.refs_5_), channel_id=1, source_target_pairs={{0,1},{1,0},{2,3},{3,2},{4,5},{5,4},{6,7},{7,6},{8,9},{9,8},{10,11... | collective-permute-start | bytes 589832 | tf_op jit(solution)/shard_map/ppermute | solution.py:656
  133.6 20.1 %collective-permute-start.17 = (bf16[2,64,768]{2,1,0:T(8,128)(2,1)S(1)}, bf16[2,64,768]{2,1,0:T(8,128)(2,1)S(1)}, u32[]{:S(2)}, u32[]{:S(2)}) collective-permute-start(bf16[2,64,768]{2,1,0:T(8,128)(2,1)S(1)} %collective-permute-done.15.refs_12_.refs_6_), channel_id=1, source_target_pairs={{0,1},{1,0},{2,3},{3,2},{4,5},{5,4},{6,7},{7,6},{8,9},{9,8},{10,11... | collective-permute-start | bytes 589832 | tf_op jit(solution)/shard_map/ppermute | solution.py:656
  142.2 23.7 %collective-permute-start.36 = (bf16[2,128,768]{2,1,0:T(8,128)(2,1)S(1)}, bf16[2,128,768]{2,1,0:T(8,128)(2,1)S(1)}, u32[]{:S(2)}, u32[]{:S(2)}) collective-permute-start(bf16[2,128,768]{2,1,0:T(8,128)(2,1)S(1)} %get-tuple-element.164), channel_id=1, source_target_pairs={{0,1},{1,0},{2,3},{3,2},{4,5},{5,4},{6,7},{7,6},{8,9},{9,8},{10,11... | collective-permute-start | bytes 1179656 | tf_op jit(solution)/shard_map/ppermute | solution.py:656
  152.2 19.9 %collective-permute-start.31 = (bf16[2,128,768]{2,1,0:T(8,128)(2,1)S(1)}, bf16[2,128,768]{2,1,0:T(8,128)(2,1)S(1)}, u32[]{:S(2)}, u32[]{:S(2)}) collective-permute-start(bf16[2,128,768]{2,1,0:T(8,128)(2,1)S(1)} %get-tuple-element.156), channel_id=1, source_target_pairs={{0,1},{1,0},{2,3},{3,2},{4,5},{5,4},{6,7},{7,6},{8,9},{9,8},{10,11... | collective-permute-start | bytes 1179656 | tf_op jit(solution)/shard_map/ppermute | solution.py:656
  161.7 18.9 %collective-permute-start.33 = (bf16[2,128,768]{2,1,0:T(8,128)(2,1)S(1)}, bf16[2,128,768]{2,1,0:T(8,128)(2,1)S(1)}, u32[]{:S(2)}, u32[]{:S(2)}) collective-permute-start(bf16[2,128,768]{2,1,0:T(8,128)(2,1)S(1)} %get-tuple-element.160), channel_id=1, source_target_pairs={{0,1},{1,0},{2,3},{3,2},{4,5},{5,4},{6,7},{7,6},{8,9},{9,8},{10,11... | collective-permute-start | bytes 1179656 | tf_op jit(solution)/shard_map/ppermute | solution.py:656
  165.3 46.6 %collective-permute-start.30 = (bf16[8,128,768]{2,1,0:T(8,128)(2,1)S(1)}, bf16[8,128,768]{2,1,0:T(8,128)(2,1)S(1)}, u32[]{:S(2)}, u32[]{:S(2)}) collective-permute-start(bf16[8,128,768]{2,1,0:T(8,128)(2,1)S(1)} %get-tuple-element.154), channel_id=1, source_target_pairs={{0,1},{1,0},{2,3},{3,2},{4,5},{5,4},{6,7},{7,6},{8,9},{9,8},{10,11... | collective-permute-start | bytes 4718600 | tf_op jit(solution)/shard_map/ppermute | solution.py:656
  180.6 17.0 %collective-permute-start.34 = (bf16[2,64,768]{2,1,0:T(8,128)(2,1)S(1)}, bf16[2,64,768]{2,1,0:T(8,128)(2,1)S(1)}, u32[]{:S(2)}, u32[]{:S(2)}) collective-permute-start(bf16[2,64,768]{2,1,0:T(8,128)(2,1)S(1)} %get-tuple-element.161), channel_id=1, source_target_pairs={{0,8},{2,10},{4,12},{6,14},{8,0},{10,2},{12,4},{14,6},{16,24},{18,... | collective-permute-start | bytes 589832 | tf_op jit(solution)/shard_map/ppermute | solution.py:663
  181.3 17.9 %collective-permute-start.35 = (bf16[2,64,768]{2,1,0:T(8,128)(2,1)S(1)}, bf16[2,64,768]{2,1,0:T(8,128)(2,1)S(1)}, u32[]{:S(2)}, u32[]{:S(2)}) collective-permute-start(bf16[2,64,768]{2,1,0:T(8,128)(2,1)S(1)} %get-tuple-element.162), channel_id=1, source_target_pairs={{0,12},{2,14},{4,8},{6,10},{8,4},{10,6},{12,0},{14,2},{16,28},{18,... | collective-permute-start | bytes 589832 | tf_op jit(solution)/shard_map/ppermute | solution.py:663
  182.8 16.4 %collective-permute-start.39 = (bf16[2,64,768]{2,1,0:T(8,128)(2,1)S(1)}, bf16[2,64,768]{2,1,0:T(8,128)(2,1)S(1)}, u32[]{:S(2)}, u32[]{:S(2)}) collective-permute-start(bf16[2,64,768]{2,1,0:T(8,128)(2,1)S(1)} %get-tuple-element.167), channel_id=1, source_target_pairs={{0,24},{2,26},{4,28},{6,30},{8,16},{10,18},{12,20},{14,22},{16,8},... | collective-permute-start | bytes 589832 | tf_op jit(solution)/shard_map/ppermute | solution.py:663
  221.9 55.4 %all-to-all-start.1 = ((bf16[16,64,768]{2,1,0:T(8,128)(2,1)}), bf16[16,64,768]{2,1,0:T(8,128)(2,1)S(1)}, u32[]{:S(2)}, u32[]{:S(2)}) async-start(bf16[16,64,768]{2,1,0:T(8,128)(2,1)} %get-tuple-element.178), calls=%async_computation.1 | async-start | bytes 3145728 | tf_op jit(solution)/shard_map/all_to_all | solution.py:918
  260.9 16.4 %collective-permute-start.50 = (bf16[800,384]{1,0:T(8,128)(2,1)}, bf16[800,384]{1,0:T(8,128)(2,1)}, u32[]{:S(2)}, u32[]{:S(2)}) collective-permute-start(bf16[800,384]{1,0:T(8,128)(2,1)} %get-tuple-element.203), channel_id=1, source_target_pairs={{0,4},{2,6},{4,0},{6,2},{8,12},{10,14},{12,8},{14,10},{16,20},{18,... | collective-permute-start | bytes 1843208 | tf_op jit(solution)/shard_map/ppermute | solution.py:663
  267.1 19.6 %collective-permute-start.49 = (bf16[512,768]{1,0:T(8,128)(2,1)}, bf16[512,768]{1,0:T(8,128)(2,1)}, u32[]{:S(2)}, u32[]{:S(2)}) collective-permute-start(bf16[512,768]{1,0:T(8,128)(2,1)} %get-tuple-element.200), channel_id=1, source_target_pairs={{0,1},{1,0},{2,3},{3,2},{4,5},{5,4},{6,7},{7,6},{8,9},{9,8},{10,11... | collective-permute-start | bytes 2359304 | tf_op jit(solution)/shard_map/ppermute | solution.py:656
  (51 other events, 546.1 us)

commit v5 on v4

--- a/solution.py
+++ b/solution.py
@@ -870,7 +870,7 @@
         (in_hbm(actives), in_hbm(grad_rows)),
         array((hidden, width), wide),
         flops=2 * chips * rows * width * hidden,
-        first=(ffn_done, done[3], *back[0], *back[1]),
+        first=(ffn_done, done[3], *back[1]),
         mark=True,
         grid=(hidden // tile,),
         in_specs=[stripe, fixed],

time: 300 us -> 300 us (level)
  no operation moved by 1% of the time
where the time goes in v5:
time: 300 us; the launch traced here: 297 us
  Pallas kernels  127 us (42%)
  waiting for transfers between devices  80.7 us (27%)
  starting transfers between devices  73.8 us (25%)
  local copies, waits for them, and re-layouts  5.83 us (2%)
  other arithmetic  4.41 us (1%)
  matrix products  3.21 us (1%)
    pallas_call x27, Pallas kernels, run(): pl.pallas_call(whole, out_shape=outs, compiler_params=pltpu.CompilerParam...  127 us
    ppermute x32, starting transfers between devices, swapped(): return lax.ppermute(values, 'fsdp', [(i, i ^ offset) for i in range(count)])  44.9 us
    ppermute x21, waiting for transfers between devices, across(): return lax.ppermute(values, 'tp', [(0, 1), (1, 0)])  35.9 us
    ppermute x32, waiting for transfers between devices, swapped(): return lax.ppermute(values, 'fsdp', [(i, i ^ offset) for i in range(count)])  33.4 us
    ppermute x21, starting transfers between devices, across(): return lax.ppermute(values, 'tp', [(0, 1), (1, 0)])  19.8 us
    all_to_all x1, waiting for transfers between devices, shards(): lax.all_to_all(packed_grads.reshape(experts_in_all, capacity, width), 'fs...  11.4 us
  transfers between devices with their start and end apart: 56, of which 21 were waited for; matrix products, arithmetic and copies ran while one was open for 4% of the time, Pallas kernels for 41%

profile of v5, /device:TPU:0, one launch (start us, length us, event | category | flops | bytes accessed | tf_op | source)
XLA Modules:
  0.0 296.8 jit_solution(12233524293689974198)
XLA Ops:
  15.9 4.1 %collective-permute-done.3 = bf16[4,48,384]{2,1,0:T(8,128)(2,1)S(1)} collective-permute-done((bf16[4,48,384]{2,1,0:T(8,128)(2,1)S(1)}, bf16[4,48,384]{2,1,0:T(8,128)(2,1)S(1)}, u32[]{:S(2)}, u32[]{:S(2)}) %collective-permute-start.3) | collective-permute-done | bytes 147488 | tf_op jit(solution)/shard_map/ppermute | solution.py:663
  29.6 5.2 %all-to-all-start = ((bf16[16,64,768]{2,1,0:T(8,128)(2,1)}), bf16[16,64,768]{2,1,0:T(8,128)(2,1)S(1)}, u32[]{:S(2)}, u32[]{:S(2)}) async-start(bf16[16,64,768]{2,1,0:T(8,128)(2,1)} %bitcast.59), calls=%async_computation | async-start | bytes 3145728 | tf_op jit(solution)/shard_map/all_to_all | solution.py:769
  37.8 6.3 %shard_map.214 = (bf16[3,768,384]{2,1,0:T(8,128)(2,1)}, bf16[768,384]{1,0:T(8,128)(2,1)}, bf16[1024,1152]{1,0:T(8,128)(2,1)}, f32[4,768]{1,0:T(4,128)S(1)}) custom-call(s32[2]{0:T(128)S(1)} %pad_add_fusion.refs_0_, bf16[512,768]{1,0:T(8,128)(2,1)S(1)} %copy-done.2, bf16[512,768]{1,0:T(8,128)(2,1)S(1)} %collective-permute-done.7.refs_3_.refs_2_, ...), custom_call_target="tpu_custom_call" | custom-call | flops 1811939328 | bytes 8675336 | tf_op jit(solution)/shard_map/pallas_call | solution.py:95
  45.6 9.2 %shard_map.215 = (bf16[1024,384]{1,0:T(8,128)(2,1)}, f32[1024,384]{1,0:T(8,128)}, bf16[512,384]{1,0:T(8,128)(2,1)S(1)}, bf16[512,384]{1,0:T(8,128)(2,1)}) custom-call(s32[2]{0:T(128)S(1)} %pad_add_fusion.refs_0_, bf16[1024,1152]{1,0:T(8,128)(2,1)} %get-tuple-element.117.refs_1_.refs_2_.refs_3_, ...), custom_call_target="tpu_custom_call" | custom-call | flops 12000000000 | bytes 10747912 | tf_op jit(solution)/shard_map/pallas_call | solution.py:95
  55.3 11.4 %all-to-all-done.refs_4_.refs_3_ = bf16[16,64,768]{2,1,0:T(8,128)(2,1)S(1)} async-done(((bf16[16,64,768]{2,1,0:T(8,128)(2,1)}), bf16[16,64,768]{2,1,0:T(8,128)(2,1)S(1)}, u32[]{:S(2)}, u32[]{:S(2)}) %all-to-all-start) | async-done | bytes 1572896 | tf_op jit(solution)/shard_map/all_to_all | solution.py:769
  78.1 4.6 %collective-permute-start.14 = (bf16[2,64,768]{2,1,0:T(8,128)(2,1)S(1)}, bf16[2,64,768]{2,1,0:T(8,128)(2,1)S(1)}, u32[]{:S(2)}, u32[]{:S(2)}) collective-permute-start(bf16[2,64,768]{2,1,0:T(8,128)(2,1)S(1)} %get-tuple-element.123), channel_id=1, source_target_pairs={{0,8},{2,10},{4,12},{6,14},{8,0},{10,2},{12,4},{14,6},{16,24},{18,... | collective-permute-start | bytes 589832 | tf_op jit(solution)/shard_map/ppermute | solution.py:663
  85.5 4.5 %collective-permute-start.19 = (bf16[2,64,768]{2,1,0:T(8,128)(2,1)S(1)}, bf16[2,64,768]{2,1,0:T(8,128)(2,1)S(1)}, u32[]{:S(2)}, u32[]{:S(2)}) collective-permute-start(bf16[2,64,768]{2,1,0:T(8,128)(2,1)S(1)} %get-tuple-element.126), channel_id=1, source_target_pairs={{0,28},{2,30},{4,24},{6,26},{8,20},{10,22},{12,16},{14,18},{16,12}... | collective-permute-start | bytes 589832 | tf_op jit(solution)/shard_map/ppermute | solution.py:663
  99.1 5.4 %collective-permute-done.19.refs_16_.refs_6_ = bf16[2,64,768]{2,1,0:T(8,128)(2,1)S(1)} collective-permute-done((bf16[2,64,768]{2,1,0:T(8,128)(2,1)S(1)}, bf16[2,64,768]{2,1,0:T(8,128)(2,1)S(1)}, u32[]{:S(2)}, u32[]{:S(2)}) %collective-permute-start.19) | collective-permute-done | bytes 196640 | tf_op jit(solution)/shard_map/ppermute | solution.py:663
  105.0 3.9 %shard_map.218 = (bf16[768,1024]{1,0:T(8,128)(2,1)}, f32[8,128]{1,0:T(8,128)S(1)}) custom-call(s32[2]{0:T(128)S(1)} %pad_add_fusion.refs_0_, bf16[512,768]{1,0:T(8,128)(2,1)} %refs_3_.3, bf16[512,768]{1,0:T(8,128)(2,1)} %copy-done.3, f32[4,768]{1,0:T(4,128)S(1)} %get-tuple-element.121.refs_5_.refs_3_.refs_12_.refs_4_, ...), custom_call_target="tpu_custom_call" | custom-call | bytes 3158024 | tf_op jit(solution)/shard_map/pallas_call | solution.py:95
  108.8 8.9 %collective-permute-done.22.refs_13_.refs_5_ = bf16[2,64,768]{2,1,0:T(8,128)(2,1)S(1)} collective-permute-done((bf16[2,64,768]{2,1,0:T(8,128)(2,1)S(1)}, bf16[2,64,768]{2,1,0:T(8,128)(2,1)S(1)}, u32[]{:S(2)}, u32[]{:S(2)}) %collective-permute-start.22) | collective-permute-done | bytes 196640 | tf_op jit(solution)/shard_map/ppermute | solution.py:663
  125.5 8.2 %shard_map.219 = (bf16[8,256,768]{2,1,0:T(8,128)(2,1)}, bf16[8,256,768]{2,1,0:T(8,128)(2,1)}, bf16[8,256,1536]{2,1,0:T(8,128)(2,1)}, bf16[8,256,1536]{2,1,0:T(8,...) custom-call(s32[2]{0:T(128)S(1)} %pad_add_fusion.refs_0_, ...), custom_call_target="tpu_custom_call" | custom-call | flops 4831838208 | bytes 33423368 | tf_op jit(solution)/shard_map/pallas_call | solution.py:95
  134.2 8.0 %shard_map.220 = (bf16[8,256,768]{2,1,0:T(8,128)(2,1)}, bf16[8,256,768]{2,1,0:T(8,128)(2,1)}, bf16[8,256,1536]{2,1,0:T(8,128)(2,1)}, bf16[8,256,1536]{2,1,0:T(8,...) custom-call(s32[2]{0:T(128)S(1)} %pad_add_fusion.refs_0_, ...), custom_call_target="tpu_custom_call", output_to_operand_aliasing={{0}: (9, {}), {1}: (10, {}), {2}: (11, {}), {3}: (12, {}), ... | custom-call | flops 4831838208 | bytes 57016328 | tf_op jit(solution)/shard_map/pallas_call | solution.py:95
  143.7 8.0 %shard_map.221 = (bf16[8,256,768]{2,1,0:T(8,128)(2,1)}, bf16[8,256,768]{2,1,0:T(8,128)(2,1)}, bf16[8,256,1536]{2,1,0:T(8,128)(2,1)}, bf16[8,256,1536]{2,1,0:T(8,...) custom-call(s32[2]{0:T(128)S(1)} %pad_add_fusion.refs_0_, ...), custom_call_target="tpu_custom_call", output_to_operand_aliasing={{0}: (9, {}), {1}: (10, {}), {2}: (11, {}), {3}: (12, {}), ... | custom-call | flops 4831838208 | bytes 57016328 | tf_op jit(solution)/shard_map/pallas_call | solution.py:95
  152.2 8.0 %shard_map.222 = (bf16[8,256,768]{2,1,0:T(8,128)(2,1)}, bf16[8,256,768]{2,1,0:T(8,128)(2,1)}, bf16[8,256,1536]{2,1,0:T(8,128)(2,1)}, bf16[8,256,1536]{2,1,0:T(8,...) custom-call(s32[2]{0:T(128)S(1)} %pad_add_fusion.refs_0_, ...), custom_call_target="tpu_custom_call", output_to_operand_aliasing={{0}: (9, {}), {1}: (10, {}), {2}: (11, {}), {3}: (12, {}), ... | custom-call | flops 4831838208 | bytes 57016328 | tf_op jit(solution)/shard_map/pallas_call | solution.py:95
  172.8 7.8 %collective-permute-done.31.refs_1_ = bf16[2,128,768]{2,1,0:T(8,128)(2,1)S(1)} collective-permute-done((bf16[2,128,768]{2,1,0:T(8,128)(2,1)S(1)}, bf16[2,128,768]{2,1,0:T(8,128)(2,1)S(1)}, u32[]{:S(2)}, u32[]{:S(2)}) %collective-permute-start.31) | collective-permute-done | bytes 393248 | tf_op jit(solution)/shard_map/ppermute | solution.py:656
  189.3 9.7 %shard_map.227 = (f32[1536,768]{1,0:T(8,128)}, f32[8,128]{1,0:T(8,128)S(1)}) custom-call(bf16[8,256,1536]{2,1,0:T(8,128)(2,1)} %get-tuple-element.169.refs_0_, bf16[8,256,768]{2,1,0:T(8,128)(2,1)} %get-tuple-element.170.refs_1_, f32[8,128]{1,0:T(8,128)S(1)} %get-tuple-element.171.refs_2_, f32[8,128]{1,0:T(8,128)S(1)} %get-tuple-element.172.refs_3_, ...), custom_call_target="tpu_custom_call" | custom-call | flops 4831838208 | bytes 14155776 | tf_op jit(solution)/shard_map/pallas_call | solution.py:95
  202.4 9.5 %collective-permute-done.30.refs_10_.refs_2_ = bf16[8,128,768]{2,1,0:T(8,128)(2,1)S(1)} collective-permute-done((bf16[8,128,768]{2,1,0:T(8,128)(2,1)S(1)}, bf16[8,128,768]{2,1,0:T(8,128)(2,1)S(1)}, u32[]{:S(2)}, u32[]{:S(2)}) %collective-permute-start.30) | collective-permute-done | bytes 1572896 | tf_op jit(solution)/shard_map/ppermute | solution.py:656
  211.9 6.1 %shard_map.229 = (f32[512,768]{1,0:T(8,128)}, bf16[512,384]{1,0:T(8,128)(2,1)S(1)}, bf16[512,384]{1,0:T(8,128)(2,1)}, f32[2,768]{1,0:T(2,128)S(1)}, f32[2,8,48,3...) custom-call(s32[2]{0:T(128)S(1)} %pad_add_fusion.refs_0_, ...), custom_call_target="tpu_custom_call" | custom-call | flops 1207959552 | bytes 10045448 | tf_op jit(solution)/shard_map/pallas_call | solution.py:95
  225.9 4.0 %collective-permute-done.42.refs_9_ = bf16[512,384]{1,0:T(8,128)(2,1)} collective-permute-done((bf16[512,384]{1,0:T(8,128)(2,1)}, bf16[512,384]{1,0:T(8,128)(2,1)}, u32[]{:S(2)}, u32[]{:S(2)}) %collective-permute-start.42) | collective-permute-done | bytes 393248 | tf_op jit(solution)/shard_map/ppermute | solution.py:656
  229.9 20.0 %shard_map.233 = (bf16[3,1024,384]{2,1,0:T(8,128)(2,1)}, bf16[2,4,3,48,384]{4,3,2,1,0:T(8,128)(2,1)S(1)}, bf16[2,4,3,48,384]{4,3,2,1,0:T(8,128)(2,1)S(1)}, f32[4,768]{1,0:T(4,128)S(1)}) custom-call(s32[2]{0:T(128)S(1)} %pad_add_fusion.refs_0_, bf16[1024,1152]{1,0:T(8,128)(2,1)} %get-tuple-element.117.refs_1_.refs_2_.refs_3_, ...), custom_call_target="tpu_custom_call" | custom-call | flops 30000001024 | bytes 18249736 | tf_op jit(solution)/shard_map/pallas_call | solution.py:95
  252.3 7.4 %collective-permute-done.47.refs_6_ = f32[4,768]{1,0:T(4,128)S(1)} collective-permute-done((f32[4,768]{1,0:T(4,128)S(1)}, f32[4,768]{1,0:T(4,128)S(1)}, u32[]{:S(2)}, u32[]{:S(2)}) %collective-permute-start.47) | collective-permute-done | bytes 12320 | tf_op jit(solution)/shard_map/ppermute | solution.py:656
  261.5 5.6 %shard_map.235 = (bf16[512,768]{1,0:T(8,128)(2,1)}, f32[512,768]{1,0:T(8,128)S(1)}, f32[8,128]{1,0:T(8,128)S(1)}) custom-call(s32[2]{0:T(128)S(1)} %pad_add_fusion.refs_0_, bf16[3,1024,384]{2,1,0:T(8,128)(2,1)} %get-tuple-element.192.refs_1_, bf16[3,768,384]{2,1,0:T(8,128)(2,1)} %get-tuple-element.186.refs_11_.refs_2_, f32[8,128]{1,0:T(8,128)S(1)} %get-tuple-element.198.refs_3_), custom_call_target="tpu_custom_call" | custom-call | tf_op jit(solution)/shard_map/pallas_call | solution.py:95
  267.6 9.7 %shard_map.237 = (f32[768,1536]{1,0:T(8,128)}, f32[8,128]{1,0:T(8,128)S(1)}) custom-call(bf16[8,256,768]{2,1,0:T(8,128)(2,1)} %get-tuple-element.205.refs_0_, bf16[8,256,1536]{2,1,0:T(8,128)(2,1)} %get-tuple-element.206.refs_1_, f32[8,128]{1,0:T(8,128)S(1)} %get-tuple-element.207.refs_2_), custom_call_target="tpu_custom_call" | custom-call | tf_op jit(solution)/shard_map/pallas_call | solution.py:95
  286.7 4.0 %shard_map.236 = (f32[512,768]{1,0:T(8,128)}, f32[8,128]{1,0:T(8,128)S(1)}) custom-call(f32[512,768]{1,0:T(8,128)} %get-tuple-element.180.refs_0_, f32[512,768]{1,0:T(8,128)S(1)} %get-tuple-element.199.refs_1_, bf16[512,768]{1,0:T(8,128)(2,1)} %collective-permute-done.49.refs_2_, bf16[512,768]{1,0:T(8,128)(2,1)} %refs_3_.3, ...), custom_call_target="tpu_custom_call" | custom-call | tf_op jit(solution)/shard_map/pallas_call | solution.py:95
  (178 shorter events, 116.1 us)
Async XLA Ops:
  1.6 20.5 %collective-permute-start = (bf16[4,48,384]{2,1,0:T(8,128)(2,1)S(1)}, bf16[4,48,384]{2,1,0:T(8,128)(2,1)S(1)}, u32[]{:S(2)}, u32[]{:S(2)}) collective-permute-start(bf16[4,48,384]{2,1,0:T(8,128)(2,1)S(1)} %pad_maximum_fusion), channel_id=1, source_target_pairs={{0,4},{2,6},{4,0},{6,2},{8,12},{10,14},{12,8},{14,10},{16,20},{18,... | collective-permute-start | bytes 442376 | tf_op jit(solution)/shard_map/ppermute | solution.py:663
  9.0 18.5 %collective-permute-start.7 = (bf16[512,768]{1,0:T(8,128)(2,1)}, bf16[512,768]{1,0:T(8,128)(2,1)S(1)}, u32[]{:S(2)}, u32[]{:S(2)}) collective-permute-start(bf16[512,768]{1,0:T(8,128)(2,1)} %refs_3_.3), channel_id=1, source_target_pairs={{0,1},{1,0},{2,3},{3,2},{4,5},{5,4},{6,7},{7,6},{8,9},{9,8},{10,11... | collective-permute-start | bytes 2359304 | tf_op jit(solution)/shard_map/ppermute | solution.py:656
  29.6 37.2 %all-to-all-start = ((bf16[16,64,768]{2,1,0:T(8,128)(2,1)}), bf16[16,64,768]{2,1,0:T(8,128)(2,1)S(1)}, u32[]{:S(2)}, u32[]{:S(2)}) async-start(bf16[16,64,768]{2,1,0:T(8,128)(2,1)} %bitcast.59), calls=%async_computation | async-start | bytes 3145728 | tf_op jit(solution)/shard_map/all_to_all | solution.py:769
  44.1 24.5 %collective-permute-start.11 = (bf16[768,384]{1,0:T(8,128)(2,1)}, bf16[768,384]{1,0:T(8,128)(2,1)S(1)}, u32[]{:S(2)}, u32[]{:S(2)}) collective-permute-start(bf16[768,384]{1,0:T(8,128)(2,1)} %get-tuple-element.120.refs_2_.refs_6_), channel_id=1, source_target_pairs={{0,1},{1,0},{2,3},{3,2},{4,5},{5,4},{6,7},{7,6},{8,9},{9,8},{10,11... | collective-permute-start | bytes 1769480 | tf_op jit(solution)/shard_map/ppermute | solution.py:656
  66.8 57.2 %collective-permute-start.8 = (bf16[16,64,768]{2,1,0:T(8,128)(2,1)S(1)}, bf16[16,64,768]{2,1,0:T(8,128)(2,1)S(1)}, u32[]{:S(2)}, u32[]{:S(2)}) collective-permute-start(bf16[16,64,768]{2,1,0:T(8,128)(2,1)S(1)} %all-to-all-done.refs_4_.refs_3_), channel_id=1, source_target_pairs={{0,1},{1,0},{2,3},{3,2},{4,5},{5,4},{6,7},{7,6},{8,9},{9,8},{10,11... | collective-permute-start | bytes 4718600 | tf_op jit(solution)/shard_map/ppermute | solution.py:656
  85.5 19.0 %collective-permute-start.19 = (bf16[2,64,768]{2,1,0:T(8,128)(2,1)S(1)}, bf16[2,64,768]{2,1,0:T(8,128)(2,1)S(1)}, u32[]{:S(2)}, u32[]{:S(2)}) collective-permute-start(bf16[2,64,768]{2,1,0:T(8,128)(2,1)S(1)} %get-tuple-element.126), channel_id=1, source_target_pairs={{0,28},{2,30},{4,24},{6,26},{8,20},{10,22},{12,16},{14,18},{16,12}... | collective-permute-start | bytes 589832 | tf_op jit(solution)/shard_map/ppermute | solution.py:663
  90.0 27.8 %collective-permute-start.22 = (bf16[2,64,768]{2,1,0:T(8,128)(2,1)S(1)}, bf16[2,64,768]{2,1,0:T(8,128)(2,1)S(1)}, u32[]{:S(2)}, u32[]{:S(2)}) collective-permute-start(bf16[2,64,768]{2,1,0:T(8,128)(2,1)S(1)} %get-tuple-element.127), channel_id=1, source_target_pairs={{0,16},{2,18},{4,20},{6,22},{8,24},{10,26},{12,28},{14,30},{16,0},... | collective-permute-start | bytes 589832 | tf_op jit(solution)/shard_map/ppermute | solution.py:663
  92.7 28.6 %collective-permute-start.23 = (bf16[2,64,768]{2,1,0:T(8,128)(2,1)S(1)}, bf16[2,64,768]{2,1,0:T(8,128)(2,1)S(1)}, u32[]{:S(2)}, u32[]{:S(2)}) collective-permute-start(bf16[2,64,768]{2,1,0:T(8,128)(2,1)S(1)} %get-tuple-element.128), channel_id=1, source_target_pairs={{0,20},{2,22},{4,16},{6,18},{8,28},{10,30},{12,24},{14,26},{16,4},... | collective-permute-start | bytes 589832 | tf_op jit(solution)/shard_map/ppermute | solution.py:663
  98.6 23.3 %collective-permute-start.27 = (bf16[2,64,768]{2,1,0:T(8,128)(2,1)S(1)}, bf16[2,64,768]{2,1,0:T(8,128)(2,1)S(1)}, u32[]{:S(2)}, u32[]{:S(2)}) collective-permute-start(bf16[2,64,768]{2,1,0:T(8,128)(2,1)S(1)} %get-tuple-element.129.refs_4_.refs_5_), channel_id=1, source_target_pairs={{0,1},{1,0},{2,3},{3,2},{4,5},{5,4},{6,7},{7,6},{8,9},{9,8},{10,11... | collective-permute-start | bytes 589832 | tf_op jit(solution)/shard_map/ppermute | solution.py:656
  104.5 19.0 %collective-permute-start.28 = (bf16[2,64,768]{2,1,0:T(8,128)(2,1)S(1)}, bf16[2,64,768]{2,1,0:T(8,128)(2,1)S(1)}, u32[]{:S(2)}, u32[]{:S(2)}) collective-permute-start(bf16[2,64,768]{2,1,0:T(8,128)(2,1)S(1)} %collective-permute-done.26.refs_6_.refs_10_), channel_id=1, source_target_pairs={{0,1},{1,0},{2,3},{3,2},{4,5},{5,4},{6,7},{7,6},{8,9},{9,8},{10,11... | collective-permute-start | bytes 589832 | tf_op jit(solution)/shard_map/ppermute | solution.py:656
  121.9 21.8 %collective-permute-start.20 = (bf16[2,64,768]{2,1,0:T(8,128)(2,1)S(1)}, bf16[2,64,768]{2,1,0:T(8,128)(2,1)S(1)}, u32[]{:S(2)}, u32[]{:S(2)}) collective-permute-start(bf16[2,64,768]{2,1,0:T(8,128)(2,1)S(1)} %collective-permute-done.18.refs_15_.refs_5_), channel_id=1, source_target_pairs={{0,1},{1,0},{2,3},{3,2},{4,5},{5,4},{6,7},{7,6},{8,9},{9,8},{10,11... | collective-permute-start | bytes 589832 | tf_op jit(solution)/shard_map/ppermute | solution.py:656
  123.4 20.3 %collective-permute-start.21 = (bf16[2,64,768]{2,1,0:T(8,128)(2,1)S(1)}, bf16[2,64,768]{2,1,0:T(8,128)(2,1)S(1)}, u32[]{:S(2)}, u32[]{:S(2)}) collective-permute-start(bf16[2,64,768]{2,1,0:T(8,128)(2,1)S(1)} %collective-permute-done.19.refs_16_.refs_6_), channel_id=1, source_target_pairs={{0,1},{1,0},{2,3},{3,2},{4,5},{5,4},{6,7},{7,6},{8,9},{9,8},{10,11... | collective-permute-start | bytes 589832 | tf_op jit(solution)/shard_map/ppermute | solution.py:656
  124.0 28.2 %collective-permute-start.16 = (bf16[2,64,768]{2,1,0:T(8,128)(2,1)S(1)}, bf16[2,64,768]{2,1,0:T(8,128)(2,1)S(1)}, u32[]{:S(2)}, u32[]{:S(2)}) collective-permute-start(bf16[2,64,768]{2,1,0:T(8,128)(2,1)S(1)} %collective-permute-done.14.refs_11_.refs_5_), channel_id=1, source_target_pairs={{0,1},{1,0},{2,3},{3,2},{4,5},{5,4},{6,7},{7,6},{8,9},{9,8},{10,11... | collective-permute-start | bytes 589832 | tf_op jit(solution)/shard_map/ppermute | solution.py:656
  133.6 18.6 %collective-permute-start.17 = (bf16[2,64,768]{2,1,0:T(8,128)(2,1)S(1)}, bf16[2,64,768]{2,1,0:T(8,128)(2,1)S(1)}, u32[]{:S(2)}, u32[]{:S(2)}) collective-permute-start(bf16[2,64,768]{2,1,0:T(8,128)(2,1)S(1)} %collective-permute-done.15.refs_12_.refs_6_), channel_id=1, source_target_pairs={{0,1},{1,0},{2,3},{3,2},{4,5},{5,4},{6,7},{7,6},{8,9},{9,8},{10,11... | collective-permute-start | bytes 589832 | tf_op jit(solution)/shard_map/ppermute | solution.py:656
  142.2 23.2 %collective-permute-start.36 = (bf16[2,128,768]{2,1,0:T(8,128)(2,1)S(1)}, bf16[2,128,768]{2,1,0:T(8,128)(2,1)S(1)}, u32[]{:S(2)}, u32[]{:S(2)}) collective-permute-start(bf16[2,128,768]{2,1,0:T(8,128)(2,1)S(1)} %get-tuple-element.164), channel_id=1, source_target_pairs={{0,1},{1,0},{2,3},{3,2},{4,5},{5,4},{6,7},{7,6},{8,9},{9,8},{10,11... | collective-permute-start | bytes 1179656 | tf_op jit(solution)/shard_map/ppermute | solution.py:656
  161.7 19.0 %collective-permute-start.31 = (bf16[2,128,768]{2,1,0:T(8,128)(2,1)S(1)}, bf16[2,128,768]{2,1,0:T(8,128)(2,1)S(1)}, u32[]{:S(2)}, u32[]{:S(2)}) collective-permute-start(bf16[2,128,768]{2,1,0:T(8,128)(2,1)S(1)} %get-tuple-element.156), channel_id=1, source_target_pairs={{0,1},{1,0},{2,3},{3,2},{4,5},{5,4},{6,7},{7,6},{8,9},{9,8},{10,11... | collective-permute-start | bytes 1179656 | tf_op jit(solution)/shard_map/ppermute | solution.py:656
  164.0 47.9 %collective-permute-start.30 = (bf16[8,128,768]{2,1,0:T(8,128)(2,1)S(1)}, bf16[8,128,768]{2,1,0:T(8,128)(2,1)S(1)}, u32[]{:S(2)}, u32[]{:S(2)}) collective-permute-start(bf16[8,128,768]{2,1,0:T(8,128)(2,1)S(1)} %get-tuple-element.154), channel_id=1, source_target_pairs={{0,1},{1,0},{2,3},{3,2},{4,5},{5,4},{6,7},{7,6},{8,9},{9,8},{10,11... | collective-permute-start | bytes 4718600 | tf_op jit(solution)/shard_map/ppermute | solution.py:656
  166.0 16.6 %collective-permute-start.37 = (bf16[2,64,768]{2,1,0:T(8,128)(2,1)S(1)}, bf16[2,64,768]{2,1,0:T(8,128)(2,1)S(1)}, u32[]{:S(2)}, u32[]{:S(2)}) collective-permute-start(bf16[2,64,768]{2,1,0:T(8,128)(2,1)S(1)} %get-tuple-element.165), channel_id=1, source_target_pairs={{0,16},{2,18},{4,20},{6,22},{8,24},{10,26},{12,28},{14,30},{16,0},... | collective-permute-start | bytes 589832 | tf_op jit(solution)/shard_map/ppermute | solution.py:663
  169.0 16.6 %collective-permute-start.38 = (bf16[2,64,768]{2,1,0:T(8,128)(2,1)S(1)}, bf16[2,64,768]{2,1,0:T(8,128)(2,1)S(1)}, u32[]{:S(2)}, u32[]{:S(2)}) collective-permute-start(bf16[2,64,768]{2,1,0:T(8,128)(2,1)S(1)} %get-tuple-element.166), channel_id=1, source_target_pairs={{0,20},{2,22},{4,16},{6,18},{8,28},{10,30},{12,24},{14,26},{16,4},... | collective-permute-start | bytes 589832 | tf_op jit(solution)/shard_map/ppermute | solution.py:663
  180.6 18.3 %collective-permute-start.35 = (bf16[2,64,768]{2,1,0:T(8,128)(2,1)S(1)}, bf16[2,64,768]{2,1,0:T(8,128)(2,1)S(1)}, u32[]{:S(2)}, u32[]{:S(2)}) collective-permute-start(bf16[2,64,768]{2,1,0:T(8,128)(2,1)S(1)} %get-tuple-element.162), channel_id=1, source_target_pairs={{0,12},{2,14},{4,8},{6,10},{8,4},{10,6},{12,0},{14,2},{16,28},{18,... | collective-permute-start | bytes 589832 | tf_op jit(solution)/shard_map/ppermute | solution.py:663
  182.6 16.3 %collective-permute-start.39 = (bf16[2,64,768]{2,1,0:T(8,128)(2,1)S(1)}, bf16[2,64,768]{2,1,0:T(8,128)(2,1)S(1)}, u32[]{:S(2)}, u32[]{:S(2)}) collective-permute-start(bf16[2,64,768]{2,1,0:T(8,128)(2,1)S(1)} %get-tuple-element.167), channel_id=1, source_target_pairs={{0,24},{2,26},{4,28},{6,30},{8,16},{10,18},{12,20},{14,22},{16,8},... | collective-permute-start | bytes 589832 | tf_op jit(solution)/shard_map/ppermute | solution.py:663
  221.9 55.4 %all-to-all-start.1 = ((bf16[16,64,768]{2,1,0:T(8,128)(2,1)}), bf16[16,64,768]{2,1,0:T(8,128)(2,1)S(1)}, u32[]{:S(2)}, u32[]{:S(2)}) async-start(bf16[16,64,768]{2,1,0:T(8,128)(2,1)} %get-tuple-element.178), calls=%async_computation.1 | async-start | bytes 3145728 | tf_op jit(solution)/shard_map/all_to_all | solution.py:918
  260.9 16.4 %collective-permute-start.50 = (bf16[800,384]{1,0:T(8,128)(2,1)}, bf16[800,384]{1,0:T(8,128)(2,1)}, u32[]{:S(2)}, u32[]{:S(2)}) collective-permute-start(bf16[800,384]{1,0:T(8,128)(2,1)} %get-tuple-element.203), channel_id=1, source_target_pairs={{0,4},{2,6},{4,0},{6,2},{8,12},{10,14},{12,8},{14,10},{16,20},{18,... | collective-permute-start | bytes 1843208 | tf_op jit(solution)/shard_map/ppermute | solution.py:663
  267.1 19.6 %collective-permute-start.49 = (bf16[512,768]{1,0:T(8,128)(2,1)}, bf16[512,768]{1,0:T(8,128)(2,1)}, u32[]{:S(2)}, u32[]{:S(2)}) collective-permute-start(bf16[512,768]{1,0:T(8,128)(2,1)} %get-tuple-element.200), channel_id=1, source_target_pairs={{0,1},{1,0},{2,3},{3,2},{4,5},{5,4},{6,7},{7,6},{8,9},{9,8},{10,11... | collective-permute-start | bytes 2359304 | tf_op jit(solution)/shard_map/ppermute | solution.py:656
  (51 other events, 542.0 us)
